TPU v7x, 512 devices: a whole 4x8x8 slice. The times are simulated.
512 devices in a mesh: frame: 16 (over z_hi, x, core), tensor: 8 (over y), dp: 4 (over z_lo).
Axes of the slice: x: 4, y: 8, z: 8 (z_hi: 2, z_lo: 4; z = z_hi * 4 + z_lo), core: 2. Of those that a mesh axis runs over, the one named last changes fastest.
Arguments:
- queries: bfloat16 [12, 16, 256, 2048], P('dp', 'frame', None, 'tensor'), may hold values from -8 to 8
- keys: bfloat16 [12, 16, 256, 2048], P('dp', 'frame', None, 'tensor'), may hold values from -8 to 8
- values: bfloat16 [12, 16, 256, 2048], P('dp', 'frame', None, 'tensor'), may hold values from -6 to 6
- out_grad: bfloat16 [12, 16, 256, 2048], P('dp', 'frame', None, 'tensor'), may hold values from -6 to 6
- out_proj: bfloat16 [2048, 2048], P('tensor'), may hold values from -0.125 to 0.125
Outputs:
- grad_queries: bfloat16 [12, 16, 256, 2048], P('dp', 'frame', None, 'tensor')
- grad_keys: bfloat16 [12, 16, 256, 2048], P('dp', 'frame', None, 'tensor')
- grad_values: bfloat16 [12, 16, 256, 2048], P('dp', 'frame', None, 'tensor')
- grad_proj: bfloat16 [2048, 2048], P('tensor')
All inputs are finite; a program needn't handle non-finite values.
Results may differ from a plain program's by a relative error of at most 0.0075.
Values may be sent and summed in bfloat16 or wider, within the bound.
No kernel may reach another device: no remote copies, remote signals or barrier semaphores. Data moves between devices by JAX's collectives and lax.ppermute only.
A program may use at most 64 MiB of HBM per device.

v0:
```python
import math

import jax
import jax.numpy as jnp
from jax import lax
from jax.sharding import PartitionSpec as P

D = 2048
HEAD = 128


def attend(queries, keys, values, grad_attended):
    lead = queries.shape[:-3]
    frames, patches, width = queries.shape[-3:]
    count = width // HEAD
    scale = 1.0 / math.sqrt(HEAD)

    def split(array):
        return array.reshape(lead + (frames, patches, count, HEAD)).astype(jnp.float32)

    query_f, key_f, value_f, grad_f = (
        split(queries),
        split(keys),
        split(values),
        split(grad_attended),
    )
    rows = lax.broadcasted_iota(jnp.int32, (frames, frames), 0)
    cols = lax.broadcasted_iota(jnp.int32, (frames, frames), 1)
    causal = cols <= rows
    scores = jnp.einsum("...ipne,...jpne->...pnij", query_f, key_f) * scale
    scores = jnp.where(causal, scores, -1e30)
    top = jnp.max(scores, axis=-1, keepdims=True)
    expon = jnp.where(causal, jnp.exp(scores - top), 0.0)
    probs = expon / jnp.sum(expon, axis=-1, keepdims=True)
    weights = lax.optimization_barrier(probs.astype(jnp.bfloat16)).astype(jnp.float32)
    attended = jnp.einsum("...pnij,...jpne->...ipne", weights, value_f).astype(jnp.bfloat16)
    grad_probs = jnp.einsum("...ipne,...jpne->...pnij", grad_f, value_f)
    grad_values = jnp.einsum("...pnij,...ipne->...jpne", weights, grad_f).astype(jnp.bfloat16)
    row_total = jnp.sum(probs * grad_probs, axis=-1, keepdims=True)
    grad_scores = (probs * (grad_probs - row_total) * scale).astype(jnp.bfloat16)
    grad_scores = lax.optimization_barrier(grad_scores).astype(jnp.float32)
    grad_queries = jnp.einsum("...pnij,...jpne->...ipne", grad_scores, key_f).astype(jnp.bfloat16)
    grad_keys = jnp.einsum("...pnij,...ipne->...jpne", grad_scores, query_f).astype(jnp.bfloat16)
    shape = lead + (frames, patches, width)
    return (
        attended.reshape(shape),
        grad_queries.reshape(shape),
        grad_keys.reshape(shape),
        grad_values.reshape(shape),
    )


def project_back(flat, out_proj, shape):
    grad_att = lax.dot_general(
        flat, out_proj, (((1,), (1,)), ((), ())), preferred_element_type=jnp.float32
    )
    return grad_att.astype(jnp.bfloat16).reshape(shape)


def proj_term(attended, flat, factor):
    width = attended.shape[-1]
    term = lax.dot_general(
        attended.reshape(-1, width),
        flat,
        (((0,), (0,)), ((), ())),
        preferred_element_type=jnp.float32,
    )
    return term * factor


def local(queries, keys, values, out_grad, out_proj):
    clips, frames_here, patches, width = queries.shape
    tokens_all = clips * frames_here * patches * lax.axis_size("frame") * lax.axis_size("dp")
    factor = 1.0 / math.sqrt(tokens_all)
    full_grad = lax.all_gather(out_grad, "tensor", axis=3, tiled=True)
    flat = full_grad.reshape(-1, D)
    grad_att = project_back(flat, out_proj, queries.shape)
    moved = (
        lax.all_to_all(queries, "frame", split_axis=2, concat_axis=1, tiled=True),
        lax.all_to_all(keys, "frame", split_axis=2, concat_axis=1, tiled=True),
        lax.all_to_all(values, "frame", split_axis=2, concat_axis=1, tiled=True),
        lax.all_to_all(grad_att, "frame", split_axis=2, concat_axis=1, tiled=True),
    )
    attended, grad_q, grad_k, grad_v = attend(moved[0], moved[1], moved[2], moved[3])
    home = (
        lax.all_to_all(grad_q, "frame", split_axis=1, concat_axis=2, tiled=True),
        lax.all_to_all(grad_k, "frame", split_axis=1, concat_axis=2, tiled=True),
        lax.all_to_all(grad_v, "frame", split_axis=1, concat_axis=2, tiled=True),
        lax.all_to_all(attended, "frame", split_axis=1, concat_axis=2, tiled=True),
    )
    grad_q, grad_k, grad_v = (home[0], home[1], home[2])
    term = proj_term(home[3], flat, factor)
    grad_proj = lax.psum(term, ("frame", "dp")).astype(jnp.bfloat16)
    return (grad_q, grad_k, grad_v, grad_proj)


def solution(mesh):
    return jax.shard_map(
        local,
        mesh=mesh,
        in_specs=(
            P("dp", "frame", None, "tensor"),
            P("dp", "frame", None, "tensor"),
            P("dp", "frame", None, "tensor"),
            P("dp", "frame", None, "tensor"),
            P("tensor", None),
        ),
        out_specs=(
            P("dp", "frame", None, "tensor"),
            P("dp", "frame", None, "tensor"),
            P("dp", "frame", None, "tensor"),
            P("tensor", None),
        ),
        check_vma=False,
    )
```

profile of v0, /device:TPU:1, one launch (start us, length us, event | category | flops | bytes accessed | tf_op | source)
XLA Modules:
  0.0 452.6 jit_solution(6205673420413861327)
XLA Ops:
  7.2 0.7 all-gather.2.cloned.1.call-update
  7.9 2.1 copy.87
  10.1 14.3 %all-to-all-start = ((bf16[3,1,256,256]{3,0,1,2:T(4,128)(2,1)}), bf16[3,1,256,256]{3,0,1,2:T(4,128)(2,1)S(1)}, u32[]{:S(2)}, u32[]{:S(2)}) async-start(bf16[3,1,256,256]{3,0,1,2:T(4,128)(2,1)} %copy.87), calls=%async_computation | async-start | bytes 1048576 | tf_op jit(solution)/shard_map/all_to_all | solution.py:79
  24.3 2.1 copy.89
  26.4 11.7 %all-to-all-done = bf16[3,1,256,256]{3,0,1,2:T(4,128)(2,1)S(1)} async-done(((bf16[3,1,256,256]{3,0,1,2:T(4,128)(2,1)}), bf16[3,1,256,256]{3,0,1,2:T(4,128)(2,1)S(1)}, u32[]{:S(2)}, u32[]{:S(2)}) %all-to-all-start) | async-done | bytes 393248 | tf_op jit(solution)/shard_map/all_to_all | solution.py:79
  38.2 7.9 %all-to-all-start.1 = ((bf16[3,1,256,256]{3,0,1,2:T(4,128)(2,1)}), bf16[3,1,256,256]{3,0,1,2:T(4,128)(2,1)S(1)}, u32[]{:S(2)}, u32[]{:S(2)}) async-start(bf16[3,1,256,256]{3,0,1,2:T(4,128)(2,1)} %copy.89), calls=%async_computation.1 | async-start | bytes 1048576 | tf_op jit(solution)/shard_map/all_to_all | solution.py:80
  46.1 1.1 copy.95
  47.2 12.7 %all-to-all-done.1 = bf16[3,1,256,256]{3,0,1,2:T(4,128)(2,1)S(1)} async-done(((bf16[3,1,256,256]{3,0,1,2:T(4,128)(2,1)}), bf16[3,1,256,256]{3,0,1,2:T(4,128)(2,1)S(1)}, u32[]{:S(2)}, u32[]{:S(2)}) %all-to-all-start.1) | async-done | bytes 393248 | tf_op jit(solution)/shard_map/all_to_all | solution.py:80
  59.9 8.0 %all-to-all-start.3 = ((bf16[3,1,256,256]{3,0,1,2:T(4,128)(2,1)}), bf16[3,1,256,256]{3,0,1,2:T(4,128)(2,1)S(1)}, u32[]{:S(2)}, u32[]{:S(2)}) async-start(bf16[3,1,256,256]{3,0,1,2:T(4,128)(2,1)} %copy.95), calls=%async_computation.3 | async-start | bytes 1048576 | tf_op jit(solution)/shard_map/all_to_all | solution.py:81
  67.9 1.1 reshape.84
  68.9 0.3 reshape.85
  69.3 1.3 all-gather.2.cloned.1.call-done
  70.6 3.0 convolution_convert_fusion
  73.6 1.1 copy.93
  74.7 6.9 %all-to-all-done.3 = bf16[3,1,256,256]{3,0,1,2:T(4,128)(2,1)S(1)} async-done(((bf16[3,1,256,256]{3,0,1,2:T(4,128)(2,1)}), bf16[3,1,256,256]{3,0,1,2:T(4,128)(2,1)S(1)}, u32[]{:S(2)}, u32[]{:S(2)}) %all-to-all-start.3) | async-done | bytes 393248 | tf_op jit(solution)/shard_map/all_to_all | solution.py:81
  81.7 8.0 %all-to-all-start.2 = ((bf16[3,1,256,256]{3,0,1,2:T(4,128)(2,1)}), bf16[3,1,256,256]{3,0,1,2:T(4,128)(2,1)S(1)}, u32[]{:S(2)}, u32[]{:S(2)}) async-start(bf16[3,1,256,256]{3,0,1,2:T(4,128)(2,1)} %copy.93), calls=%async_computation.2 | async-start | bytes 1048576 | tf_op jit(solution)/shard_map/all_to_all | solution.py:82
  89.6 1.5 fusion.25
  91.2 1.2 fusion.24
  92.4 0.3 reshape.87
  92.8 0.3 fusion.12
  93.1 0.3 copy.137
  93.4 1.0 reshape.91
  94.4 9.1 %all-to-all-done.2 = bf16[3,1,256,256]{3,0,1,2:T(4,128)(2,1)S(1)} async-done(((bf16[3,1,256,256]{3,0,1,2:T(4,128)(2,1)}), bf16[3,1,256,256]{3,0,1,2:T(4,128)(2,1)S(1)}, u32[]{:S(2)}, u32[]{:S(2)}) %all-to-all-start.2) | async-done | bytes 393248 | tf_op jit(solution)/shard_map/all_to_all | solution.py:82
  103.4 8.0 %all-to-all-start.7 = ((bf16[3,16,16,256]{3,2,0,1:T(8,128)(2,1)}), bf16[3,16,16,256]{3,2,0,1:T(8,128)(2,1)}, u32[]{:S(2)}, u32[]{:S(2)}) async-start(bf16[3,16,16,256]{3,2,0,1:T(8,128)(2,1)} %reshape.91), calls=%async_computation.7 | async-start | bytes 786432 | tf_op jit(solution)/shard_map/all_to_all | solution.py:89
  111.4 0.3 reshape.86
  111.8 0.4 fusion.13
  112.1 0.3 copy.135
  112.4 1.0 reshape.90
  113.4 10.5 %all-to-all-done.7 = bf16[3,16,16,256]{3,2,0,1:T(8,128)(2,1)} async-done(((bf16[3,16,16,256]{3,2,0,1:T(8,128)(2,1)}), bf16[3,16,16,256]{3,2,0,1:T(8,128)(2,1)}, u32[]{:S(2)}, u32[]{:S(2)}) %all-to-all-start.7) | async-done | bytes 393248 | tf_op jit(solution)/shard_map/all_to_all | solution.py:89
  123.9 6.6 %all-to-all-start.6 = ((bf16[3,16,16,256]{3,2,0,1:T(8,128)(2,1)}), bf16[3,16,16,256]{3,2,0,1:T(8,128)(2,1)S(1)}, u32[]{:S(2)}, u32[]{:S(2)}) async-start(bf16[3,16,16,256]{3,2,0,1:T(8,128)(2,1)} %reshape.90), calls=%async_computation.6 | async-start | bytes 786432 | tf_op jit(solution)/shard_map/all_to_all | solution.py:88
  130.5 0.4 fusion.16
  130.9 1.7 fusion.9
  132.7 0.4 fusion.11
  133.1 0.3 copy.133
  133.4 1.0 reshape.89
  134.4 8.6 %all-to-all-done.6 = bf16[3,16,16,256]{3,2,0,1:T(8,128)(2,1)S(1)} async-done(((bf16[3,16,16,256]{3,2,0,1:T(8,128)(2,1)}), bf16[3,16,16,256]{3,2,0,1:T(8,128)(2,1)S(1)}, u32[]{:S(2)}, u32[]{:S(2)}) %all-to-all-start.6) | async-done | bytes 393248 | tf_op jit(solution)/shard_map/all_to_all | solution.py:88
  142.9 6.6 %all-to-all-start.5 = ((bf16[3,16,16,256]{3,2,0,1:T(8,128)(2,1)}), bf16[3,16,16,256]{3,2,0,1:T(8,128)(2,1)}, u32[]{:S(2)}, u32[]{:S(2)}) async-start(bf16[3,16,16,256]{3,2,0,1:T(8,128)(2,1)} %reshape.89), calls=%async_computation.5 | async-start | bytes 786432 | tf_op jit(solution)/shard_map/all_to_all | solution.py:87
  149.5 1.0 copy.116
  150.6 2.9 convolution_multiply_fusion
  153.5 0.3 fusion.10
  153.9 1.1 copy.131
  154.9 2.0 reshape.88
  156.9 5.1 %all-to-all-done.5 = bf16[3,16,16,256]{3,2,0,1:T(8,128)(2,1)} async-done(((bf16[3,16,16,256]{3,2,0,1:T(8,128)(2,1)}), bf16[3,16,16,256]{3,2,0,1:T(8,128)(2,1)}, u32[]{:S(2)}, u32[]{:S(2)}) %all-to-all-start.5) | async-done | bytes 393248 | tf_op jit(solution)/shard_map/all_to_all | solution.py:87
  162.0 6.6 %all-to-all-start.4 = ((bf16[3,16,16,256]{3,2,0,1:T(8,128)(2,1)}), bf16[3,16,16,256]{3,2,0,1:T(8,128)(2,1)}, u32[]{:S(2)}, u32[]{:S(2)}) async-start(bf16[3,16,16,256]{3,2,0,1:T(8,128)(2,1)} %reshape.88), calls=%async_computation.4 | async-start | bytes 786432 | tf_op jit(solution)/shard_map/all_to_all | solution.py:86
  168.6 272.8 %all-reduce.1 = bf16[256,2048]{1,0:T(8,128)(2,1)} all-reduce(f32[256,2048]{1,0:T(8,128)S(1)} %convolution_multiply_fusion), channel_id=1, replica_groups=mesh['frame'=16,'tensor'=8,'dp'=4] {'frame','dp'}, use_global_device_ids=true, to_apply=%region_3.4 | all-reduce | flops 524288 | bytes 3145728 | tf_op jit(solution)/shard_map/psum | solution.py:93
  441.4 0.8 copy.111
  442.2 1.8 copy.107
  444.0 1.8 copy.103
  (19 shorter events, 0.1 us)
Async XLA Ops:
  7.2 63.5 %copy-start = (bf16[256,2048]{1,0:T(8,128)(2,1)S(1)}, bf16[256,2048]{1,0:T(8,128)(2,1)}, u32[]{:S(2)}) copy-start(bf16[256,2048]{1,0:T(8,128)(2,1)} %param.9) | copy-start | bytes 3145732
  7.2 38.9 %copy-start.7 = (bf16[3,1,256,256]{3,2,1,0:T(8,128)(2,1)S(1)}, bf16[3,1,256,256]{3,2,1,0:T(8,128)(2,1)}, u32[]{:S(2)}) copy-start(bf16[3,1,256,256]{3,2,1,0:T(8,128)(2,1)} %param.7) | copy-start | bytes 1179652
  7.2 63.4 %all-gather.2.cloned.1.call-start = ((), (), s32[]{:S(2)}) async-start(), calls=%async_computation.8 | async-start | bytes 3538944 | tf_op jit(solution)/shard_map/all_gather | solution.py:75
  10.1 28.1 %all-to-all-start = ((bf16[3,1,256,256]{3,0,1,2:T(4,128)(2,1)}), bf16[3,1,256,256]{3,0,1,2:T(4,128)(2,1)S(1)}, u32[]{:S(2)}, u32[]{:S(2)}) async-start(bf16[3,1,256,256]{3,0,1,2:T(4,128)(2,1)} %copy.87), calls=%async_computation | async-start | bytes 1048576 | tf_op jit(solution)/shard_map/all_to_all | solution.py:79
  38.2 21.7 %all-to-all-start.1 = ((bf16[3,1,256,256]{3,0,1,2:T(4,128)(2,1)}), bf16[3,1,256,256]{3,0,1,2:T(4,128)(2,1)S(1)}, u32[]{:S(2)}, u32[]{:S(2)}) async-start(bf16[3,1,256,256]{3,0,1,2:T(4,128)(2,1)} %copy.89), calls=%async_computation.1 | async-start | bytes 1048576 | tf_op jit(solution)/shard_map/all_to_all | solution.py:80
  59.9 21.8 %all-to-all-start.3 = ((bf16[3,1,256,256]{3,0,1,2:T(4,128)(2,1)}), bf16[3,1,256,256]{3,0,1,2:T(4,128)(2,1)S(1)}, u32[]{:S(2)}, u32[]{:S(2)}) async-start(bf16[3,1,256,256]{3,0,1,2:T(4,128)(2,1)} %copy.95), calls=%async_computation.3 | async-start | bytes 1048576 | tf_op jit(solution)/shard_map/all_to_all | solution.py:81
  70.6 19.0 %copy-start.1 = (bf16[3,16,16,2,128]{4,3,0,2,1:T(2,128)(2,1)S(1)}, bf16[3,16,16,2,128]{4,3,0,2,1:T(2,128)(2,1)}, u32[]{:S(2)}) copy-start(bf16[3,16,16,2,128]{4,3,0,2,1:T(2,128)(2,1)} %reshape.84) | copy-start | bytes 1179652
  81.7 21.8 %all-to-all-start.2 = ((bf16[3,1,256,256]{3,0,1,2:T(4,128)(2,1)}), bf16[3,1,256,256]{3,0,1,2:T(4,128)(2,1)S(1)}, u32[]{:S(2)}, u32[]{:S(2)}) async-start(bf16[3,1,256,256]{3,0,1,2:T(4,128)(2,1)} %copy.93), calls=%async_computation.2 | async-start | bytes 1048576 | tf_op jit(solution)/shard_map/all_to_all | solution.py:82
  103.4 20.5 %all-to-all-start.7 = ((bf16[3,16,16,256]{3,2,0,1:T(8,128)(2,1)}), bf16[3,16,16,256]{3,2,0,1:T(8,128)(2,1)}, u32[]{:S(2)}, u32[]{:S(2)}) async-start(bf16[3,16,16,256]{3,2,0,1:T(8,128)(2,1)} %reshape.91), calls=%async_computation.7 | async-start | bytes 786432 | tf_op jit(solution)/shard_map/all_to_all | solution.py:89
  123.9 19.0 %all-to-all-start.6 = ((bf16[3,16,16,256]{3,2,0,1:T(8,128)(2,1)}), bf16[3,16,16,256]{3,2,0,1:T(8,128)(2,1)S(1)}, u32[]{:S(2)}, u32[]{:S(2)}) async-start(bf16[3,16,16,256]{3,2,0,1:T(8,128)(2,1)} %reshape.90), calls=%async_computation.6 | async-start | bytes 786432 | tf_op jit(solution)/shard_map/all_to_all | solution.py:88
  130.9 1.8 copy-start.2
  132.7 17.9 %copy-start.5 = (bf16[3,16,2,16,16]{3,4,2,1,0:T(8,128)(2,1)}, bf16[3,16,2,16,16]{3,4,2,1,0:T(8,128)(2,1)S(1)}, u32[]{:S(2)}) copy-start(bf16[3,16,2,16,16]{3,4,2,1,0:T(8,128)(2,1)S(1)} %fusion.9) | copy-start | bytes 147460
  142.9 7.6 %copy-start.3 = (bf16[3,16,16,256]{3,2,0,1:T(8,128)(2,1)}, bf16[3,16,16,256]{3,2,0,1:T(8,128)(2,1)S(1)}, u32[]{:S(2)}) copy-start(bf16[3,16,16,256]{3,2,0,1:T(8,128)(2,1)S(1)} %all-to-all-done.6) | copy-start | bytes 1179652
  142.9 19.1 %all-to-all-start.5 = ((bf16[3,16,16,256]{3,2,0,1:T(8,128)(2,1)}), bf16[3,16,16,256]{3,2,0,1:T(8,128)(2,1)}, u32[]{:S(2)}, u32[]{:S(2)}) async-start(bf16[3,16,16,256]{3,2,0,1:T(8,128)(2,1)} %reshape.89), calls=%async_computation.5 | async-start | bytes 786432 | tf_op jit(solution)/shard_map/all_to_all | solution.py:87
  150.5 3.0 copy-start.6
  153.8 287.6 %copy-start.4 = (bf16[3,16,16,256]{3,2,0,1:T(8,128)(2,1)S(1)}, bf16[3,16,16,256]{3,2,0,1:T(8,128)(2,1)}, u32[]{:S(2)}) copy-start(bf16[3,16,16,256]{3,2,0,1:T(8,128)(2,1)} %copy-done.3) | copy-start | bytes 1179652
  162.0 282.0 %all-to-all-start.4 = ((bf16[3,16,16,256]{3,2,0,1:T(8,128)(2,1)}), bf16[3,16,16,256]{3,2,0,1:T(8,128)(2,1)}, u32[]{:S(2)}, u32[]{:S(2)}) async-start(bf16[3,16,16,256]{3,2,0,1:T(8,128)(2,1)} %reshape.88), calls=%async_computation.4 | async-start | bytes 786432 | tf_op jit(solution)/shard_map/all_to_all | solution.py:86
Sparse Core Ops, SparseCore 0:
  10.0 60.5 all-gather.1
where the time goes:
time: 457 us; the launch traced here: 453 us
  blocking collectives  273 us (60%)
  waiting for transfers between devices  66.6 us (15%)
  starting transfers between devices  65.9 us (14%)
  local copies, waits for them, and re-layouts  21 us (5%)
  between operations  14.2 us (3%)
  matrix products  9.14 us (2%)
    psum x1, blocking collectives, local(): grad_proj = lax.psum(term, ('frame', 'dp')).astype(jnp.bfloat16)  273 us
    all_to_all x1, starting transfers between devices, local(): lax.all_to_all(queries, 'frame', split_axis=2, concat_axis=1, tiled=True)  14.3 us
    all_to_all x1, waiting for transfers between devices, local(): lax.all_to_all(keys, 'frame', split_axis=2, concat_axis=1, tiled=True)  12.7 us
    all_to_all x1, waiting for transfers between devices, local(): lax.all_to_all(queries, 'frame', split_axis=2, concat_axis=1, tiled=True)  11.7 us
    all_to_all x1, waiting for transfers between devices, local(): lax.all_to_all(attended, 'frame', split_axis=1, concat_axis=2, tiled=True)  10.5 us
  transfers between devices with their start and end apart: 9, of which 8 were waited for; matrix products, arithmetic and copies ran while one was open for 7% of the time, Pallas kernels for 0%

commit v1 on v0

v1 whole, which is shorter than its diff:
```python
import functools
import math

import jax
import jax.numpy as jnp
from jax import lax
from jax.experimental import pallas as pl
from jax.experimental.pallas import tpu as pltpu
from jax.sharding import Mesh, PartitionSpec as P

HEAD = 128
SCALE = 1.0 / math.sqrt(HEAD)
GROUP = 16
FRAME = ("zh", "x", "core")
BF16 = jnp.bfloat16
F32 = jnp.float32


def dot(a, b, dims):
    return lax.dot_general(a, b, (dims, ((), ())), preferred_element_type=F32)


def dot_nt(a, b):
    return dot(a, b, ((1,), (1,)))


def dot_nn(a, b):
    return dot(a, b, ((1,), (0,)))


def dot_tn(a, b):
    return dot(a, b, ((0,), (0,)))


def causal_mask(rows):
    r = lax.broadcasted_iota(jnp.int32, (rows, rows), 0)
    c = lax.broadcasted_iota(jnp.int32, (rows, rows), 1)
    return ((r % GROUP) == (c % GROUP)) & (c // GROUP <= r // GROUP)


def softmax(q, k):
    mask = causal_mask(q.shape[0])
    scores = jnp.where(mask, dot_nt(q, k) * SCALE, -1e30)
    top = jnp.max(scores, axis=1, keepdims=True)
    expon = jnp.where(mask, jnp.exp(scores - top), 0.0)
    return expon / jnp.sum(expon, axis=1, keepdims=True)


def forward_kernel(qkv_ref, att_ref):
    frames = qkv_ref.shape[0]
    rows = frames * GROUP
    q, k, v = (qkv_ref[:, j].reshape(rows, HEAD) for j in range(3))
    weights = softmax(q, k).astype(BF16)
    att_ref[...] = dot_nn(weights, v).astype(BF16).reshape(frames, GROUP, HEAD)


def backward_kernel(qkv_ref, g_ref, out_ref):
    frames = qkv_ref.shape[0]
    rows = frames * GROUP
    q, k, v = (qkv_ref[:, j].reshape(rows, HEAD) for j in range(3))
    g = g_ref[...].reshape(rows, HEAD)
    probs = softmax(q, k)
    weights = probs.astype(BF16)
    grad_probs = dot_nt(g, v)
    total = jnp.sum(probs * grad_probs, axis=1, keepdims=True)
    grad_scores = (probs * (grad_probs - total) * SCALE).astype(BF16)
    shape = (frames, GROUP, HEAD)
    out_ref[:, 0] = dot_nn(grad_scores, k).astype(BF16).reshape(shape)
    out_ref[:, 1] = dot_tn(grad_scores, q).astype(BF16).reshape(shape)
    out_ref[:, 2] = dot_tn(weights, g).astype(BF16).reshape(shape)


def project_kernel(grad_ref, w_ref, att_ref, g_ref, term_ref, acc_ref):
    step = pl.program_id(0)
    block = grad_ref[0]
    part = dot_nt(block, w_ref[...])

    @pl.when(step == 0)
    def _():
        acc_ref[...] = part

    @pl.when(step > 0)
    def _():
        acc_ref[...] += part

    term_ref[...] = dot_tn(att_ref[...], block).astype(BF16)

    @pl.when(step == pl.num_programs(0) - 1)
    def _():
        g_ref[...] = acc_ref[...].astype(BF16)


def forward(qkv):
    frames, _, items, width = qkv.shape
    return pl.pallas_call(
        forward_kernel,
        grid=(items // GROUP, width // HEAD),
        in_specs=[pl.BlockSpec((frames, 3, GROUP, HEAD), lambda i, h: (0, 0, i, h))],
        out_specs=pl.BlockSpec((frames, GROUP, HEAD), lambda i, h: (0, i, h)),
        out_shape=jax.ShapeDtypeStruct((frames, items, width), BF16),
        cost_estimate=pl.CostEstimate(flops=400_000_000, bytes_accessed=1_600_000, transcendentals=400_000),
        name="attention_forward",
    )(qkv)


def backward(qkv, g):
    frames, _, items, width = qkv.shape
    return pl.pallas_call(
        backward_kernel,
        grid=(items // GROUP, width // HEAD),
        in_specs=[
            pl.BlockSpec((frames, 3, GROUP, HEAD), lambda i, h: (0, 0, i, h)),
            pl.BlockSpec((frames, GROUP, HEAD), lambda i, h: (0, i, h)),
        ],
        out_specs=pl.BlockSpec((frames, 3, GROUP, HEAD), lambda i, h: (0, 0, i, h)),
        out_shape=jax.ShapeDtypeStruct(qkv.shape, BF16),
        cost_estimate=pl.CostEstimate(flops=1_000_000_000, bytes_accessed=3_000_000, transcendentals=400_000),
        name="attention_backward",
    )(qkv, g)


def project(grad_all, w, att):
    parts, tokens, width = grad_all.shape
    return pl.pallas_call(
        project_kernel,
        grid=(parts,),
        in_specs=[
            pl.BlockSpec((1, tokens, width), lambda s: (s, 0, 0)),
            pl.BlockSpec((width, width), lambda s: (0, s)),
            pl.BlockSpec((tokens, width), lambda s: (0, 0)),
        ],
        out_specs=[
            pl.BlockSpec((tokens, width), lambda s: (0, 0)),
            pl.BlockSpec((width, width), lambda s: (0, s)),
        ],
        out_shape=[
            jax.ShapeDtypeStruct((tokens, width), BF16),
            jax.ShapeDtypeStruct((width, parts * width), BF16),
        ],
        scratch_shapes=[pltpu.VMEM((tokens, width), F32)],
        compiler_params=pltpu.CompilerParams(vmem_limit_bytes=16 * 1024 * 1024),
        cost_estimate=pl.CostEstimate(flops=1_600_000_000, bytes_accessed=6_000_000, transcendentals=0),
        name="projections",
    )(grad_all, w, att)


def exchange(x, axes):
    return lax.all_to_all(x, axes, 0, 0, tiled=True)


def scatter_sum(x, axes, size):
    parts = exchange(x.reshape(size, -1, x.shape[-1]), axes)
    return jnp.sum(parts.astype(F32), axis=0)


def gather(x, axes, size):
    return exchange(jnp.broadcast_to(x[None], (size,) + x.shape), axes).reshape(-1, x.shape[-1])


def local(queries, keys, values, out_grad, out_proj):
    clips, _, patches, width = queries.shape
    frames = lax.axis_size(FRAME)
    tokens = clips * patches
    items = tokens // frames
    factor = 1.0 / math.sqrt(tokens * frames * lax.axis_size("dp"))

    grad_own = exchange(out_grad.reshape(frames, items, width), FRAME)
    grad_all = lax.all_gather(grad_own.reshape(tokens, width), "tensor")
    qkv = jnp.stack([a.reshape(frames, items, width) for a in (queries, keys, values)], axis=1)
    qkv = exchange(qkv, FRAME)
    att = forward(qkv)
    g, term = project(grad_all, out_proj, att.reshape(tokens, width))
    grads = backward(qkv, g.reshape(frames, items, width))

    total = scatter_sum(term, "core", 2).astype(BF16)
    total = scatter_sum(total, "x", 4).astype(BF16)
    total = (scatter_sum(total, ("zh", "dp"), 8) * factor).astype(BF16)
    total = gather(total, ("zh", "dp"), 8)
    total = gather(total, "x", 4)
    grad_proj = gather(total, "core", 2)

    home = exchange(grads, FRAME)
    return tuple(home[:, j].reshape(queries.shape) for j in range(3)) + (grad_proj,)


def solution(mesh):
    fine = Mesh(mesh.devices.reshape(2, 4, 2, 8, 4), ("zh", "x", "core", "tensor", "dp"))
    spec = P("dp", FRAME, None, "tensor")
    return jax.shard_map(
        local,
        mesh=fine,
        in_specs=(spec, spec, spec, spec, P("tensor", None)),
        out_specs=(spec, spec, spec, P("tensor", None)),
        check_vma=False,
    )
```

time: 457 us -> 203 us (0.44)
  the two profiles are of different devices: /device:TPU:1 before, /device:TPU:64 now
where the time goes in v1:
time: 203 us; the launch traced here: 202 us
  blocking collectives  117 us (58%)
  waiting for transfers between devices  36.3 us (18%)
  Pallas kernels  19.6 us (10%)
  between operations  14.2 us (7%)
  starting transfers between devices  7.65 us (4%)
  local copies, waits for them, and re-layouts  6.73 us (3%)
    all_to_all x7, blocking collectives, exchange(): return lax.all_to_all(x, axes, 0, 0, tiled=True)  117 us
    all_to_all x2, waiting for transfers between devices, exchange(): return lax.all_to_all(x, axes, 0, 0, tiled=True)  35.7 us
    all_to_all x2, starting transfers between devices, exchange(): return lax.all_to_all(x, axes, 0, 0, tiled=True)  7.61 us
    pallas_call x1, Pallas kernels, project(): pl.pallas_call(project_kernel, grid=(parts,), in_specs=[pl.BlockSpec((1,...  6.95 us
    pallas_call x1, Pallas kernels, backward(): pl.pallas_call(backward_kernel, grid=(items // GROUP, width // HEAD), in_...  6.79 us
    pallas_call x1, Pallas kernels, forward(): pl.pallas_call(forward_kernel, grid=(items // GROUP, width // HEAD), in_s...  5.85 us
    unnamed x15, local copies, waits for them, and re-layouts  4.61 us
  transfers between devices with their start and end apart: 3, of which 3 were waited for; matrix products, arithmetic and copies ran while one was open for 0% of the time, Pallas kernels for 6%

profile of v1, /device:TPU:64, one launch (start us, length us, event | category | flops | bytes accessed | tf_op | source)
XLA Modules:
  0.0 202.1 jit_solution(12034752962049633882)
XLA Ops:
  7.2 0.0 copy-start.4
  7.2 0.0 copy-start.5
  7.2 0.0 copy-start.6
  7.2 0.0 all-gather.2.cloned.1.call-start
  7.2 29.8 %all_to_all.45 = bf16[16,48,256]{2,1,0:T(8,128)(2,1)} all-to-all(bf16[16,48,256]{2,1,0:T(8,128)(2,1)} %bitcast.33), channel_id=1, replica_groups=mesh['zh'=2,'x'=4,'core'=2,'tensor'=8,'dp'=4] {'zh','x','core'}, dimensions={0} | all-to-all | bytes 786432 | tf_op jit(solution)/shard_map/all_to_all | solution.py:148
  37.0 0.0 all-gather.2.cloned.1.call-update
  37.0 0.0 copy-done.4
  37.0 0.0 copy-done.5
  37.1 0.0 copy-done.6
  37.1 0.1 pad_maximum_fusion
  37.2 37.5 %all_to_all.46.qkv_ref = bf16[16,3,48,256]{3,2,1,0:T(8,128)(2,1)} all-to-all(bf16[16,3,48,256]{3,2,1,0:T(8,128)(2,1)S(1)} %pad_maximum_fusion), channel_id=1, replica_groups=mesh['zh'=2,'x'=4,'core'=2,'tensor'=8,'dp'=4] {'zh','x','core'}, dimensions={0} | all-to-all | bytes 2359296 | tf_op jit(solution)/shard_map/all_to_all | solution.py:148
  74.7 0.0 copy-start.2
  74.7 5.8 %attention_forward.1 = bf16[16,48,256]{2,1,0:T(8,128)(2,1)} custom-call(bf16[16,3,48,256]{3,2,1,0:T(8,128)(2,1)} %all_to_all.46.qkv_ref), custom_call_target="tpu_custom_call" | custom-call | flops 400000000 | bytes 1600000 | tf_op jit(solution)/shard_map/attention_forward/pallas_call | solution.py:95
  80.5 0.6 all-gather.2.cloned.1.call-done.grad_ref
  81.2 0.0 copy-done.2
  81.2 0.0 copy-start
  81.2 1.0 copy-done
  82.2 0.0 copy-start.1
  82.2 1.9 copy-done.1
  84.1 7.0 %projections.1 = (bf16[768,256]{1,0:T(8,128)(2,1)S(1)}, bf16[256,2048]{1,0:T(8,128)(2,1)S(1)}) custom-call(bf16[8,768,256]{2,1,0:T(8,128)(2,1)S(1)} %copy-done.1, bf16[256,2048]{1,0:T(8,128)(2,1)S(1)} %copy-done.2, bf16[768,256]{1,0:T(8,128)(2,1)S(1)} %bitcast.21), custom_call_target="tpu_custom_call" | custom-call | flops 1600000000 | bytes 6000000 | tf_op jit(solution)/shard_map/projections/pallas_call | solution.py:124
  91.0 0.0 copy-start.3
  91.0 0.7 copy-done.3
  91.8 4.6 %all_to_all.47 = bf16[2,128,2048]{2,1,0:T(8,128)(2,1)S(1)} all-to-all(bf16[2,128,2048]{2,1,0:T(8,128)(2,1)S(1)} %bitcast.20), channel_id=1, replica_groups=mesh['zh'=2,'x'=4,'core'=2,'tensor'=8,'dp'=4] {'core'}, dimensions={0} | all-to-all | bytes 2097152 | tf_op jit(solution)/shard_map/all_to_all | solution.py:148
  96.3 0.3 reduce_sum.33
  96.7 13.9 %all_to_all.48 = bf16[4,32,2048]{2,1,0:T(8,128)(2,1)S(1)} all-to-all(bf16[4,32,2048]{2,1,0:T(8,128)(2,1)S(1)} %bitcast.25), channel_id=1, replica_groups=mesh['zh'=2,'x'=4,'core'=2,'tensor'=8,'dp'=4] {'x'}, dimensions={0} | all-to-all | bytes 1048576 | tf_op jit(solution)/shard_map/all_to_all | solution.py:148
  110.5 0.1 reduce_sum.34
  110.6 0.1 reshape.40
  110.7 15.2 %all_to_all.49 = bf16[8,4,2048]{2,1,0:T(4,128)(2,1)S(1)} all-to-all(bf16[8,4,2048]{2,1,0:T(4,128)(2,1)S(1)} %reshape.40), channel_id=1, replica_groups=mesh['zh'=2,'x'=4,'core'=2,'tensor'=8,'dp'=4] {'zh','dp'}, dimensions={0} | all-to-all | bytes 262144 | tf_op jit(solution)/shard_map/all_to_all | solution.py:148
  125.8 0.2 convert_reduce_fusion
  126.1 11.5 %all_to_all.50 = bf16[8,4,2048]{2,1,0:T(4,128)(2,1)S(1)} all-to-all(bf16[8,4,2048]{2,1,0:T(4,128)(2,1)S(1)} %broadcast_in_dim.20), channel_id=1, replica_groups=mesh['zh'=2,'x'=4,'core'=2,'tensor'=8,'dp'=4] {'zh','dp'}, dimensions={0} | all-to-all | bytes 262144 | tf_op jit(solution)/shard_map/all_to_all | solution.py:148
  137.6 0.8 broadcast_in_dim.22
  138.4 3.5 %all-to-all-start.7 = ((bf16[4,32,2048]{2,1,0:T(8,128)(2,1)}), bf16[4,32,2048]{2,1,0:T(8,128)(2,1)S(1)}, u32[]{:S(2)}, u32[]{:S(2)}) async-start(bf16[4,32,2048]{2,1,0:T(8,128)(2,1)} %broadcast_in_dim.22), calls=%async_computation.7 | async-start | bytes 1048576 | tf_op jit(solution)/shard_map/all_to_all | solution.py:148
  141.9 6.8 %attention_backward.1 = bf16[16,3,48,256]{3,2,1,0:T(8,128)(2,1)} custom-call(bf16[16,3,48,256]{3,2,1,0:T(8,128)(2,1)} %all_to_all.46.qkv_ref, bf16[16,48,256]{2,1,0:T(8,128)(2,1)} %bitcast.22), custom_call_target="tpu_custom_call" | custom-call | flops 1000000000 | bytes 3000000 | tf_op jit(solution)/shard_map/attention_backward/pallas_call | solution.py:108
  148.7 1.3 all-to-all-done.7
  149.9 0.1 broadcast_in_dim.24
  150.1 4.6 %all_to_all.51 = bf16[2,128,2048]{2,1,0:T(8,128)(2,1)S(1)} all-to-all(bf16[2,128,2048]{2,1,0:T(8,128)(2,1)S(1)} %broadcast_in_dim.24), channel_id=1, replica_groups=mesh['zh'=2,'x'=4,'core'=2,'tensor'=8,'dp'=4] {'core'}, dimensions={0} | all-to-all | bytes 2097152 | tf_op jit(solution)/shard_map/all_to_all | solution.py:148
  154.6 4.1 %all-to-all-start.2 = ((bf16[16,3,48,256]{3,2,1,0:T(8,128)(2,1)}), bf16[16,3,48,256]{3,2,1,0:T(8,128)(2,1)S(1)}, u32[]{:S(2)}, u32[]{:S(2)}) async-start(bf16[16,3,48,256]{3,2,1,0:T(8,128)(2,1)} %attention_backward.1), calls=%async_computation.2 | async-start | bytes 2359296 | tf_op jit(solution)/shard_map/all_to_all | solution.py:148
  158.8 34.4 %all-to-all-done.2 = bf16[16,3,48,256]{3,2,1,0:T(8,128)(2,1)S(1)} async-done(((bf16[16,3,48,256]{3,2,1,0:T(8,128)(2,1)}), bf16[16,3,48,256]{3,2,1,0:T(8,128)(2,1)S(1)}, u32[]{:S(2)}, u32[]{:S(2)}) %all-to-all-start.2) | async-done | bytes 1179680 | tf_op jit(solution)/shard_map/all_to_all | solution.py:148
  193.2 1.0 fusion
  194.2 1.0 copy.29
  (3 shorter events, 0.1 us)
Async XLA Ops:
  7.2 29.9 %copy-start.4 = (bf16[3,1,256,256]{3,2,1,0:T(8,128)(2,1)S(1)}, bf16[3,1,256,256]{3,2,1,0:T(8,128)(2,1)}, u32[]{:S(2)}) copy-start(bf16[3,1,256,256]{3,2,1,0:T(8,128)(2,1)} %param.7) | copy-start | bytes 1179652
  7.2 29.9 %copy-start.5 = (bf16[3,1,256,256]{3,2,1,0:T(8,128)(2,1)S(1)}, bf16[3,1,256,256]{3,2,1,0:T(8,128)(2,1)}, u32[]{:S(2)}) copy-start(bf16[3,1,256,256]{3,2,1,0:T(8,128)(2,1)} %param.6) | copy-start | bytes 1179652
  7.2 29.9 %copy-start.6 = (bf16[3,1,256,256]{3,2,1,0:T(8,128)(2,1)S(1)}, bf16[3,1,256,256]{3,2,1,0:T(8,128)(2,1)}, u32[]{:S(2)}) copy-start(bf16[3,1,256,256]{3,2,1,0:T(8,128)(2,1)} %param.5) | copy-start | bytes 1179652
  7.2 74.0 %all-gather.2.cloned.1.call-start = ((), (), s32[]{:S(2)}) async-start(), calls=%async_computation.9 | async-start | bytes 3538944 | tf_op jit(solution)/shard_map/all_gather | solution.py:168
  74.7 6.5 %copy-start.2 = (bf16[256,2048]{1,0:T(8,128)(2,1)S(1)}, bf16[256,2048]{1,0:T(8,128)(2,1)}, u32[]{:S(2)}) copy-start(bf16[256,2048]{1,0:T(8,128)(2,1)} %w_ref.1) | copy-start | bytes 3145732
  81.2 1.0 copy-start
  82.2 1.9 copy-start.1
  91.0 0.7 copy-start.3
  138.4 11.5 %all-to-all-start.7 = ((bf16[4,32,2048]{2,1,0:T(8,128)(2,1)}), bf16[4,32,2048]{2,1,0:T(8,128)(2,1)S(1)}, u32[]{:S(2)}, u32[]{:S(2)}) async-start(bf16[4,32,2048]{2,1,0:T(8,128)(2,1)} %broadcast_in_dim.22), calls=%async_computation.7 | async-start | bytes 1048576 | tf_op jit(solution)/shard_map/all_to_all | solution.py:148
  154.6 38.6 %all-to-all-start.2 = ((bf16[16,3,48,256]{3,2,1,0:T(8,128)(2,1)}), bf16[16,3,48,256]{3,2,1,0:T(8,128)(2,1)S(1)}, u32[]{:S(2)}, u32[]{:S(2)}) async-start(bf16[16,3,48,256]{3,2,1,0:T(8,128)(2,1)} %attention_backward.1), calls=%async_computation.2 | async-start | bytes 2359296 | tf_op jit(solution)/shard_map/all_to_all | solution.py:148
Sparse Core Ops, SparseCore 0:
  37.2 43.9 all-gather.1

commit v2 on v1

v2 whole, which is shorter than its diff:
```python
import functools
import math

import jax
import jax.numpy as jnp
from jax import lax
from jax.experimental import pallas as pl
from jax.experimental.pallas import tpu as pltpu
from jax.sharding import Mesh, PartitionSpec as P

HEAD = 128
SCALE = 1.0 / math.sqrt(HEAD)
MASKED = -1e30
GROUP = 16
STEP = 2
NEAR = ("x", "core")
BF16 = jnp.bfloat16
F32 = jnp.float32
SMEM = pl.BlockSpec(memory_space=pltpu.SMEM)
PARAMS = pltpu.CompilerParams(vmem_limit_bytes=32 * 1024 * 1024)


def dot(a, b, dims):
    return lax.dot_general(a, b, (dims, ((), ())), preferred_element_type=F32)


def dot_nt(a, b):
    return dot(a, b, ((1,), (1,)))


def dot_nn(a, b):
    return dot(a, b, ((1,), (0,)))


def dot_tn(a, b):
    return dot(a, b, ((0,), (0,)))


def masks(rows, crossing):
    key = lax.broadcasted_iota(jnp.int32, (rows, rows), 0)
    query = lax.broadcasted_iota(jnp.int32, (rows, rows), 1)
    own = (key % GROUP == query % GROUP) & (key // GROUP <= query // GROUP)
    cross = key % GROUP == query % GROUP + jnp.where(crossing, 0, GROUP)
    return own, cross


def scores_of(mask, keys, queries):
    return jnp.where(mask, dot_nt(keys, queries) * SCALE, MASKED)


def head_slices(ref):
    return [slice(h * HEAD, (h + 1) * HEAD) for h in range(ref.shape[-1] // HEAD)]


def take(ref, j, cols):
    return ref[:, j, :, cols].reshape(-1, HEAD)


def softmax(q, k, k_cross, own_mask, cross_mask):
    s_own, s_cross = scores_of(own_mask, k, q), scores_of(cross_mask, k_cross, q)
    top = jnp.maximum(jnp.max(s_own, axis=0, keepdims=True), jnp.max(s_cross, axis=0, keepdims=True))
    e_own, e_cross = jnp.exp(s_own - top), jnp.exp(s_cross - top)
    total = jnp.sum(e_own, axis=0, keepdims=True) + jnp.sum(e_cross, axis=0, keepdims=True)
    return e_own / total, e_cross / total, top, total


def attend_kernel(side_ref, q_ref, kv_ref, recv_ref, att_ref):
    frames = q_ref.shape[0]
    own_mask, cross_mask = masks(frames * GROUP, side_ref[0] == 1)
    for cols in head_slices(q_ref):
        (k, v), (k_cross, v_cross) = ([take(ref, j, cols) for j in range(2)] for ref in (kv_ref, recv_ref))
        q = q_ref[:, :, cols].reshape(-1, HEAD)
        p_own, p_cross, _, _ = softmax(q, k, k_cross, own_mask, cross_mask)
        att = dot_tn(p_own.astype(BF16), v) + dot_tn(p_cross.astype(BF16), v_cross)
        att_ref[:, :, cols] = att.astype(BF16).reshape(frames, GROUP, HEAD)


def query_kernel(side_ref, q_ref, kv_ref, recv_ref, g_ref, out_ref, stats_ref):
    frames = q_ref.shape[0]
    own_mask, cross_mask = masks(frames * GROUP, side_ref[0] == 1)
    for h, cols in enumerate(head_slices(q_ref)):
        (k, v), (k_cross, v_cross) = ([take(ref, j, cols) for j in range(2)] for ref in (kv_ref, recv_ref))
        q = q_ref[:, :, cols].reshape(-1, HEAD)
        p_own, p_cross, top, total = softmax(q, k, k_cross, own_mask, cross_mask)
        g = g_ref[:, :, cols].reshape(-1, HEAD)
        gp_own, gp_cross = dot_nt(v, g), dot_nt(v_cross, g)
        row = jnp.sum(p_own * gp_own, axis=0, keepdims=True) + jnp.sum(p_cross * gp_cross, axis=0, keepdims=True)
        ds_own = (p_own * (gp_own - row) * SCALE).astype(BF16)
        ds_cross = (p_cross * (gp_cross - row) * SCALE).astype(BF16)
        grad = dot_tn(ds_own, k) + dot_tn(ds_cross, k_cross)
        out_ref[:, :, cols] = grad.astype(BF16).reshape(frames, GROUP, HEAD)
        for j, stat in enumerate((top, total, row)):
            stats_ref[0, 3 * h + j : 3 * h + j + 1] = stat


def key_kernel(side_ref, q_ref, kv_ref, q_recv_ref, g_ref, g_recv_ref, stats_ref, stats_recv_ref, gq_ref, out_ref):
    frames = q_ref.shape[0]
    shape = (frames, GROUP, HEAD)
    own_mask, cross_mask = masks(frames * GROUP, side_ref[0] == 0)
    out_ref[:, 0] = gq_ref[...]
    for h, cols in enumerate(head_slices(q_ref)):
        k, v = take(kv_ref, 0, cols), take(kv_ref, 1, cols)
        grad_k, grad_v = 0.0, 0.0
        for mask, q, g, stats in (
            (own_mask, q_ref[:, :, cols], g_ref[:, :, cols], stats_ref),
            (cross_mask, q_recv_ref[:, :, cols], g_recv_ref[:, :, cols], stats_recv_ref),
        ):
            top, total, row = (stats[0, 3 * h + j : 3 * h + j + 1] for j in range(3))
            q, g = q.reshape(-1, HEAD), g.reshape(-1, HEAD)
            probs = jnp.where(mask, jnp.exp(scores_of(mask, k, q) - top) / total, 0.0)
            ds = (probs * (dot_nt(v, g) - row) * SCALE).astype(BF16)
            grad_k = grad_k + dot_nn(ds, q)
            grad_v = grad_v + dot_nn(probs.astype(BF16), g)
        out_ref[:, 1, :, cols] = grad_k.astype(BF16).reshape(shape)
        out_ref[:, 2, :, cols] = grad_v.astype(BF16).reshape(shape)


def project_kernel(offsets, place_ref, w_ref, att_ref, *refs):
    blocks, (g_ref, term_ref) = refs[:-2], refs[-2:]
    width = w_ref.shape[0]
    parts = w_ref.shape[1] // width
    half = att_ref.shape[0] // 2

    def columns(offset):
        owner = lax.rem(place_ref[0] + offset + parts, parts)
        return pl.ds(pl.multiple_of(owner * width, width), width)

    acc = 0.0
    for offset, ref in zip(offsets, blocks[:-2]):
        acc = acc + dot_nt(ref[...], w_ref[:, columns(offset)])
        term_ref[:, columns(offset)] = dot_tn(att_ref[...], ref[...]).astype(BF16)
    last = columns(parts // 2)
    low, high = blocks[-2][...], blocks[-1][...]
    g_ref[:half] = (acc[:half] + dot_nt(low, w_ref[:, last])).astype(BF16)
    g_ref[half:] = (acc[half:] + dot_nt(high, w_ref[:, last])).astype(BF16)
    term_ref[:, last] = (dot_tn(att_ref[:half], low) + dot_tn(att_ref[half:], high)).astype(BF16)


def per_group(kernel, name, flops, side, args, outs, vmem=32):
    items = args[0].shape[-2]

    def spec(a):
        if a.dtype == F32:
            return pl.BlockSpec((1,) + a.shape[1:], lambda i: (i, 0, 0))
        block = a.shape[:-2] + (GROUP, a.shape[-1])
        lead = (0,) * (len(a.shape) - 2)
        return pl.BlockSpec(block, lambda i: lead + (i, 0))

    return pl.pallas_call(
        kernel,
        grid=(items // GROUP,),
        in_specs=[SMEM] + [spec(a) for a in args],
        out_specs=[spec(a) for a in outs],
        out_shape=[jax.ShapeDtypeStruct(a.shape, a.dtype) for a in outs],
        compiler_params=pltpu.CompilerParams(vmem_limit_bytes=vmem * 1024 * 1024),
        cost_estimate=pl.CostEstimate(flops=flops, bytes_accessed=4_000_000, transcendentals=400_000),
        name=name,
    )(side, *args)


def project(blocks, offsets, w, att):
    tokens, width = att.shape
    vmem = pl.BlockSpec(memory_space=pltpu.VMEM)
    return pl.pallas_call(
        functools.partial(project_kernel, offsets),
        in_specs=[pl.BlockSpec(memory_space=pltpu.SMEM)] + [vmem] * (2 + len(blocks)),
        out_specs=[vmem, vmem],
        out_shape=[
            jax.ShapeDtypeStruct((tokens, width), BF16),
            jax.ShapeDtypeStruct(w.shape, BF16),
        ],
        compiler_params=pltpu.CompilerParams(vmem_limit_bytes=24 * 1024 * 1024),
        cost_estimate=pl.CostEstimate(flops=1_600_000_000, bytes_accessed=6_000_000, transcendentals=0),
        name="projections",
    )(lax.axis_index("tensor").reshape(1), w, att, *blocks)


def exchange(x, axes):
    return lax.all_to_all(x, axes, 0, 0, tiled=True)


def scatter_sum(x, axes):
    parts = exchange(x.reshape(lax.axis_size(axes), -1, x.shape[-1]), axes)
    return jnp.sum(parts.astype(F32), axis=0)


def shift(x, axis, by):
    size = lax.axis_size(axis)
    return lax.ppermute(x, axis, [(i, (i + by) % size) for i in range(size)])


def ring(x):
    size = lax.axis_size("tensor")
    half = x.shape[0] // 2
    blocks, offsets, up, down = [x], [0], x, x
    for step in range(1, size // 2):
        up, down = shift(up, "tensor", 1), shift(down, "tensor", -1)
        blocks += [up, down]
        offsets += [-step, step]
    blocks += [shift(up[:half], "tensor", 1), shift(down[half:], "tensor", -1)]
    return blocks, offsets


def gather(x, axes):
    copies = jnp.broadcast_to(x[None], (lax.axis_size(axes),) + x.shape)
    return exchange(copies, axes).reshape(-1, x.shape[-1])


def local(queries, keys, values, out_grad, out_proj):
    clips, _, patches, width = queries.shape
    near = lax.axis_size(NEAR)
    tokens = clips * patches
    items = tokens // near
    factor = 1.0 / math.sqrt(tokens * near * lax.axis_size("zh") * lax.axis_size("dp"))
    side = lax.axis_index("zh").astype(jnp.int32).reshape(1)
    queries, keys, values, out_grad = (a.reshape(near, items, width) for a in (queries, keys, values, out_grad))

    grad_own = exchange(out_grad, NEAR).reshape(tokens, width)
    qkv, grad_own = lax.optimization_barrier((jnp.stack([queries, keys, values], axis=1), grad_own))
    qkv = exchange(qkv, NEAR)
    q, kv = qkv[:, 0], qkv[:, 1:]
    kv_recv = lax.ppermute(kv, "zh", [(0, 1)])
    blocks, offsets = ring(grad_own)
    like = jax.ShapeDtypeStruct(q.shape, BF16)
    q_recv = lax.ppermute(q, "zh", [(1, 0)])
    (att,) = per_group(attend_kernel, "attend", 400_000_000, side, [q, kv, kv_recv], [like])
    g, term = project(blocks, offsets, out_proj, att.reshape(tokens, width))
    g, term, q_recv = lax.optimization_barrier((g, term, q_recv))
    g = g.reshape(att.shape)
    g_recv = lax.ppermute(g, "zh", [(1, 0)])

    stats = jax.ShapeDtypeStruct((items // GROUP, 8, near * GROUP), F32)
    grad_q, stats = per_group(query_kernel, "grad_queries", 700_000_000, side, [q, kv, kv_recv, g], [like, stats])

    total = scatter_sum(term, "x").astype(BF16)
    total = scatter_sum(total, "core").astype(BF16)
    total, g_recv, grad_q, stats = lax.optimization_barrier((total, g_recv, grad_q, stats))
    stats_recv = lax.ppermute(stats, "zh", [(1, 0)])
    total = (scatter_sum(total, ("zh", "dp")) * factor).astype(BF16)
    total, stats_recv = lax.optimization_barrier((total, stats_recv))
    args = [q, kv, q_recv, g, g_recv, stats, stats_recv, grad_q]
    grads = jax.ShapeDtypeStruct((near, 3, items, width), BF16)
    (grads,) = per_group(key_kernel, "grad_keys_values", 1_000_000_000, side, args, [grads], 60)
    total = gather(total, ("zh", "dp"))
    total, grads = lax.optimization_barrier((total, grads))
    home = exchange(grads, NEAR)
    total, home = lax.optimization_barrier((total, home))
    total = gather(total, "x")
    grad_proj = gather(total, "core").reshape(lax.axis_size("core"), lax.axis_size("x"), -1, total.shape[-1])
    grad_proj = jnp.swapaxes(grad_proj, 0, 1).reshape(out_proj.shape)
    return tuple(home[:, j].reshape(clips, 1, patches, width) for j in range(3)) + (grad_proj,)


def solution(mesh):
    fine = Mesh(mesh.devices.reshape(2, 4, 2, 8, 4), ("zh", "x", "core", "tensor", "dp"))
    spec = P("dp", ("zh", "x", "core"), None, "tensor")
    return jax.shard_map(
        local,
        mesh=fine,
        in_specs=(spec, spec, spec, spec, P("tensor", None)),
        out_specs=(spec, spec, spec, P("tensor", None)),
        check_vma=False,
    )
```

time: 203 us -> 197 us (0.970)
  the two profiles are of different devices: /device:TPU:64 before, /device:TPU:1 now
where the time goes in v2:
time: 197 us; the launch traced here: 196 us
  starting transfers between devices  79 us (40%)
  blocking collectives  44.3 us (22%)
  waiting for transfers between devices  36.1 us (18%)
  Pallas kernels  20.5 us (10%)
  local copies, waits for them, and re-layouts  12.1 us (6%)
  other arithmetic  2.81 us (1%)
    all_to_all x3, blocking collectives, exchange(): return lax.all_to_all(x, axes, 0, 0, tiled=True)  44.3 us
    all_to_all x6, starting transfers between devices, exchange(): return lax.all_to_all(x, axes, 0, 0, tiled=True)  42.1 us
    ppermute x8, starting transfers between devices, shift(): return lax.ppermute(x, axis, [(i, (i + by) % size) for i in range(size)])  25.9 us
    all_to_all x6, waiting for transfers between devices, exchange(): return lax.all_to_all(x, axes, 0, 0, tiled=True)  23.6 us
    pallas_call x3, Pallas kernels, per_group(): pl.pallas_call(kernel, grid=(items // GROUP,), in_specs=[SMEM] + [spec(a)...  16.5 us
    ppermute x8, waiting for transfers between devices, shift(): return lax.ppermute(x, axis, [(i, (i + by) % size) for i in range(size)])  10.8 us
    ppermute x1, starting transfers between devices, local(): kv_recv = lax.ppermute(kv, 'zh', [(0, 1)])  7.1 us
    unnamed x30, local copies, waits for them, and re-layouts  3.98 us
  transfers between devices with their start and end apart: 18, of which 8 were waited for; matrix products, arithmetic and copies ran while one was open for 4% of the time, Pallas kernels for 10%

profile of v2, /device:TPU:1, one launch (start us, length us, event | category | flops | bytes accessed | tf_op | source)
XLA Modules:
  0.0 195.7 jit_solution(1876140252969045338)
XLA Ops:
  0.6 10.2 %all-to-all-start = ((bf16[8,96,256]{2,1,0:T(8,128)(2,1)}), bf16[8,96,256]{2,1,0:T(8,128)(2,1)S(1)}, u32[]{:S(2)}, u32[]{:S(2)}) async-start(bf16[8,96,256]{2,1,0:T(8,128)(2,1)} %bitcast.46), calls=%async_computation | async-start | bytes 786432 | tf_op jit(solution)/shard_map/all_to_all | solution.py:179
  10.9 2.4 %pad_maximum_fusion = bf16[8,3,96,256]{3,2,1,0:T(8,128)(2,1)} fusion(bf16[8,1,96,256]{3,2,1,0:T(8,128)(2,1)} %bitcast.40, bf16[8,1,96,256]{3,2,1,0:T(8,128)(2,1)} %bitcast.41, bf16[8,1,96,256]{3,2,1,0:T(8,128)(2,1)} %bitcast.42), kind=kLoop, calls=%fused_computation | loop fusion | flops 1179648 | bytes 2359296 | tf_op jit(solution)/shard_map/stack | solution.py:219
  13.3 5.7 %all-to-all-done = bf16[8,96,256]{2,1,0:T(8,128)(2,1)S(1)} async-done(((bf16[8,96,256]{2,1,0:T(8,128)(2,1)}), bf16[8,96,256]{2,1,0:T(8,128)(2,1)S(1)}, u32[]{:S(2)}, u32[]{:S(2)}) %all-to-all-start) | async-done | bytes 393248 | tf_op jit(solution)/shard_map/all_to_all | solution.py:179
  19.0 5.0 %all-to-all-start.1 = ((bf16[8,3,96,256]{3,2,1,0:T(8,128)(2,1)}), bf16[8,3,96,256]{3,2,1,0:T(8,128)(2,1)}, u32[]{:S(2)}, u32[]{:S(2)}) async-start(bf16[8,3,96,256]{3,2,1,0:T(8,128)(2,1)} %pad_maximum_fusion), calls=%async_computation.1 | async-start | bytes 2359296 | tf_op jit(solution)/shard_map/all_to_all | solution.py:179
  24.0 1.9 collective-permute-start.1
  25.9 4.6 %collective-permute-start.2 = (bf16[768,256]{1,0:T(8,128)(2,1)S(1)}, bf16[768,256]{1,0:T(8,128)(2,1)S(1)}, u32[]{:S(2)}, u32[]{:S(2)}) collective-permute-start(bf16[768,256]{1,0:T(8,128)(2,1)S(1)} %bitcast.34), channel_id=1, source_target_pairs={{0,28},{4,0},{8,4},{12,8},{16,12},{20,16},{24,20},{28,24},{1,29},{... | collective-permute-start | bytes 1179656 | tf_op jit(solution)/shard_map/ppermute | solution.py:189
  30.5 7.2 %collective-permute-done.1.refs_1_ = bf16[768,256]{1,0:T(8,128)(2,1)S(1)} collective-permute-done((bf16[768,256]{1,0:T(8,128)(2,1)S(1)}, bf16[768,256]{1,0:T(8,128)(2,1)S(1)}, u32[]{:S(2)}, u32[]{:S(2)}) %collective-permute-start.1) | collective-permute-done | bytes 393248 | tf_op jit(solution)/shard_map/ppermute | solution.py:189
  37.6 1.9 collective-permute-start.3
  39.6 4.6 %collective-permute-start.4 = (bf16[768,256]{1,0:T(8,128)(2,1)S(1)}, bf16[768,256]{1,0:T(8,128)(2,1)}, u32[]{:S(2)}, u32[]{:S(2)}) collective-permute-start(bf16[768,256]{1,0:T(8,128)(2,1)S(1)} %collective-permute-done.2.refs_2_), channel_id=1, source_target_pairs={{0,28},{4,0},{8,4},{12,8},{16,12},{20,16},{24,20},{28,24},{1,29},{... | collective-permute-start | bytes 1179656 | tf_op jit(solution)/shard_map/ppermute | solution.py:189
  44.2 1.2 slice.29.kv_ref
  45.4 7.1 %collective-permute-start = (bf16[8,2,96,256]{3,2,1,0:T(8,128)(2,1)S(1)}, bf16[8,2,96,256]{3,2,1,0:T(8,128)(2,1)S(1)}, u32[]{:S(2)}, u32[]{:S(2)}) collective-permute-start(bf16[8,2,96,256]{3,2,1,0:T(8,128)(2,1)S(1)} %slice.29.kv_ref), channel_id=1, source_target_pairs={{0,256},{1,257},{2,258},{3,259},{4,260},{5,261},{6,262},{7,263},{8... | collective-permute-start | bytes 2359304 | tf_op jit(solution)/shard_map/ppermute | solution.py:222
  52.5 1.9 collective-permute-start.5
  54.5 4.6 %collective-permute-start.6 = (bf16[768,256]{1,0:T(8,128)(2,1)}, bf16[768,256]{1,0:T(8,128)(2,1)S(1)}, u32[]{:S(2)}, u32[]{:S(2)}) collective-permute-start(bf16[768,256]{1,0:T(8,128)(2,1)} %collective-permute-done.4.refs_4_), channel_id=1, source_target_pairs={{0,28},{4,0},{8,4},{12,8},{16,12},{20,16},{24,20},{28,24},{1,29},{... | collective-permute-start | bytes 1179656 | tf_op jit(solution)/shard_map/ppermute | solution.py:189
  59.0 1.0 slice_bitcast_fusion.q_ref
  60.1 1.3 collective-permute-start.9
  61.4 3.6 %collective-permute-done.5.refs_5_ = bf16[768,256]{1,0:T(8,128)(2,1)S(1)} collective-permute-done((bf16[768,256]{1,0:T(8,128)(2,1)}, bf16[768,256]{1,0:T(8,128)(2,1)S(1)}, u32[]{:S(2)}, u32[]{:S(2)}) %collective-permute-start.5) | collective-permute-done | bytes 393248 | tf_op jit(solution)/shard_map/ppermute | solution.py:189
  65.0 0.7 slice.30
  65.7 1.9 collective-permute-start.7
  67.6 0.7 slice.31
  68.3 4.6 %collective-permute-start.8 = (bf16[384,256]{1,0:T(8,128)(2,1)}, bf16[384,256]{1,0:T(8,128)(2,1)S(1)}, u32[]{:S(2)}, u32[]{:S(2)}) collective-permute-start(bf16[384,256]{1,0:T(8,128)(2,1)} %slice.31), channel_id=1, source_target_pairs={{0,28},{4,0},{8,4},{12,8},{16,12},{20,16},{24,20},{28,24},{1,29},{... | collective-permute-start | bytes 589832 | tf_op jit(solution)/shard_map/ppermute | solution.py:189
  72.9 4.6 %attend.1 = bf16[8,96,256]{2,1,0:T(8,128)(2,1)S(1)} custom-call(s32[1]{0:T(128)} %bitcast.1.side_ref, bf16[8,96,256]{2,1,0:T(8,128)(2,1)S(1)} %slice_bitcast_fusion.q_ref, bf16[8,2,96,256]{3,2,1,0:T(8,128)(2,1)S(1)} %slice.29.kv_ref, bf16[8,2,96,256]{3,2,1,0:T(8,128)(2,1)S(1)} %collective-permute-done.recv_ref), custom_call_target="tpu_custom_call" | custom-call | flops 400000000 | bytes 4000000 | tf_op jit(solution)/shard_map/attend/pallas_call | solution.py:149
  77.6 0.7 copy-done.10
  78.2 0.7 copy-done.12
  78.9 0.9 copy-done.11
  79.8 0.9 copy-done.13
  80.8 4.0 %projections.1 = (bf16[768,256]{1,0:T(8,128)(2,1)S(1)}, bf16[256,2048]{1,0:T(8,128)(2,1)}) custom-call(s32[1]{0:T(128)} %bitcast.place_ref, bf16[256,2048]{1,0:T(8,128)(2,1)S(1)} %copy-done.5, bf16[768,256]{1,0:T(8,128)(2,1)S(1)} %bitcast.32, bf16[768,256]{1,0:T(8,128)(2,1)S(1)} %bitcast.35, bf16[768,256]{1,0:T(8,128)(2,1)S(1)} %copy-done.7, ...), custom_call_target="tpu_custom_call" | custom-call | flops 1600000000 | bytes 6000000 | tf_op jit(solution)/shard_map/projections/pallas_call | solution.py:164
  84.7 3.7 %all-to-all-start.2 = ((bf16[4,64,2048]{2,1,0:T(8,128)(2,1)}), bf16[4,64,2048]{2,1,0:T(8,128)(2,1)S(1)}, u32[]{:S(2)}, u32[]{:S(2)}) async-start(bf16[4,64,2048]{2,1,0:T(8,128)(2,1)} %bitcast.9), calls=%async_computation.2 | async-start | bytes 2097152 | tf_op jit(solution)/shard_map/all_to_all | solution.py:179
  88.4 1.3 collective-permute-start.10
  89.7 5.2 %grad_queries.1 = (bf16[8,96,256]{2,1,0:T(8,128)(2,1)S(1)}, f32[6,8,128]{2,1,0:T(8,128)S(1)}) custom-call(s32[1]{0:T(128)} %bitcast.1.side_ref, bf16[8,96,256]{2,1,0:T(8,128)(2,1)S(1)} %slice_bitcast_fusion.q_ref, bf16[8,2,96,256]{3,2,1,0:T(8,128)(2,1)S(1)} %slice.29.kv_ref, bf16[8,2,96,256]{3,2,1,0:T(8,128)(2,1)S(1)} %collective-permute-done.recv_ref, ...), custom_call_target="tpu_custom_call" | custom-call | flops 700000000 | bytes 4000000 | tf_op jit(solution)/shard_map/grad_queries/pallas_call | solution.py:149
  95.0 0.7 copy-done.3
  95.7 2.4 %all-to-all-done.2 = bf16[4,64,2048]{2,1,0:T(8,128)(2,1)S(1)} async-done(((bf16[4,64,2048]{2,1,0:T(8,128)(2,1)}), bf16[4,64,2048]{2,1,0:T(8,128)(2,1)S(1)}, u32[]{:S(2)}, u32[]{:S(2)}) %all-to-all-start.2) | async-done | bytes 1048608 | tf_op jit(solution)/shard_map/all_to_all | solution.py:179
  98.4 14.8 %all_to_all.45 = bf16[2,32,2048]{2,1,0:T(8,128)(2,1)S(1)} all-to-all(bf16[2,32,2048]{2,1,0:T(8,128)(2,1)S(1)} %bitcast.38), channel_id=1, replica_groups=mesh['zh'=2,'x'=4,'core'=2,'tensor'=8,'dp'=4] {'core'}, dimensions={0} | all-to-all | bytes 524288 | tf_op jit(solution)/shard_map/all_to_all | solution.py:179
  113.3 0.7 reshape.52
  114.0 16.3 %all-to-all-start.4 = ((bf16[8,4,2048]{2,1,0:T(4,128)(2,1)}), bf16[8,4,2048]{2,1,0:T(4,128)(2,1)S(1)}, u32[]{:S(2)}, u32[]{:S(2)}) async-start(bf16[8,4,2048]{2,1,0:T(4,128)(2,1)} %reshape.52), calls=%async_computation.4 | async-start | bytes 262144 | tf_op jit(solution)/shard_map/all_to_all | solution.py:179
  130.3 1.3 collective-permute-start.11
  131.6 6.6 %all-to-all-done.4 = bf16[8,4,2048]{2,1,0:T(4,128)(2,1)S(1)} async-done(((bf16[8,4,2048]{2,1,0:T(4,128)(2,1)}), bf16[8,4,2048]{2,1,0:T(4,128)(2,1)S(1)}, u32[]{:S(2)}, u32[]{:S(2)}) %all-to-all-start.4) | async-done | bytes 131104 | tf_op jit(solution)/shard_map/all_to_all | solution.py:179
  138.4 1.7 collective-permute-done.11.stats_recv_ref
  140.1 0.7 broadcast_in_dim.8
  140.8 3.4 %all-to-all-start.5 = ((bf16[8,4,2048]{2,1,0:T(4,128)(2,1)}), bf16[8,4,2048]{2,1,0:T(4,128)(2,1)S(1)}, u32[]{:S(2)}, u32[]{:S(2)}) async-start(bf16[8,4,2048]{2,1,0:T(4,128)(2,1)} %broadcast_in_dim.8), calls=%async_computation.5 | async-start | bytes 262144 | tf_op jit(solution)/shard_map/all_to_all | solution.py:179
  144.1 6.7 %grad_keys_values.1 = bf16[8,3,96,256]{3,2,1,0:T(8,128)(2,1)} custom-call(s32[1]{0:T(128)} %bitcast.1.side_ref, bf16[8,96,256]{2,1,0:T(8,128)(2,1)} %copy-done.1, bf16[8,2,96,256]{3,2,1,0:T(8,128)(2,1)} %copy-done, bf16[8,96,256]{2,1,0:T(8,128)(2,1)} %collective-permute-done.9.q_recv_ref, bf16[8,96,256]{2,1,0:T(8,128)(2,1)} %bitcast.31, ...), custom_call_target="tpu_custom_call" | custom-call | flops 1000000000 | bytes 4000000 | tf_op jit(solution)/shard_map/grad_keys_values/pallas_call | solution.py:149
  150.8 1.3 all-to-all-done.5
  152.1 23.5 %all_to_all.46 = bf16[8,3,96,256]{3,2,1,0:T(8,128)(2,1)S(1)} all-to-all(bf16[8,3,96,256]{3,2,1,0:T(8,128)(2,1)} %grad_keys_values.1), channel_id=1, replica_groups=mesh['zh'=2,'x'=4,'core'=2,'tensor'=8,'dp'=4] {'x','core'}, dimensions={0} | all-to-all | bytes 2359296 | tf_op jit(solution)/shard_map/all_to_all | solution.py:179
  175.6 0.8 broadcast_in_dim.9
  176.4 3.5 %all-to-all-start.7 = ((bf16[4,32,2048]{2,1,0:T(8,128)(2,1)}), bf16[4,32,2048]{2,1,0:T(8,128)(2,1)S(1)}, u32[]{:S(2)}, u32[]{:S(2)}) async-start(bf16[4,32,2048]{2,1,0:T(8,128)(2,1)} %broadcast_in_dim.9), calls=%async_computation.7 | async-start | bytes 1048576 | tf_op jit(solution)/shard_map/all_to_all | solution.py:179
  179.9 1.0 fusion
  180.9 7.6 %all-to-all-done.7 = bf16[4,32,2048]{2,1,0:T(8,128)(2,1)S(1)} async-done(((bf16[4,32,2048]{2,1,0:T(8,128)(2,1)}), bf16[4,32,2048]{2,1,0:T(8,128)(2,1)S(1)}, u32[]{:S(2)}, u32[]{:S(2)}) %all-to-all-start.7) | async-done | bytes 524320 | tf_op jit(solution)/shard_map/all_to_all | solution.py:179
  188.7 6.0 %all_to_all.47 = bf16[2,128,2048]{2,1,0:T(8,128)(2,1)S(1)} all-to-all(bf16[2,128,2048]{2,1,0:T(8,128)(2,1)S(1)} %broadcast_in_dim.22), channel_id=1, replica_groups=mesh['zh'=2,'x'=4,'core'=2,'tensor'=8,'dp'=4] {'core'}, dimensions={0} | all-to-all | bytes 2097152 | tf_op jit(solution)/shard_map/all_to_all | solution.py:179
  194.6 1.0 copy.53
  (41 shorter events, 0.7 us)
Async XLA Ops:
  0.6 18.3 %all-to-all-start = ((bf16[8,96,256]{2,1,0:T(8,128)(2,1)}), bf16[8,96,256]{2,1,0:T(8,128)(2,1)S(1)}, u32[]{:S(2)}, u32[]{:S(2)}) async-start(bf16[8,96,256]{2,1,0:T(8,128)(2,1)} %bitcast.46), calls=%async_computation | async-start | bytes 786432 | tf_op jit(solution)/shard_map/all_to_all | solution.py:179
  19.0 25.2 %all-to-all-start.1 = ((bf16[8,3,96,256]{3,2,1,0:T(8,128)(2,1)}), bf16[8,3,96,256]{3,2,1,0:T(8,128)(2,1)}, u32[]{:S(2)}, u32[]{:S(2)}) async-start(bf16[8,3,96,256]{3,2,1,0:T(8,128)(2,1)} %pad_maximum_fusion), calls=%async_computation.1 | async-start | bytes 2359296 | tf_op jit(solution)/shard_map/all_to_all | solution.py:179
  24.0 13.7 %collective-permute-start.1 = (bf16[768,256]{1,0:T(8,128)(2,1)S(1)}, bf16[768,256]{1,0:T(8,128)(2,1)S(1)}, u32[]{:S(2)}, u32[]{:S(2)}) collective-permute-start(bf16[768,256]{1,0:T(8,128)(2,1)S(1)} %bitcast.33), channel_id=1, source_target_pairs={{0,4},{4,8},{8,12},{12,16},{16,20},{20,24},{24,28},{28,0},{1,5},{5... | collective-permute-start | bytes 1179656 | tf_op jit(solution)/shard_map/ppermute | solution.py:189
  25.9 13.7 %collective-permute-start.2 = (bf16[768,256]{1,0:T(8,128)(2,1)S(1)}, bf16[768,256]{1,0:T(8,128)(2,1)S(1)}, u32[]{:S(2)}, u32[]{:S(2)}) collective-permute-start(bf16[768,256]{1,0:T(8,128)(2,1)S(1)} %bitcast.34), channel_id=1, source_target_pairs={{0,28},{4,0},{8,4},{12,8},{16,12},{20,16},{24,20},{28,24},{1,29},{... | collective-permute-start | bytes 1179656 | tf_op jit(solution)/shard_map/ppermute | solution.py:189
  37.6 16.8 %copy-start.6 = (bf16[768,256]{1,0:T(8,128)(2,1)}, bf16[768,256]{1,0:T(8,128)(2,1)S(1)}, u32[]{:S(2)}) copy-start(bf16[768,256]{1,0:T(8,128)(2,1)S(1)} %collective-permute-done.1.refs_1_) | copy-start | bytes 1179652
  37.6 14.9 %collective-permute-start.3 = (bf16[768,256]{1,0:T(8,128)(2,1)S(1)}, bf16[768,256]{1,0:T(8,128)(2,1)}, u32[]{:S(2)}, u32[]{:S(2)}) collective-permute-start(bf16[768,256]{1,0:T(8,128)(2,1)S(1)} %collective-permute-done.1.refs_1_), channel_id=1, source_target_pairs={{0,4},{4,8},{8,12},{12,16},{16,20},{20,24},{24,28},{28,0},{1,5},{5... | collective-permute-start | bytes 1179656 | tf_op jit(solution)/shard_map/ppermute | solution.py:189
  39.6 20.5 %copy-start.8 = (bf16[768,256]{1,0:T(8,128)(2,1)}, bf16[768,256]{1,0:T(8,128)(2,1)S(1)}, u32[]{:S(2)}) copy-start(bf16[768,256]{1,0:T(8,128)(2,1)S(1)} %collective-permute-done.2.refs_2_) | copy-start | bytes 1179652
  39.6 14.9 %collective-permute-start.4 = (bf16[768,256]{1,0:T(8,128)(2,1)S(1)}, bf16[768,256]{1,0:T(8,128)(2,1)}, u32[]{:S(2)}, u32[]{:S(2)}) collective-permute-start(bf16[768,256]{1,0:T(8,128)(2,1)S(1)} %collective-permute-done.2.refs_2_), channel_id=1, source_target_pairs={{0,28},{4,0},{8,4},{12,8},{16,12},{20,16},{24,20},{28,24},{1,29},{... | collective-permute-start | bytes 1179656 | tf_op jit(solution)/shard_map/ppermute | solution.py:189
  45.4 44.3 %copy-start = (bf16[8,2,96,256]{3,2,1,0:T(8,128)(2,1)}, bf16[8,2,96,256]{3,2,1,0:T(8,128)(2,1)S(1)}, u32[]{:S(2)}) copy-start(bf16[8,2,96,256]{3,2,1,0:T(8,128)(2,1)S(1)} %slice.29.kv_ref) | copy-start | bytes 2359300
  45.4 27.5 %collective-permute-start = (bf16[8,2,96,256]{3,2,1,0:T(8,128)(2,1)S(1)}, bf16[8,2,96,256]{3,2,1,0:T(8,128)(2,1)S(1)}, u32[]{:S(2)}, u32[]{:S(2)}) collective-permute-start(bf16[8,2,96,256]{3,2,1,0:T(8,128)(2,1)S(1)} %slice.29.kv_ref), channel_id=1, source_target_pairs={{0,256},{1,257},{2,258},{3,259},{4,260},{5,261},{6,262},{7,263},{8... | collective-permute-start | bytes 2359304 | tf_op jit(solution)/shard_map/ppermute | solution.py:222
  52.5 12.5 %collective-permute-start.5 = (bf16[768,256]{1,0:T(8,128)(2,1)}, bf16[768,256]{1,0:T(8,128)(2,1)S(1)}, u32[]{:S(2)}, u32[]{:S(2)}) collective-permute-start(bf16[768,256]{1,0:T(8,128)(2,1)} %collective-permute-done.3.refs_3_), channel_id=1, source_target_pairs={{0,4},{4,8},{8,12},{12,16},{16,20},{20,24},{24,28},{28,0},{1,5},{5... | collective-permute-start | bytes 1179656 | tf_op jit(solution)/shard_map/ppermute | solution.py:189
  54.5 13.1 %collective-permute-start.6 = (bf16[768,256]{1,0:T(8,128)(2,1)}, bf16[768,256]{1,0:T(8,128)(2,1)S(1)}, u32[]{:S(2)}, u32[]{:S(2)}) collective-permute-start(bf16[768,256]{1,0:T(8,128)(2,1)} %collective-permute-done.4.refs_4_), channel_id=1, source_target_pairs={{0,28},{4,0},{8,4},{12,8},{16,12},{20,16},{24,20},{28,24},{1,29},{... | collective-permute-start | bytes 1179656 | tf_op jit(solution)/shard_map/ppermute | solution.py:189
  60.1 29.6 %copy-start.1 = (bf16[8,96,256]{2,1,0:T(8,128)(2,1)}, bf16[8,96,256]{2,1,0:T(8,128)(2,1)S(1)}, u32[]{:S(2)}) copy-start(bf16[8,96,256]{2,1,0:T(8,128)(2,1)S(1)} %slice_bitcast_fusion.q_ref) | copy-start | bytes 1179652
  60.1 24.7 %collective-permute-start.9 = (bf16[8,96,256]{2,1,0:T(8,128)(2,1)S(1)}, bf16[8,96,256]{2,1,0:T(8,128)(2,1)}, u32[]{:S(2)}, u32[]{:S(2)}) collective-permute-start(bf16[8,96,256]{2,1,0:T(8,128)(2,1)S(1)} %slice_bitcast_fusion.q_ref), channel_id=1, source_target_pairs={{256,0},{257,1},{258,2},{259,3},{260,4},{261,5},{262,6},{263,7},{2... | collective-permute-start | bytes 1179656 | tf_op jit(solution)/shard_map/ppermute | solution.py:225
  65.7 11.9 %collective-permute-start.7 = (bf16[384,256]{1,0:T(8,128)(2,1)}, bf16[384,256]{1,0:T(8,128)(2,1)S(1)}, u32[]{:S(2)}, u32[]{:S(2)}) collective-permute-start(bf16[384,256]{1,0:T(8,128)(2,1)} %slice.30), channel_id=1, source_target_pairs={{0,4},{4,8},{8,12},{12,16},{16,20},{20,24},{24,28},{28,0},{1,5},{5... | collective-permute-start | bytes 589832 | tf_op jit(solution)/shard_map/ppermute | solution.py:189
  68.3 10.0 %collective-permute-start.8 = (bf16[384,256]{1,0:T(8,128)(2,1)}, bf16[384,256]{1,0:T(8,128)(2,1)S(1)}, u32[]{:S(2)}, u32[]{:S(2)}) collective-permute-start(bf16[384,256]{1,0:T(8,128)(2,1)} %slice.31), channel_id=1, source_target_pairs={{0,28},{4,0},{8,4},{12,8},{16,12},{20,16},{24,20},{28,24},{1,29},{... | collective-permute-start | bytes 589832 | tf_op jit(solution)/shard_map/ppermute | solution.py:189
  72.9 6.0 %copy-start.5 = (bf16[256,2048]{1,0:T(8,128)(2,1)S(1)}, bf16[256,2048]{1,0:T(8,128)(2,1)}, u32[]{:S(2)}) copy-start(bf16[256,2048]{1,0:T(8,128)(2,1)} %w_ref.1) | copy-start | bytes 3145732
  72.9 6.0 %copy-start.7 = (bf16[768,256]{1,0:T(8,128)(2,1)S(1)}, bf16[768,256]{1,0:T(8,128)(2,1)}, u32[]{:S(2)}) copy-start(bf16[768,256]{1,0:T(8,128)(2,1)} %copy-done.6) | copy-start | bytes 1179652
  72.9 6.0 %copy-start.9 = (bf16[768,256]{1,0:T(8,128)(2,1)S(1)}, bf16[768,256]{1,0:T(8,128)(2,1)}, u32[]{:S(2)}) copy-start(bf16[768,256]{1,0:T(8,128)(2,1)} %copy-done.8) | copy-start | bytes 1179652
  77.6 0.7 copy-start.10
  78.2 0.7 copy-start.12
  78.9 0.9 copy-start.11
  79.8 0.9 copy-start.13
  84.7 10.2 %copy-start.2 = (bf16[768,256]{1,0:T(8,128)(2,1)}, bf16[768,256]{1,0:T(8,128)(2,1)S(1)}, u32[]{:S(2)}) copy-start(bf16[768,256]{1,0:T(8,128)(2,1)S(1)} %get-tuple-element.28) | copy-start | bytes 1179652
  84.7 13.4 %all-to-all-start.2 = ((bf16[4,64,2048]{2,1,0:T(8,128)(2,1)}), bf16[4,64,2048]{2,1,0:T(8,128)(2,1)S(1)}, u32[]{:S(2)}, u32[]{:S(2)}) async-start(bf16[4,64,2048]{2,1,0:T(8,128)(2,1)} %bitcast.9), calls=%async_computation.2 | async-start | bytes 2097152 | tf_op jit(solution)/shard_map/all_to_all | solution.py:179
  88.4 24.8 %collective-permute-start.10 = (bf16[8,96,256]{2,1,0:T(8,128)(2,1)S(1)}, bf16[8,96,256]{2,1,0:T(8,128)(2,1)}, u32[]{:S(2)}, u32[]{:S(2)}) collective-permute-start(bf16[8,96,256]{2,1,0:T(8,128)(2,1)S(1)} %bitcast.29), channel_id=1, source_target_pairs={{256,0},{257,1},{258,2},{259,3},{260,4},{261,5},{262,6},{263,7},{2... | collective-permute-start | bytes 1179656 | tf_op jit(solution)/shard_map/ppermute | solution.py:230
  95.0 0.7 copy-start.3
  95.7 34.6 %copy-start.4 = (f32[6,8,128]{2,1,0:T(8,128)}, f32[6,8,128]{2,1,0:T(8,128)S(1)}, u32[]{:S(2)}) copy-start(f32[6,8,128]{2,1,0:T(8,128)S(1)} %get-tuple-element.32.stats_ref) | copy-start | bytes 73732
  114.0 24.2 %all-to-all-start.4 = ((bf16[8,4,2048]{2,1,0:T(4,128)(2,1)}), bf16[8,4,2048]{2,1,0:T(4,128)(2,1)S(1)}, u32[]{:S(2)}, u32[]{:S(2)}) async-start(bf16[8,4,2048]{2,1,0:T(4,128)(2,1)} %reshape.52), calls=%async_computation.4 | async-start | bytes 262144 | tf_op jit(solution)/shard_map/all_to_all | solution.py:179
  130.3 9.8 %collective-permute-start.11 = (f32[6,8,128]{2,1,0:T(8,128)S(1)}, f32[6,8,128]{2,1,0:T(8,128)S(1)}, u32[]{:S(2)}, u32[]{:S(2)}) collective-permute-start(f32[6,8,128]{2,1,0:T(8,128)S(1)} %get-tuple-element.32.stats_ref), channel_id=1, source_target_pairs={{256,0},{257,1},{258,2},{259,3},{260,4},{261,5},{262,6},{263,7},{2... | collective-permute-start | bytes 73736 | tf_op jit(solution)/shard_map/ppermute | solution.py:238
  140.1 4.1 %copy-start.14 = (f32[6,8,128]{2,1,0:T(8,128)}, f32[6,8,128]{2,1,0:T(8,128)S(1)}, u32[]{:S(2)}) copy-start(f32[6,8,128]{2,1,0:T(8,128)S(1)} %collective-permute-done.11.stats_recv_ref) | copy-start | bytes 73732
  140.8 11.3 %all-to-all-start.5 = ((bf16[8,4,2048]{2,1,0:T(4,128)(2,1)}), bf16[8,4,2048]{2,1,0:T(4,128)(2,1)S(1)}, u32[]{:S(2)}, u32[]{:S(2)}) async-start(bf16[8,4,2048]{2,1,0:T(4,128)(2,1)} %broadcast_in_dim.8), calls=%async_computation.5 | async-start | bytes 262144 | tf_op jit(solution)/shard_map/all_to_all | solution.py:179
  176.4 12.1 %all-to-all-start.7 = ((bf16[4,32,2048]{2,1,0:T(8,128)(2,1)}), bf16[4,32,2048]{2,1,0:T(8,128)(2,1)S(1)}, u32[]{:S(2)}, u32[]{:S(2)}) async-start(bf16[4,32,2048]{2,1,0:T(8,128)(2,1)} %broadcast_in_dim.9), calls=%async_computation.7 | async-start | bytes 1048576 | tf_op jit(solution)/shard_map/all_to_all | solution.py:179

commit v3 on v2

--- a/solution.py
+++ b/solution.py
@@ -116,27 +116,27 @@
 
 
 def project_kernel(offsets, place_ref, w_ref, att_ref, *refs):
-    blocks, (g_ref, term_ref) = refs[:-2], refs[-2:]
+    blocks, (acc_ref, term_ref) = refs[:-2], refs[-2:]
     width = w_ref.shape[0]
     parts = w_ref.shape[1] // width
-    half = att_ref.shape[0] // 2
-
-    def columns(offset):
+    acc = 0.0
+    for offset, ref in zip(offsets, blocks):
         owner = lax.rem(place_ref[0] + offset + parts, parts)
-        return pl.ds(pl.multiple_of(owner * width, width), width)
-
-    acc = 0.0
-    for offset, ref in zip(offsets, blocks[:-2]):
-        acc = acc + dot_nt(ref[...], w_ref[:, columns(offset)])
-        term_ref[:, columns(offset)] = dot_tn(att_ref[...], ref[...]).astype(BF16)
-    last = columns(parts // 2)
-    low, high = blocks[-2][...], blocks[-1][...]
-    g_ref[:half] = (acc[:half] + dot_nt(low, w_ref[:, last])).astype(BF16)
-    g_ref[half:] = (acc[half:] + dot_nt(high, w_ref[:, last])).astype(BF16)
-    term_ref[:, last] = (dot_tn(att_ref[:half], low) + dot_tn(att_ref[half:], high)).astype(BF16)
-
-
-def per_group(kernel, name, flops, side, args, outs, vmem=32):
+        cols = pl.ds(pl.multiple_of(owner * width, width), width)
+        acc = acc + dot_nt(ref[...], w_ref[:, cols])
+        term_ref[:, cols] = dot_tn(att_ref[...], ref[...]).astype(BF16)
+    acc_ref[...] = acc
+
+
+def finish_kernel(place_ref, w_ref, att_ref, acc_ref, low_ref, high_ref, _, g_ref, term_ref):
+    half = low_ref.shape[0]
+    low, high = low_ref[...], high_ref[...]
+    g_ref[:half] = (acc_ref[:half] + dot_nt(low, w_ref[...])).astype(BF16)
+    g_ref[half:] = (acc_ref[half:] + dot_nt(high, w_ref[...])).astype(BF16)
+    term_ref[...] = (dot_tn(att_ref[:half], low) + dot_tn(att_ref[half:], high)).astype(BF16)
+
+
+def per_group(kernel, name, flops, side, args, outs, vmem=32, out_specs=None):
     items = args[0].shape[-2]
 
     def spec(a):
@@ -150,7 +150,7 @@
         kernel,
         grid=(items // GROUP,),
         in_specs=[SMEM] + [spec(a) for a in args],
-        out_specs=[spec(a) for a in outs],
+        out_specs=out_specs or [spec(a) for a in outs],
         out_shape=[jax.ShapeDtypeStruct(a.shape, a.dtype) for a in outs],
         compiler_params=pltpu.CompilerParams(vmem_limit_bytes=vmem * 1024 * 1024),
         cost_estimate=pl.CostEstimate(flops=flops, bytes_accessed=4_000_000, transcendentals=400_000),
@@ -160,19 +160,39 @@
 
 def project(blocks, offsets, w, att):
     tokens, width = att.shape
+    parts = w.shape[1] // width
+    place = lax.axis_index("tensor")
     vmem = pl.BlockSpec(memory_space=pltpu.VMEM)
+    acc, term = pl.pallas_call(
+        functools.partial(project_kernel, offsets),
+        in_specs=[SMEM] + [vmem] * len(blocks),
+        out_specs=[vmem, vmem],
+        out_shape=[jax.ShapeDtypeStruct((tokens, width), F32), jax.ShapeDtypeStruct(w.shape, BF16)],
+        compiler_params=PARAMS,
+        cost_estimate=pl.CostEstimate(flops=1_400_000_000, bytes_accessed=6_000_000, transcendentals=0),
+        name="projections",
+    )(place.reshape(1), w, att, *blocks[:-2])
+    strip = pl.BlockSpec((width, width), lambda i, owner: (0, owner[0]))
+
+    def whole(a):
+        return pl.BlockSpec(a.shape, lambda i, owner: (0, 0))
+
+    owner = lax.rem(place + parts // 2, parts).reshape(1)
+    args = [w, att, acc, *blocks[-2:], term]
     return pl.pallas_call(
-        functools.partial(project_kernel, offsets),
-        in_specs=[pl.BlockSpec(memory_space=pltpu.SMEM)] + [vmem] * (2 + len(blocks)),
-        out_specs=[vmem, vmem],
-        out_shape=[
-            jax.ShapeDtypeStruct((tokens, width), BF16),
-            jax.ShapeDtypeStruct(w.shape, BF16),
-        ],
-        compiler_params=pltpu.CompilerParams(vmem_limit_bytes=24 * 1024 * 1024),
-        cost_estimate=pl.CostEstimate(flops=1_600_000_000, bytes_accessed=6_000_000, transcendentals=0),
-        name="projections",
-    )(lax.axis_index("tensor").reshape(1), w, att, *blocks)
+        finish_kernel,
+        grid_spec=pltpu.PrefetchScalarGridSpec(
+            num_scalar_prefetch=1,
+            grid=(1,),
+            in_specs=[strip] + [whole(a) for a in args[1:-1]] + [pl.BlockSpec(memory_space=pl.ANY)],
+            out_specs=[whole(att), strip],
+        ),
+        out_shape=[jax.ShapeDtypeStruct(att.shape, BF16), jax.ShapeDtypeStruct(term.shape, BF16)],
+        input_output_aliases={len(args): 1},
+        compiler_params=PARAMS,
+        cost_estimate=pl.CostEstimate(flops=200_000_000, bytes_accessed=3_000_000, transcendentals=0),
+        name="last_projections",
+    )(owner, *args)
 
 
 def exchange(x, axes):
@@ -239,16 +259,17 @@
     total = (scatter_sum(total, ("zh", "dp")) * factor).astype(BF16)
     total, stats_recv = lax.optimization_barrier((total, stats_recv))
     args = [q, kv, q_recv, g, g_recv, stats, stats_recv, grad_q]
-    grads = jax.ShapeDtypeStruct((near, 3, items, width), BF16)
-    (grads,) = per_group(key_kernel, "grad_keys_values", 1_000_000_000, side, args, [grads], 60)
+    groups, share = items // GROUP, out_proj.size // (near * GROUP * width)
+    grads = jax.ShapeDtypeStruct((near, 3 * groups + share, GROUP, width), BF16)
+    block = pl.BlockSpec((near, 3, GROUP, width), lambda i: (0, i, 0, 0))
+    (grads,) = per_group(key_kernel, "grad_keys_values", 1_000_000_000, side, args, [grads], 60, [block])
     total = gather(total, ("zh", "dp"))
     total, grads = lax.optimization_barrier((total, grads))
-    home = exchange(grads, NEAR)
-    total, home = lax.optimization_barrier((total, home))
-    total = gather(total, "x")
-    grad_proj = gather(total, "core").reshape(lax.axis_size("core"), lax.axis_size("x"), -1, total.shape[-1])
-    grad_proj = jnp.swapaxes(grad_proj, 0, 1).reshape(out_proj.shape)
-    return tuple(home[:, j].reshape(clips, 1, patches, width) for j in range(3)) + (grad_proj,)
+    copies = jnp.broadcast_to(total.reshape(1, share, GROUP, width), (near, share, GROUP, width))
+    home = exchange(lax.dynamic_update_slice(grads, copies, (0, 3 * groups, 0, 0)), NEAR)
+    grad_proj = home[:, 3 * groups :].reshape(out_proj.shape)
+    grads = home[:, : 3 * groups].reshape(near, groups, 3, GROUP, width)
+    return tuple(grads[:, :, j].reshape(clips, 1, patches, width) for j in range(3)) + (grad_proj,)
 
 
 def solution(mesh):

time: 197 us -> 189 us (0.959)
  blocking collectives: 44.3 us -> 52.1 us
  waiting for transfers between devices: 36.1 us -> 28.5 us
  starting transfers between devices: 79 us -> 73.1 us
  local copies, waits for them, and re-layouts: 12.1 us -> 9.46 us
    all_to_all x3 -> x2, blocking collectives: 44.3 us -> 52.1 us  [exchange(): return lax.all_to_all(x, axes, 0, 0, tiled=True)]
    all_to_all x6 -> x5, waiting for transfers between devices: 23.6 us -> 16 us  [exchange(): return lax.all_to_all(x, axes, 0, 0, tiled=True)]
    all_to_all x6 -> x5, starting transfers between devices: 42.1 us -> 36.3 us  [exchange(): return lax.all_to_all(x, axes, 0, 0, tiled=True)]
    unnamed x30 -> x22, local copies, waits for them, and re-layouts: 3.98 us -> 0.79 us
    pallas_call x1 -> x2, Pallas kernels: 3.97 us -> 4.81 us  [the longest x1 3.72 us: project(): pl.pallas_call(functools.partial(project_kernel, offsets), in_specs=[SMEM...]
  transfers between devices with their start and end apart: 18 -> 17, of which waited for: 8 -> 7; matrix products, arithmetic and copies ran while one was open for 4% -> 3% of each run, Pallas kernels for 10% -> 11%
where the time goes in v3:
time: 189 us; the launch traced here: 188 us
  starting transfers between devices  73.1 us (39%)
  blocking collectives  52.1 us (28%)
  waiting for transfers between devices  28.5 us (15%)
  Pallas kernels  21.3 us (11%)
  local copies, waits for them, and re-layouts  9.46 us (5%)
  other arithmetic  2.82 us (1%)
    all_to_all x2, blocking collectives, exchange(): return lax.all_to_all(x, axes, 0, 0, tiled=True)  52.1 us
    all_to_all x5, starting transfers between devices, exchange(): return lax.all_to_all(x, axes, 0, 0, tiled=True)  36.3 us
    ppermute x8, starting transfers between devices, shift(): return lax.ppermute(x, axis, [(i, (i + by) % size) for i in range(size)])  25.9 us
    pallas_call x3, Pallas kernels, per_group(): pl.pallas_call(kernel, grid=(items // GROUP,), in_specs=[SMEM] + [spec(a)...  16.5 us
    all_to_all x5, waiting for transfers between devices, exchange(): return lax.all_to_all(x, axes, 0, 0, tiled=True)  16 us
    ppermute x8, waiting for transfers between devices, shift(): return lax.ppermute(x, axis, [(i, (i + by) % size) for i in range(size)])  10.8 us
    ppermute x1, starting transfers between devices, local(): kv_recv = lax.ppermute(kv, 'zh', [(0, 1)])  7.1 us
  transfers between devices with their start and end apart: 17, of which 7 were waited for; matrix products, arithmetic and copies ran while one was open for 3% of the time, Pallas kernels for 11%

profile of v3, /device:TPU:1, one launch (start us, length us, event | category | flops | bytes accessed | tf_op | source)
XLA Modules:
  0.0 188.3 jit_solution(13326864464960439985)
XLA Ops:
  0.6 10.2 %all-to-all-start = ((bf16[8,96,256]{2,1,0:T(8,128)(2,1)}), bf16[8,96,256]{2,1,0:T(8,128)(2,1)S(1)}, u32[]{:S(2)}, u32[]{:S(2)}) async-start(bf16[8,96,256]{2,1,0:T(8,128)(2,1)} %bitcast.38), calls=%async_computation | async-start | bytes 786432 | tf_op jit(solution)/shard_map/all_to_all | solution.py:199
  10.9 2.4 %pad_maximum_fusion = bf16[8,3,96,256]{3,2,1,0:T(8,128)(2,1)} fusion(bf16[8,1,96,256]{3,2,1,0:T(8,128)(2,1)} %bitcast.32, bf16[8,1,96,256]{3,2,1,0:T(8,128)(2,1)} %bitcast.33, bf16[8,1,96,256]{3,2,1,0:T(8,128)(2,1)} %bitcast.34), kind=kLoop, calls=%fused_computation | loop fusion | flops 1179648 | bytes 2359296 | tf_op jit(solution)/shard_map/stack | solution.py:239
  13.3 5.7 %all-to-all-done = bf16[8,96,256]{2,1,0:T(8,128)(2,1)S(1)} async-done(((bf16[8,96,256]{2,1,0:T(8,128)(2,1)}), bf16[8,96,256]{2,1,0:T(8,128)(2,1)S(1)}, u32[]{:S(2)}, u32[]{:S(2)}) %all-to-all-start) | async-done | bytes 393248 | tf_op jit(solution)/shard_map/all_to_all | solution.py:199
  19.0 5.0 %all-to-all-start.1 = ((bf16[8,3,96,256]{3,2,1,0:T(8,128)(2,1)}), bf16[8,3,96,256]{3,2,1,0:T(8,128)(2,1)}, u32[]{:S(2)}, u32[]{:S(2)}) async-start(bf16[8,3,96,256]{3,2,1,0:T(8,128)(2,1)} %pad_maximum_fusion), calls=%async_computation.1 | async-start | bytes 2359296 | tf_op jit(solution)/shard_map/all_to_all | solution.py:199
  24.0 1.9 %collective-permute-start.1 = (bf16[768,256]{1,0:T(8,128)(2,1)S(1)}, bf16[768,256]{1,0:T(8,128)(2,1)S(1)}, u32[]{:S(2)}, u32[]{:S(2)}) collective-permute-start(bf16[768,256]{1,0:T(8,128)(2,1)S(1)} %bitcast.24), channel_id=1, source_target_pairs={{0,4},{4,8},{8,12},{12,16},{16,20},{20,24},{24,28},{28,0},{1,5},{5... | collective-permute-start | bytes 1179656 | tf_op jit(solution)/shard_map/ppermute | solution.py:209
  25.9 4.6 %collective-permute-start.2 = (bf16[768,256]{1,0:T(8,128)(2,1)S(1)}, bf16[768,256]{1,0:T(8,128)(2,1)S(1)}, u32[]{:S(2)}, u32[]{:S(2)}) collective-permute-start(bf16[768,256]{1,0:T(8,128)(2,1)S(1)} %bitcast.25), channel_id=1, source_target_pairs={{0,28},{4,0},{8,4},{12,8},{16,12},{20,16},{24,20},{28,24},{1,29},{... | collective-permute-start | bytes 1179656 | tf_op jit(solution)/shard_map/ppermute | solution.py:209
  30.5 7.2 %collective-permute-done.1.refs_1_ = bf16[768,256]{1,0:T(8,128)(2,1)S(1)} collective-permute-done((bf16[768,256]{1,0:T(8,128)(2,1)S(1)}, bf16[768,256]{1,0:T(8,128)(2,1)S(1)}, u32[]{:S(2)}, u32[]{:S(2)}) %collective-permute-start.1) | collective-permute-done | bytes 393248 | tf_op jit(solution)/shard_map/ppermute | solution.py:209
  37.6 1.9 %collective-permute-start.3 = (bf16[768,256]{1,0:T(8,128)(2,1)S(1)}, bf16[768,256]{1,0:T(8,128)(2,1)}, u32[]{:S(2)}, u32[]{:S(2)}) collective-permute-start(bf16[768,256]{1,0:T(8,128)(2,1)S(1)} %collective-permute-done.1.refs_1_), channel_id=1, source_target_pairs={{0,4},{4,8},{8,12},{12,16},{16,20},{20,24},{24,28},{28,0},{1,5},{5... | collective-permute-start | bytes 1179656 | tf_op jit(solution)/shard_map/ppermute | solution.py:209
  39.6 0.0 copy-start.8
  39.6 4.6 %collective-permute-start.4 = (bf16[768,256]{1,0:T(8,128)(2,1)S(1)}, bf16[768,256]{1,0:T(8,128)(2,1)}, u32[]{:S(2)}, u32[]{:S(2)}) collective-permute-start(bf16[768,256]{1,0:T(8,128)(2,1)S(1)} %collective-permute-done.2.refs_2_), channel_id=1, source_target_pairs={{0,28},{4,0},{8,4},{12,8},{16,12},{20,16},{24,20},{28,24},{1,29},{... | collective-permute-start | bytes 1179656 | tf_op jit(solution)/shard_map/ppermute | solution.py:209
  44.2 1.2 slice.37.kv_ref
  45.4 7.1 %collective-permute-start = (bf16[8,2,96,256]{3,2,1,0:T(8,128)(2,1)S(1)}, bf16[8,2,96,256]{3,2,1,0:T(8,128)(2,1)S(1)}, u32[]{:S(2)}, u32[]{:S(2)}) collective-permute-start(bf16[8,2,96,256]{3,2,1,0:T(8,128)(2,1)S(1)} %slice.37.kv_ref), channel_id=1, source_target_pairs={{0,256},{1,257},{2,258},{3,259},{4,260},{5,261},{6,262},{7,263},{8... | collective-permute-start | bytes 2359304 | tf_op jit(solution)/shard_map/ppermute | solution.py:242
  52.5 1.9 %collective-permute-start.5 = (bf16[768,256]{1,0:T(8,128)(2,1)}, bf16[768,256]{1,0:T(8,128)(2,1)S(1)}, u32[]{:S(2)}, u32[]{:S(2)}) collective-permute-start(bf16[768,256]{1,0:T(8,128)(2,1)} %collective-permute-done.3.refs_3_), channel_id=1, source_target_pairs={{0,4},{4,8},{8,12},{12,16},{16,20},{20,24},{24,28},{28,0},{1,5},{5... | collective-permute-start | bytes 1179656 | tf_op jit(solution)/shard_map/ppermute | solution.py:209
  54.5 4.6 %collective-permute-start.6 = (bf16[768,256]{1,0:T(8,128)(2,1)}, bf16[768,256]{1,0:T(8,128)(2,1)S(1)}, u32[]{:S(2)}, u32[]{:S(2)}) collective-permute-start(bf16[768,256]{1,0:T(8,128)(2,1)} %collective-permute-done.4.refs_4_), channel_id=1, source_target_pairs={{0,28},{4,0},{8,4},{12,8},{16,12},{20,16},{24,20},{28,24},{1,29},{... | collective-permute-start | bytes 1179656 | tf_op jit(solution)/shard_map/ppermute | solution.py:209
  59.0 1.0 slice_bitcast_fusion.q_ref
  60.1 1.3 collective-permute-start.9
  61.4 3.6 %collective-permute-done.5.refs_5_ = bf16[768,256]{1,0:T(8,128)(2,1)S(1)} collective-permute-done((bf16[768,256]{1,0:T(8,128)(2,1)}, bf16[768,256]{1,0:T(8,128)(2,1)S(1)}, u32[]{:S(2)}, u32[]{:S(2)}) %collective-permute-start.5) | collective-permute-done | bytes 393248 | tf_op jit(solution)/shard_map/ppermute | solution.py:209
  65.0 0.7 slice.38
  65.7 1.9 %collective-permute-start.7 = (bf16[384,256]{1,0:T(8,128)(2,1)}, bf16[384,256]{1,0:T(8,128)(2,1)S(1)}, u32[]{:S(2)}, u32[]{:S(2)}) collective-permute-start(bf16[384,256]{1,0:T(8,128)(2,1)} %slice.38), channel_id=1, source_target_pairs={{0,4},{4,8},{8,12},{12,16},{16,20},{20,24},{24,28},{28,0},{1,5},{5... | collective-permute-start | bytes 589832 | tf_op jit(solution)/shard_map/ppermute | solution.py:209
  67.6 0.7 slice.39
  68.3 4.6 %collective-permute-start.8 = (bf16[384,256]{1,0:T(8,128)(2,1)}, bf16[384,256]{1,0:T(8,128)(2,1)S(1)}, u32[]{:S(2)}, u32[]{:S(2)}) collective-permute-start(bf16[384,256]{1,0:T(8,128)(2,1)} %slice.39), channel_id=1, source_target_pairs={{0,28},{4,0},{8,4},{12,8},{16,12},{20,16},{24,20},{28,24},{1,29},{... | collective-permute-start | bytes 589832 | tf_op jit(solution)/shard_map/ppermute | solution.py:209
  72.9 4.6 %attend.1 = bf16[8,96,256]{2,1,0:T(8,128)(2,1)S(1)} custom-call(s32[1]{0:T(128)} %bitcast.1.side_ref, bf16[8,96,256]{2,1,0:T(8,128)(2,1)S(1)} %slice_bitcast_fusion.q_ref, bf16[8,2,96,256]{3,2,1,0:T(8,128)(2,1)S(1)} %slice.37.kv_ref, bf16[8,2,96,256]{3,2,1,0:T(8,128)(2,1)S(1)} %collective-permute-done.recv_ref), custom_call_target="tpu_custom_call" | custom-call | flops 400000000 | bytes 4000000 | tf_op jit(solution)/shard_map/attend/pallas_call | solution.py:149
  77.6 3.7 %projections.1 = (f32[768,256]{1,0:T(8,128)S(1)}, bf16[256,2048]{1,0:T(8,128)(2,1)}) custom-call(s32[1]{0:T(128)} %bitcast.9.place_ref, bf16[256,2048]{1,0:T(8,128)(2,1)S(1)} %copy-done.2, bf16[768,256]{1,0:T(8,128)(2,1)S(1)} %bitcast.22, bf16[768,256]{1,0:T(8,128)(2,1)S(1)} %bitcast.26, bf16[768,256]{1,0:T(8,128)(2,1)S(1)} %copy-done.7, ...), custom_call_target="tpu_custom_call" | custom-call | flops 1400000000 | bytes 6000000 | tf_op jit(solution)/shard_map/projections/pallas_call | solution.py:166
  81.3 1.1 last_projections.1
  82.4 3.7 %all-to-all-start.2 = ((bf16[4,64,2048]{2,1,0:T(8,128)(2,1)}), bf16[4,64,2048]{2,1,0:T(8,128)(2,1)S(1)}, u32[]{:S(2)}, u32[]{:S(2)}) async-start(bf16[4,64,2048]{2,1,0:T(8,128)(2,1)} %bitcast.10), calls=%async_computation.2 | async-start | bytes 2097152 | tf_op jit(solution)/shard_map/all_to_all | solution.py:199
  86.1 1.3 collective-permute-start.10
  87.4 5.2 %grad_queries.1 = (bf16[8,96,256]{2,1,0:T(8,128)(2,1)S(1)}, f32[6,8,128]{2,1,0:T(8,128)S(1)}) custom-call(s32[1]{0:T(128)} %bitcast.1.side_ref, bf16[8,96,256]{2,1,0:T(8,128)(2,1)S(1)} %slice_bitcast_fusion.q_ref, bf16[8,2,96,256]{3,2,1,0:T(8,128)(2,1)S(1)} %slice.37.kv_ref, bf16[8,2,96,256]{3,2,1,0:T(8,128)(2,1)S(1)} %collective-permute-done.recv_ref, ...), custom_call_target="tpu_custom_call" | custom-call | flops 700000000 | bytes 4000000 | tf_op jit(solution)/shard_map/grad_queries/pallas_call | solution.py:149
  92.6 0.7 copy-done.4
  93.4 2.4 %all-to-all-done.2 = bf16[4,64,2048]{2,1,0:T(8,128)(2,1)S(1)} async-done(((bf16[4,64,2048]{2,1,0:T(8,128)(2,1)}), bf16[4,64,2048]{2,1,0:T(8,128)(2,1)S(1)}, u32[]{:S(2)}, u32[]{:S(2)}) %all-to-all-start.2) | async-done | bytes 1048608 | tf_op jit(solution)/shard_map/all_to_all | solution.py:199
  95.8 0.2 reduce_sum.33
  96.0 17.2 %all_to_all.35 = bf16[2,32,2048]{2,1,0:T(8,128)(2,1)S(1)} all-to-all(bf16[2,32,2048]{2,1,0:T(8,128)(2,1)S(1)} %bitcast.31), channel_id=1, replica_groups=mesh['zh'=2,'x'=4,'core'=2,'tensor'=8,'dp'=4] {'core'}, dimensions={0} | all-to-all | bytes 524288 | tf_op jit(solution)/shard_map/all_to_all | solution.py:199
  113.3 0.7 reshape.59
  114.0 14.0 %all-to-all-start.4 = ((bf16[8,4,2048]{2,1,0:T(4,128)(2,1)}), bf16[8,4,2048]{2,1,0:T(4,128)(2,1)S(1)}, u32[]{:S(2)}, u32[]{:S(2)}) async-start(bf16[8,4,2048]{2,1,0:T(4,128)(2,1)} %reshape.59), calls=%async_computation.4 | async-start | bytes 262144 | tf_op jit(solution)/shard_map/all_to_all | solution.py:199
  128.0 1.3 collective-permute-start.11
  129.3 6.6 %all-to-all-done.4 = bf16[8,4,2048]{2,1,0:T(4,128)(2,1)S(1)} async-done(((bf16[8,4,2048]{2,1,0:T(4,128)(2,1)}), bf16[8,4,2048]{2,1,0:T(4,128)(2,1)S(1)}, u32[]{:S(2)}, u32[]{:S(2)}) %all-to-all-start.4) | async-done | bytes 131104 | tf_op jit(solution)/shard_map/all_to_all | solution.py:199
  135.9 0.2 convert_reduce_fusion
  136.0 1.7 collective-permute-done.11.stats_recv_ref
  137.7 0.7 broadcast_in_dim.6
  138.4 3.4 %all-to-all-start.5 = ((bf16[8,4,2048]{2,1,0:T(4,128)(2,1)}), bf16[8,4,2048]{2,1,0:T(4,128)(2,1)S(1)}, u32[]{:S(2)}, u32[]{:S(2)}) async-start(bf16[8,4,2048]{2,1,0:T(4,128)(2,1)} %broadcast_in_dim.6), calls=%async_computation.5 | async-start | bytes 262144 | tf_op jit(solution)/shard_map/all_to_all | solution.py:199
  141.8 6.7 %grad_keys_values.1 = bf16[8,34,16,256]{3,2,1,0:T(8,128)(2,1)} custom-call(s32[1]{0:T(128)} %bitcast.1.side_ref, bf16[8,96,256]{2,1,0:T(8,128)(2,1)} %copy-done.1, bf16[8,2,96,256]{3,2,1,0:T(8,128)(2,1)} %copy-done, bf16[8,96,256]{2,1,0:T(8,128)(2,1)} %collective-permute-done.9.q_recv_ref, bf16[8,96,256]{2,1,0:T(8,128)(2,1)} %bitcast.29, ...), custom_call_target="tpu_custom_call" | custom-call | flops 1000000000 | bytes 4000000 | tf_op jit(solution)/shard_map/grad_keys_values/pallas_call | solution.py:149
  148.5 1.3 all-to-all-done.5
  149.8 0.1 broadcast_in_dim.14
  149.8 1.1 broadcast_dynamic-update-slice_fusion
  150.9 34.9 %all_to_all.36 = bf16[8,34,16,256]{3,2,1,0:T(8,128)(2,1)S(1)} all-to-all(bf16[8,34,16,256]{3,2,1,0:T(8,128)(2,1)} %broadcast_dynamic-update-slice_fusion), channel_id=1, replica_groups=mesh['zh'=2,'x'=4,'core'=2,'tensor'=8,'dp'=4] {'x','core'}, dimensions={0} | all-to-all | bytes 4456448 | tf_op jit(solution)/shard_map/all_to_all | solution.py:199
  185.8 0.1 slice.40
  185.9 1.0 fusion
  186.9 0.1 slice.44
  187.0 1.3 reshape.62
  (33 shorter events, 0.2 us)
Async XLA Ops:
  0.6 18.3 %all-to-all-start = ((bf16[8,96,256]{2,1,0:T(8,128)(2,1)}), bf16[8,96,256]{2,1,0:T(8,128)(2,1)S(1)}, u32[]{:S(2)}, u32[]{:S(2)}) async-start(bf16[8,96,256]{2,1,0:T(8,128)(2,1)} %bitcast.38), calls=%async_computation | async-start | bytes 786432 | tf_op jit(solution)/shard_map/all_to_all | solution.py:199
  19.0 25.2 %all-to-all-start.1 = ((bf16[8,3,96,256]{3,2,1,0:T(8,128)(2,1)}), bf16[8,3,96,256]{3,2,1,0:T(8,128)(2,1)}, u32[]{:S(2)}, u32[]{:S(2)}) async-start(bf16[8,3,96,256]{3,2,1,0:T(8,128)(2,1)} %pad_maximum_fusion), calls=%async_computation.1 | async-start | bytes 2359296 | tf_op jit(solution)/shard_map/all_to_all | solution.py:199
  24.0 13.7 %collective-permute-start.1 = (bf16[768,256]{1,0:T(8,128)(2,1)S(1)}, bf16[768,256]{1,0:T(8,128)(2,1)S(1)}, u32[]{:S(2)}, u32[]{:S(2)}) collective-permute-start(bf16[768,256]{1,0:T(8,128)(2,1)S(1)} %bitcast.24), channel_id=1, source_target_pairs={{0,4},{4,8},{8,12},{12,16},{16,20},{20,24},{24,28},{28,0},{1,5},{5... | collective-permute-start | bytes 1179656 | tf_op jit(solution)/shard_map/ppermute | solution.py:209
  25.9 13.7 %collective-permute-start.2 = (bf16[768,256]{1,0:T(8,128)(2,1)S(1)}, bf16[768,256]{1,0:T(8,128)(2,1)S(1)}, u32[]{:S(2)}, u32[]{:S(2)}) collective-permute-start(bf16[768,256]{1,0:T(8,128)(2,1)S(1)} %bitcast.25), channel_id=1, source_target_pairs={{0,28},{4,0},{8,4},{12,8},{16,12},{20,16},{24,20},{28,24},{1,29},{... | collective-permute-start | bytes 1179656 | tf_op jit(solution)/shard_map/ppermute | solution.py:209
  37.6 16.8 %copy-start.6 = (bf16[768,256]{1,0:T(8,128)(2,1)}, bf16[768,256]{1,0:T(8,128)(2,1)S(1)}, u32[]{:S(2)}) copy-start(bf16[768,256]{1,0:T(8,128)(2,1)S(1)} %collective-permute-done.1.refs_1_) | copy-start | bytes 1179652
  37.6 14.9 %collective-permute-start.3 = (bf16[768,256]{1,0:T(8,128)(2,1)S(1)}, bf16[768,256]{1,0:T(8,128)(2,1)}, u32[]{:S(2)}, u32[]{:S(2)}) collective-permute-start(bf16[768,256]{1,0:T(8,128)(2,1)S(1)} %collective-permute-done.1.refs_1_), channel_id=1, source_target_pairs={{0,4},{4,8},{8,12},{12,16},{16,20},{20,24},{24,28},{28,0},{1,5},{5... | collective-permute-start | bytes 1179656 | tf_op jit(solution)/shard_map/ppermute | solution.py:209
  39.6 20.5 %copy-start.8 = (bf16[768,256]{1,0:T(8,128)(2,1)}, bf16[768,256]{1,0:T(8,128)(2,1)S(1)}, u32[]{:S(2)}) copy-start(bf16[768,256]{1,0:T(8,128)(2,1)S(1)} %collective-permute-done.2.refs_2_) | copy-start | bytes 1179652
  39.6 14.9 %collective-permute-start.4 = (bf16[768,256]{1,0:T(8,128)(2,1)S(1)}, bf16[768,256]{1,0:T(8,128)(2,1)}, u32[]{:S(2)}, u32[]{:S(2)}) collective-permute-start(bf16[768,256]{1,0:T(8,128)(2,1)S(1)} %collective-permute-done.2.refs_2_), channel_id=1, source_target_pairs={{0,28},{4,0},{8,4},{12,8},{16,12},{20,16},{24,20},{28,24},{1,29},{... | collective-permute-start | bytes 1179656 | tf_op jit(solution)/shard_map/ppermute | solution.py:209
  45.4 42.0 %copy-start = (bf16[8,2,96,256]{3,2,1,0:T(8,128)(2,1)}, bf16[8,2,96,256]{3,2,1,0:T(8,128)(2,1)S(1)}, u32[]{:S(2)}) copy-start(bf16[8,2,96,256]{3,2,1,0:T(8,128)(2,1)S(1)} %slice.37.kv_ref) | copy-start | bytes 2359300
  45.4 27.5 %collective-permute-start = (bf16[8,2,96,256]{3,2,1,0:T(8,128)(2,1)S(1)}, bf16[8,2,96,256]{3,2,1,0:T(8,128)(2,1)S(1)}, u32[]{:S(2)}, u32[]{:S(2)}) collective-permute-start(bf16[8,2,96,256]{3,2,1,0:T(8,128)(2,1)S(1)} %slice.37.kv_ref), channel_id=1, source_target_pairs={{0,256},{1,257},{2,258},{3,259},{4,260},{5,261},{6,262},{7,263},{8... | collective-permute-start | bytes 2359304 | tf_op jit(solution)/shard_map/ppermute | solution.py:242
  52.5 12.5 %collective-permute-start.5 = (bf16[768,256]{1,0:T(8,128)(2,1)}, bf16[768,256]{1,0:T(8,128)(2,1)S(1)}, u32[]{:S(2)}, u32[]{:S(2)}) collective-permute-start(bf16[768,256]{1,0:T(8,128)(2,1)} %collective-permute-done.3.refs_3_), channel_id=1, source_target_pairs={{0,4},{4,8},{8,12},{12,16},{16,20},{20,24},{24,28},{28,0},{1,5},{5... | collective-permute-start | bytes 1179656 | tf_op jit(solution)/shard_map/ppermute | solution.py:209
  54.5 13.1 %collective-permute-start.6 = (bf16[768,256]{1,0:T(8,128)(2,1)}, bf16[768,256]{1,0:T(8,128)(2,1)S(1)}, u32[]{:S(2)}, u32[]{:S(2)}) collective-permute-start(bf16[768,256]{1,0:T(8,128)(2,1)} %collective-permute-done.4.refs_4_), channel_id=1, source_target_pairs={{0,28},{4,0},{8,4},{12,8},{16,12},{20,16},{24,20},{28,24},{1,29},{... | collective-permute-start | bytes 1179656 | tf_op jit(solution)/shard_map/ppermute | solution.py:209
  60.1 27.3 %copy-start.1 = (bf16[8,96,256]{2,1,0:T(8,128)(2,1)}, bf16[8,96,256]{2,1,0:T(8,128)(2,1)S(1)}, u32[]{:S(2)}) copy-start(bf16[8,96,256]{2,1,0:T(8,128)(2,1)S(1)} %slice_bitcast_fusion.q_ref) | copy-start | bytes 1179652
  60.1 22.3 %collective-permute-start.9 = (bf16[8,96,256]{2,1,0:T(8,128)(2,1)S(1)}, bf16[8,96,256]{2,1,0:T(8,128)(2,1)}, u32[]{:S(2)}, u32[]{:S(2)}) collective-permute-start(bf16[8,96,256]{2,1,0:T(8,128)(2,1)S(1)} %slice_bitcast_fusion.q_ref), channel_id=1, source_target_pairs={{256,0},{257,1},{258,2},{259,3},{260,4},{261,5},{262,6},{263,7},{2... | collective-permute-start | bytes 1179656 | tf_op jit(solution)/shard_map/ppermute | solution.py:245
  65.7 15.6 %collective-permute-start.7 = (bf16[384,256]{1,0:T(8,128)(2,1)}, bf16[384,256]{1,0:T(8,128)(2,1)S(1)}, u32[]{:S(2)}, u32[]{:S(2)}) collective-permute-start(bf16[384,256]{1,0:T(8,128)(2,1)} %slice.38), channel_id=1, source_target_pairs={{0,4},{4,8},{8,12},{12,16},{16,20},{20,24},{24,28},{28,0},{1,5},{5... | collective-permute-start | bytes 589832 | tf_op jit(solution)/shard_map/ppermute | solution.py:209
  68.3 13.0 %collective-permute-start.8 = (bf16[384,256]{1,0:T(8,128)(2,1)}, bf16[384,256]{1,0:T(8,128)(2,1)S(1)}, u32[]{:S(2)}, u32[]{:S(2)}) collective-permute-start(bf16[384,256]{1,0:T(8,128)(2,1)} %slice.39), channel_id=1, source_target_pairs={{0,28},{4,0},{8,4},{12,8},{16,12},{20,16},{24,20},{28,24},{1,29},{... | collective-permute-start | bytes 589832 | tf_op jit(solution)/shard_map/ppermute | solution.py:209
  72.9 4.7 %copy-start.2 = (bf16[256,2048]{1,0:T(8,128)(2,1)S(1)}, bf16[256,2048]{1,0:T(8,128)(2,1)}, u32[]{:S(2)}) copy-start(bf16[256,2048]{1,0:T(8,128)(2,1)} %w_ref.3) | copy-start | bytes 3145732
  72.9 4.7 %copy-start.7 = (bf16[768,256]{1,0:T(8,128)(2,1)S(1)}, bf16[768,256]{1,0:T(8,128)(2,1)}, u32[]{:S(2)}) copy-start(bf16[768,256]{1,0:T(8,128)(2,1)} %copy-done.6) | copy-start | bytes 1179652
  72.9 4.7 %copy-start.9 = (bf16[768,256]{1,0:T(8,128)(2,1)S(1)}, bf16[768,256]{1,0:T(8,128)(2,1)}, u32[]{:S(2)}) copy-start(bf16[768,256]{1,0:T(8,128)(2,1)} %copy-done.8) | copy-start | bytes 1179652
  82.4 10.2 %copy-start.3 = (bf16[768,256]{1,0:T(8,128)(2,1)}, bf16[768,256]{1,0:T(8,128)(2,1)S(1)}, u32[]{:S(2)}) copy-start(bf16[768,256]{1,0:T(8,128)(2,1)S(1)} %get-tuple-element.30) | copy-start | bytes 1179652
  82.4 13.4 %all-to-all-start.2 = ((bf16[4,64,2048]{2,1,0:T(8,128)(2,1)}), bf16[4,64,2048]{2,1,0:T(8,128)(2,1)S(1)}, u32[]{:S(2)}, u32[]{:S(2)}) async-start(bf16[4,64,2048]{2,1,0:T(8,128)(2,1)} %bitcast.10), calls=%async_computation.2 | async-start | bytes 2097152 | tf_op jit(solution)/shard_map/all_to_all | solution.py:199
  86.1 27.2 %collective-permute-start.10 = (bf16[8,96,256]{2,1,0:T(8,128)(2,1)S(1)}, bf16[8,96,256]{2,1,0:T(8,128)(2,1)}, u32[]{:S(2)}, u32[]{:S(2)}) collective-permute-start(bf16[8,96,256]{2,1,0:T(8,128)(2,1)S(1)} %bitcast.27), channel_id=1, source_target_pairs={{256,0},{257,1},{258,2},{259,3},{260,4},{261,5},{262,6},{263,7},{2... | collective-permute-start | bytes 1179656 | tf_op jit(solution)/shard_map/ppermute | solution.py:250
  92.6 0.7 copy-start.4
  93.4 34.6 %copy-start.5 = (f32[6,8,128]{2,1,0:T(8,128)}, f32[6,8,128]{2,1,0:T(8,128)S(1)}, u32[]{:S(2)}) copy-start(f32[6,8,128]{2,1,0:T(8,128)S(1)} %get-tuple-element.34.stats_ref) | copy-start | bytes 73732
  114.0 21.9 %all-to-all-start.4 = ((bf16[8,4,2048]{2,1,0:T(4,128)(2,1)}), bf16[8,4,2048]{2,1,0:T(4,128)(2,1)S(1)}, u32[]{:S(2)}, u32[]{:S(2)}) async-start(bf16[8,4,2048]{2,1,0:T(4,128)(2,1)} %reshape.59), calls=%async_computation.4 | async-start | bytes 262144 | tf_op jit(solution)/shard_map/all_to_all | solution.py:199
  128.0 9.8 %collective-permute-start.11 = (f32[6,8,128]{2,1,0:T(8,128)S(1)}, f32[6,8,128]{2,1,0:T(8,128)S(1)}, u32[]{:S(2)}, u32[]{:S(2)}) collective-permute-start(f32[6,8,128]{2,1,0:T(8,128)S(1)} %get-tuple-element.34.stats_ref), channel_id=1, source_target_pairs={{256,0},{257,1},{258,2},{259,3},{260,4},{261,5},{262,6},{263,7},{2... | collective-permute-start | bytes 73736 | tf_op jit(solution)/shard_map/ppermute | solution.py:258
  137.7 4.1 %copy-start.10 = (f32[6,8,128]{2,1,0:T(8,128)}, f32[6,8,128]{2,1,0:T(8,128)S(1)}, u32[]{:S(2)}) copy-start(f32[6,8,128]{2,1,0:T(8,128)S(1)} %collective-permute-done.11.stats_recv_ref) | copy-start | bytes 73732
  138.4 11.3 %all-to-all-start.5 = ((bf16[8,4,2048]{2,1,0:T(4,128)(2,1)}), bf16[8,4,2048]{2,1,0:T(4,128)(2,1)S(1)}, u32[]{:S(2)}, u32[]{:S(2)}) async-start(bf16[8,4,2048]{2,1,0:T(4,128)(2,1)} %broadcast_in_dim.6), calls=%async_computation.5 | async-start | bytes 262144 | tf_op jit(solution)/shard_map/all_to_all | solution.py:199

commit v4 on v2

v4 whole, which is shorter than its diff:
```python
import functools
import math

import jax
import jax.numpy as jnp
from jax import lax
from jax.experimental import pallas as pl
from jax.experimental.pallas import tpu as pltpu
from jax.sharding import Mesh, PartitionSpec as P

HEAD = 128
SCALE = 1.0 / math.sqrt(HEAD)
MASKED = -1e30
GROUP = 16
STEP_GROUPS = 2
NEAR = ("x", "core")
BF16 = jnp.bfloat16
F32 = jnp.float32
SMEM = pl.BlockSpec(memory_space=pltpu.SMEM)
PARAMS = pltpu.CompilerParams(vmem_limit_bytes=16 * 1024 * 1024)


def dot(a, b, dims):
    return lax.dot_general(a, b, (dims, ((), ())), preferred_element_type=F32)


def dot_nt(a, b):
    return dot(a, b, ((1,), (1,)))


def dot_nn(a, b):
    return dot(a, b, ((1,), (0,)))


def dot_tn(a, b):
    return dot(a, b, ((0,), (0,)))


def masks(rows, crossing):
    key = lax.broadcasted_iota(jnp.int32, (rows, rows), 0)
    query = lax.broadcasted_iota(jnp.int32, (rows, rows), 1)
    own = (key % GROUP == query % GROUP) & (key // GROUP <= query // GROUP)
    cross = key % GROUP == query % GROUP + jnp.where(crossing, 0, GROUP)
    return own, cross


def scores_of(mask, keys, queries):
    return jnp.where(mask, dot_nt(keys, queries) * SCALE, MASKED)


def pieces(ref):
    for i in range(STEP_GROUPS):
        for h in range(ref.shape[-1] // HEAD):
            yield i, h, slice(i * GROUP, (i + 1) * GROUP), slice(h * HEAD, (h + 1) * HEAD)


def take(ref, j, rows, cols):
    return ref[:, j, rows, cols].reshape(-1, HEAD)


def softmax(q, k, k_cross, own_mask, cross_mask):
    s_own, s_cross = scores_of(own_mask, k, q), scores_of(cross_mask, k_cross, q)
    top = jnp.maximum(jnp.max(s_own, axis=0, keepdims=True), jnp.max(s_cross, axis=0, keepdims=True))
    e_own, e_cross = jnp.exp(s_own - top), jnp.exp(s_cross - top)
    total = jnp.sum(e_own, axis=0, keepdims=True) + jnp.sum(e_cross, axis=0, keepdims=True)
    return e_own / total, e_cross / total, top, total


def attend_kernel(side_ref, q_ref, kv_ref, recv_ref, att_ref):
    frames = q_ref.shape[0]
    own_mask, cross_mask = masks(frames * GROUP, side_ref[0] == 1)
    for _, _, rows, cols in pieces(q_ref):
        (k, v), (k_cross, v_cross) = ([take(ref, j, rows, cols) for j in range(2)] for ref in (kv_ref, recv_ref))
        q = q_ref[:, rows, cols].reshape(-1, HEAD)
        p_own, p_cross, _, _ = softmax(q, k, k_cross, own_mask, cross_mask)
        att = dot_tn(p_own.astype(BF16), v) + dot_tn(p_cross.astype(BF16), v_cross)
        att_ref[:, rows, cols] = att.astype(BF16).reshape(frames, GROUP, HEAD)


def query_kernel(side_ref, q_ref, kv_ref, recv_ref, g_ref, out_ref, stats_ref):
    frames = q_ref.shape[0]
    own_mask, cross_mask = masks(frames * GROUP, side_ref[0] == 1)
    for i, h, rows, cols in pieces(q_ref):
        (k, v), (k_cross, v_cross) = ([take(ref, j, rows, cols) for j in range(2)] for ref in (kv_ref, recv_ref))
        q = q_ref[:, rows, cols].reshape(-1, HEAD)
        p_own, p_cross, top, total = softmax(q, k, k_cross, own_mask, cross_mask)
        g = g_ref[:, rows, cols].reshape(-1, HEAD)
        gp_own, gp_cross = dot_nt(v, g), dot_nt(v_cross, g)
        row = jnp.sum(p_own * gp_own, axis=0, keepdims=True) + jnp.sum(p_cross * gp_cross, axis=0, keepdims=True)
        ds_own = (p_own * (gp_own - row) * SCALE).astype(BF16)
        ds_cross = (p_cross * (gp_cross - row) * SCALE).astype(BF16)
        grad = dot_tn(ds_own, k) + dot_tn(ds_cross, k_cross)
        out_ref[:, rows, cols] = grad.astype(BF16).reshape(frames, GROUP, HEAD)
        for j, stat in enumerate((top, total, row)):
            stats_ref[i, 3 * h + j : 3 * h + j + 1] = stat


def key_kernel(side_ref, q_ref, kv_ref, q_recv_ref, g_ref, g_recv_ref, stats_ref, stats_recv_ref, gq_ref, out_ref):
    frames = q_ref.shape[0]
    shape = (frames, GROUP, HEAD)
    own_mask, cross_mask = masks(frames * GROUP, side_ref[0] == 0)
    for i, h, rows, cols in pieces(q_ref):
        k, v = take(kv_ref, 0, rows, cols), take(kv_ref, 1, rows, cols)
        grad_k, grad_v = 0.0, 0.0
        for mask, q, g, stats in (
            (own_mask, q_ref[:, rows, cols], g_ref[:, rows, cols], stats_ref),
            (cross_mask, q_recv_ref[:, rows, cols], g_recv_ref[:, rows, cols], stats_recv_ref),
        ):
            top, total, row = (stats[i, 3 * h + j : 3 * h + j + 1] for j in range(3))
            q, g = q.reshape(-1, HEAD), g.reshape(-1, HEAD)
            probs = jnp.where(mask, jnp.exp(scores_of(mask, k, q) - top) / total, 0.0)
            ds = (probs * (dot_nt(v, g) - row) * SCALE).astype(BF16)
            grad_k = grad_k + dot_nn(ds, q)
            grad_v = grad_v + dot_nn(probs.astype(BF16), g)
        out_ref[:, 3 * i, :, cols] = gq_ref[:, rows, cols]
        out_ref[:, 3 * i + 1, :, cols] = grad_k.astype(BF16).reshape(shape)
        out_ref[:, 3 * i + 2, :, cols] = grad_v.astype(BF16).reshape(shape)


def owner_columns(place_ref, offset, w_shape):
    width, parts = w_shape[0], w_shape[1] // w_shape[0]
    owner = lax.rem(place_ref[0] + offset + parts, parts)
    return pl.ds(pl.multiple_of(owner * width, width), width)


def attended_kernel(offsets, place_ref, w_ref, *refs):
    blocks, g_ref = refs[:-1], refs[-1]
    half = blocks[-1].shape[0]
    acc = 0.0
    for offset, ref in zip(offsets, blocks[:-2]):
        acc = acc + dot_nt(ref[...], w_ref[:, owner_columns(place_ref, offset, w_ref.shape)])
    last = w_ref[:, owner_columns(place_ref, len(offsets) // 2 + 1, w_ref.shape)]
    g_ref[:half] = (acc[:half] + dot_nt(blocks[-2][...], last)).astype(BF16)
    g_ref[half:] = (acc[half:] + dot_nt(blocks[-1][...], last)).astype(BF16)


def term_kernel(offsets, place_ref, att_ref, *refs):
    blocks, term_ref = refs[:-1], refs[-1]
    half = blocks[-1].shape[0]
    for offset, ref in zip(offsets, blocks[:-2]):
        term_ref[:, owner_columns(place_ref, offset, term_ref.shape)] = dot_tn(att_ref[...], ref[...]).astype(BF16)
    last = dot_tn(att_ref[:half], blocks[-2][...]) + dot_tn(att_ref[half:], blocks[-1][...])
    term_ref[:, owner_columns(place_ref, len(offsets) // 2 + 1, term_ref.shape)] = last.astype(BF16)


def per_group(kernel, name, flops, side, args, outs, vmem=32, out_specs=None):
    items = args[0].shape[-2]

    def spec(a):
        if a.dtype == F32:
            return pl.BlockSpec((STEP_GROUPS,) + a.shape[1:], lambda i: (i, 0, 0))
        block = a.shape[:-2] + (STEP_GROUPS * GROUP, a.shape[-1])
        lead = (0,) * (len(a.shape) - 2)
        return pl.BlockSpec(block, lambda i: lead + (i, 0))

    return pl.pallas_call(
        kernel,
        grid=(items // (STEP_GROUPS * GROUP),),
        in_specs=[SMEM] + [spec(a) for a in args],
        out_specs=out_specs or [spec(a) for a in outs],
        out_shape=[jax.ShapeDtypeStruct(a.shape, a.dtype) for a in outs],
        compiler_params=pltpu.CompilerParams(vmem_limit_bytes=vmem * 1024 * 1024),
        cost_estimate=pl.CostEstimate(flops=flops, bytes_accessed=4_000_000, transcendentals=400_000),
        name=name,
    )(side, *args)


def project(kernel, name, blocks, offsets, first, shape):
    vmem = pl.BlockSpec(memory_space=pltpu.VMEM)
    return pl.pallas_call(
        functools.partial(kernel, offsets),
        in_specs=[SMEM] + [vmem] * (1 + len(blocks)),
        out_specs=vmem,
        out_shape=jax.ShapeDtypeStruct(shape, BF16),
        compiler_params=PARAMS,
        cost_estimate=pl.CostEstimate(flops=800_000_000, bytes_accessed=4_500_000, transcendentals=0),
        name=name,
    )(lax.axis_index("tensor").reshape(1), first, *blocks)


def exchange(x, axes):
    return lax.all_to_all(x, axes, 0, 0, tiled=True)


def scatter_sum(x, axes):
    parts = exchange(x.reshape(lax.axis_size(axes), -1, x.shape[-1]), axes)
    return jnp.sum(parts.astype(F32), axis=0)


def shift(x, axis, by):
    size = lax.axis_size(axis)
    return lax.ppermute(x, axis, [(i, (i + by) % size) for i in range(size)])


def ring(x):
    size = lax.axis_size("tensor")
    half = x.shape[0] // 2
    blocks, offsets, up, down = [x], [0], x, x
    for step in range(1, size // 2):
        up, down = shift(up, "tensor", 1), shift(down, "tensor", -1)
        blocks += [up, down]
        offsets += [-step, step]
    blocks += [shift(up[:half], "tensor", 1), shift(down[half:], "tensor", -1)]
    return blocks, offsets


def gather(x, axes):
    copies = jnp.broadcast_to(x[None], (lax.axis_size(axes),) + x.shape)
    return exchange(copies, axes).reshape(-1, x.shape[-1])


def local(queries, keys, values, out_grad, out_proj):
    clips, _, patches, width = queries.shape
    near = lax.axis_size(NEAR)
    tokens = clips * patches
    items = tokens // near
    factor = 1.0 / math.sqrt(tokens * near * lax.axis_size("zh") * lax.axis_size("dp"))
    side = lax.axis_index("zh").astype(jnp.int32).reshape(1)
    queries, keys, values, out_grad = (a.reshape(near, items, width) for a in (queries, keys, values, out_grad))

    grad_own = exchange(out_grad, NEAR).reshape(tokens, width)
    qkv, grad_own = lax.optimization_barrier((jnp.stack([queries, keys, values], axis=1), grad_own))
    qkv = exchange(qkv, NEAR)
    q, kv = qkv[:, 0], qkv[:, 1:]
    kv_recv = lax.ppermute(kv, "zh", [(0, 1)])
    blocks, offsets = ring(grad_own)
    like = jax.ShapeDtypeStruct(q.shape, BF16)
    q_recv = lax.ppermute(q, "zh", [(1, 0)])
    g = project(attended_kernel, "grad_attended", blocks, offsets, out_proj, (tokens, width)).reshape(q.shape)
    g, kv_recv = lax.optimization_barrier((g, kv_recv))
    (att,) = per_group(attend_kernel, "attend", 400_000_000, side, [q, kv, kv_recv], [like], 8)
    term = project(term_kernel, "term", blocks, offsets, att.reshape(tokens, width), out_proj.shape)
    term, q_recv = lax.optimization_barrier((term, q_recv))
    g_recv = lax.ppermute(g, "zh", [(1, 0)])

    stats = jax.ShapeDtypeStruct((items // GROUP, 8, near * GROUP), F32)
    grad_q, stats = per_group(query_kernel, "grad_queries", 700_000_000, side, [q, kv, kv_recv, g], [like, stats], 8)

    total = scatter_sum(term, "x").astype(BF16)
    total = scatter_sum(total, "core").astype(BF16)
    total, g_recv, grad_q, stats = lax.optimization_barrier((total, g_recv, grad_q, stats))
    stats_recv = lax.ppermute(stats, "zh", [(1, 0)])
    total = (scatter_sum(total, ("zh", "dp")) * factor).astype(BF16)
    total, stats_recv = lax.optimization_barrier((total, stats_recv))
    args = [q, kv, q_recv, g, g_recv, stats, stats_recv, grad_q]
    groups, share = items // GROUP, out_proj.size // (near * GROUP * width)
    grads = jax.ShapeDtypeStruct((near, 3 * groups + share, GROUP, width), BF16)
    block = pl.BlockSpec((near, 3 * STEP_GROUPS, GROUP, width), lambda i: (0, i, 0, 0))
    (grads,) = per_group(key_kernel, "grad_keys_values", 1_000_000_000, side, args, [grads], 8, [block])
    total = gather(total, ("zh", "dp"))
    total, grads = lax.optimization_barrier((total, grads))
    copies = jnp.broadcast_to(total.reshape(1, share, GROUP, width), (near, share, GROUP, width))
    home = exchange(lax.dynamic_update_slice(grads, copies, (0, 3 * groups, 0, 0)), NEAR)
    grad_proj = home[:, 3 * groups :].reshape(out_proj.shape)
    grads = home[:, : 3 * groups].reshape(near, groups, 3, GROUP, width)
    return tuple(grads[:, :, j].reshape(clips, 1, patches, width) for j in range(3)) + (grad_proj,)


def solution(mesh):
    fine = Mesh(mesh.devices.reshape(2, 4, 2, 8, 4), ("zh", "x", "core", "tensor", "dp"))
    spec = P("dp", ("zh", "x", "core"), None, "tensor")
    return jax.shard_map(
        local,
        mesh=fine,
        in_specs=(spec, spec, spec, spec, P("tensor", None)),
        out_specs=(spec, spec, spec, P("tensor", None)),
        check_vma=False,
    )
```

time: 197 us -> 188 us (0.954)
  starting transfers between devices: 79 us -> 73 us
  waiting for transfers between devices: 36.1 us -> 30.1 us
  local copies, waits for them, and re-layouts: 12.1 us -> 14.3 us
    all_to_all x6 -> x5, waiting for transfers between devices: 23.6 us -> 14.7 us  [exchange(): return lax.all_to_all(x, axes, 0, 0, tiled=True)]
    all_to_all x6 -> x5, starting transfers between devices: 42.1 us -> 35.2 us  [exchange(): return lax.all_to_all(x, axes, 0, 0, tiled=True)]
    ppermute x8, waiting for transfers between devices: 10.8 us -> 13.7 us  [shift(): return lax.ppermute(x, axis, [(i, (i + by) % size) for i in range(size)])]
    unnamed x30 -> x16, local copies, waits for them, and re-layouts: 3.98 us -> 5.7 us
    all_to_all x3 -> x2, blocking collectives: 44.3 us -> 44.6 us  [exchange(): return lax.all_to_all(x, axes, 0, 0, tiled=True)]
    pallas_call x4 -> x5, Pallas kernels: 20.5 us -> 20.7 us  [the longest x3 15.3 us: per_group(): pl.pallas_call(kernel, grid=(items // (STEP_GROUPS * GROUP),), in_specs=[...]
  transfers between devices with their start and end apart: 18 -> 17, of which waited for: 8 -> 9; matrix products, arithmetic and copies ran while one was open for 4% -> 3% of each run, Pallas kernels for 10% -> 11%
where the time goes in v4:
time: 188 us; the launch traced here: 186 us
  starting transfers between devices  73 us (39%)
  blocking collectives  44.6 us (24%)
  waiting for transfers between devices  30.1 us (16%)
  Pallas kernels  20.7 us (11%)
  local copies, waits for them, and re-layouts  14.3 us (8%)
  other arithmetic  2.79 us (1%)
    all_to_all x2, blocking collectives, exchange(): return lax.all_to_all(x, axes, 0, 0, tiled=True)  44.6 us
    all_to_all x5, starting transfers between devices, exchange(): return lax.all_to_all(x, axes, 0, 0, tiled=True)  35.2 us
    ppermute x8, starting transfers between devices, shift(): return lax.ppermute(x, axis, [(i, (i + by) % size) for i in range(size)])  25.9 us
    pallas_call x3, Pallas kernels, per_group(): pl.pallas_call(kernel, grid=(items // (STEP_GROUPS * GROUP),), in_specs=[...  15.3 us
    all_to_all x5, waiting for transfers between devices, exchange(): return lax.all_to_all(x, axes, 0, 0, tiled=True)  14.7 us
    ppermute x8, waiting for transfers between devices, shift(): return lax.ppermute(x, axis, [(i, (i + by) % size) for i in range(size)])  13.7 us
    ppermute x1, starting transfers between devices, local(): kv_recv = lax.ppermute(kv, 'zh', [(0, 1)])  7.95 us
    unnamed x16, local copies, waits for them, and re-layouts  5.7 us
  transfers between devices with their start and end apart: 17, of which 9 were waited for; matrix products, arithmetic and copies ran while one was open for 3% of the time, Pallas kernels for 11%

profile of v4, /device:TPU:1, one launch (start us, length us, event | category | flops | bytes accessed | tf_op | source)
XLA Modules:
  0.0 186.3 jit_solution(203654670389751195)
XLA Ops:
  0.6 10.2 %all-to-all-start = ((bf16[8,96,256]{2,1,0:T(8,128)(2,1)}), bf16[8,96,256]{2,1,0:T(8,128)(2,1)S(1)}, u32[]{:S(2)}, u32[]{:S(2)}) async-start(bf16[8,96,256]{2,1,0:T(8,128)(2,1)} %bitcast.37), calls=%async_computation | async-start | bytes 786432 | tf_op jit(solution)/shard_map/all_to_all | solution.py:182
  10.9 2.4 %pad_maximum_fusion = bf16[8,3,96,256]{3,2,1,0:T(8,128)(2,1)} fusion(bf16[8,1,96,256]{3,2,1,0:T(8,128)(2,1)} %bitcast.31, bf16[8,1,96,256]{3,2,1,0:T(8,128)(2,1)} %bitcast.32, bf16[8,1,96,256]{3,2,1,0:T(8,128)(2,1)} %bitcast.33), kind=kLoop, calls=%fused_computation | loop fusion | flops 1179648 | bytes 2359296 | tf_op jit(solution)/shard_map/stack | solution.py:222
  13.2 5.7 %all-to-all-done = bf16[8,96,256]{2,1,0:T(8,128)(2,1)S(1)} async-done(((bf16[8,96,256]{2,1,0:T(8,128)(2,1)}), bf16[8,96,256]{2,1,0:T(8,128)(2,1)S(1)}, u32[]{:S(2)}, u32[]{:S(2)}) %all-to-all-start) | async-done | bytes 393248 | tf_op jit(solution)/shard_map/all_to_all | solution.py:182
  19.0 5.0 %all-to-all-start.1 = ((bf16[8,3,96,256]{3,2,1,0:T(8,128)(2,1)}), bf16[8,3,96,256]{3,2,1,0:T(8,128)(2,1)}, u32[]{:S(2)}, u32[]{:S(2)}) async-start(bf16[8,3,96,256]{3,2,1,0:T(8,128)(2,1)} %pad_maximum_fusion), calls=%async_computation.1 | async-start | bytes 2359296 | tf_op jit(solution)/shard_map/all_to_all | solution.py:182
  24.0 1.9 %collective-permute-start = (bf16[768,256]{1,0:T(8,128)(2,1)S(1)}, bf16[768,256]{1,0:T(8,128)(2,1)S(1)}, u32[]{:S(2)}, u32[]{:S(2)}) collective-permute-start(bf16[768,256]{1,0:T(8,128)(2,1)S(1)} %bitcast.21), channel_id=1, source_target_pairs={{0,4},{4,8},{8,12},{12,16},{16,20},{20,24},{24,28},{28,0},{1,5},{5... | collective-permute-start | bytes 1179656 | tf_op jit(solution)/shard_map/ppermute | solution.py:192
  25.9 4.6 %collective-permute-start.1 = (bf16[768,256]{1,0:T(8,128)(2,1)S(1)}, bf16[768,256]{1,0:T(8,128)(2,1)S(1)}, u32[]{:S(2)}, u32[]{:S(2)}) collective-permute-start(bf16[768,256]{1,0:T(8,128)(2,1)S(1)} %bitcast.22), channel_id=1, source_target_pairs={{0,28},{4,0},{8,4},{12,8},{16,12},{20,16},{24,20},{28,24},{1,29},{... | collective-permute-start | bytes 1179656 | tf_op jit(solution)/shard_map/ppermute | solution.py:192
  30.5 7.2 %collective-permute-done.refs_1_ = bf16[768,256]{1,0:T(8,128)(2,1)S(1)} collective-permute-done((bf16[768,256]{1,0:T(8,128)(2,1)S(1)}, bf16[768,256]{1,0:T(8,128)(2,1)S(1)}, u32[]{:S(2)}, u32[]{:S(2)}) %collective-permute-start) | collective-permute-done | bytes 393248 | tf_op jit(solution)/shard_map/ppermute | solution.py:192
  37.6 1.9 %collective-permute-start.2 = (bf16[768,256]{1,0:T(8,128)(2,1)S(1)}, bf16[768,256]{1,0:T(8,128)(2,1)}, u32[]{:S(2)}, u32[]{:S(2)}) collective-permute-start(bf16[768,256]{1,0:T(8,128)(2,1)S(1)} %collective-permute-done.refs_1_), channel_id=1, source_target_pairs={{0,4},{4,8},{8,12},{12,16},{16,20},{20,24},{24,28},{28,0},{1,5},{5... | collective-permute-start | bytes 1179656 | tf_op jit(solution)/shard_map/ppermute | solution.py:192
  39.6 4.6 %collective-permute-start.3 = (bf16[768,256]{1,0:T(8,128)(2,1)S(1)}, bf16[768,256]{1,0:T(8,128)(2,1)}, u32[]{:S(2)}, u32[]{:S(2)}) collective-permute-start(bf16[768,256]{1,0:T(8,128)(2,1)S(1)} %collective-permute-done.1.refs_2_), channel_id=1, source_target_pairs={{0,28},{4,0},{8,4},{12,8},{16,12},{20,16},{24,20},{28,24},{1,29},{... | collective-permute-start | bytes 1179656 | tf_op jit(solution)/shard_map/ppermute | solution.py:192
  44.2 1.2 slice.37.kv_ref
  45.4 8.0 %collective-permute-start.8 = (bf16[8,2,96,256]{3,2,1,0:T(8,128)(2,1)S(1)}, bf16[8,2,96,256]{3,2,1,0:T(8,128)(2,1)}, u32[]{:S(2)}, u32[]{:S(2)}) collective-permute-start(bf16[8,2,96,256]{3,2,1,0:T(8,128)(2,1)S(1)} %slice.37.kv_ref), channel_id=1, source_target_pairs={{0,256},{1,257},{2,258},{3,259},{4,260},{5,261},{6,262},{7,263},{8... | collective-permute-start | bytes 2359304 | tf_op jit(solution)/shard_map/ppermute | solution.py:225
  53.3 1.9 %collective-permute-start.4 = (bf16[768,256]{1,0:T(8,128)(2,1)}, bf16[768,256]{1,0:T(8,128)(2,1)S(1)}, u32[]{:S(2)}, u32[]{:S(2)}) collective-permute-start(bf16[768,256]{1,0:T(8,128)(2,1)} %collective-permute-done.2.refs_3_), channel_id=1, source_target_pairs={{0,4},{4,8},{8,12},{12,16},{16,20},{20,24},{24,28},{28,0},{1,5},{5... | collective-permute-start | bytes 1179656 | tf_op jit(solution)/shard_map/ppermute | solution.py:192
  55.2 4.6 %collective-permute-start.5 = (bf16[768,256]{1,0:T(8,128)(2,1)}, bf16[768,256]{1,0:T(8,128)(2,1)S(1)}, u32[]{:S(2)}, u32[]{:S(2)}) collective-permute-start(bf16[768,256]{1,0:T(8,128)(2,1)} %collective-permute-done.3.refs_4_), channel_id=1, source_target_pairs={{0,28},{4,0},{8,4},{12,8},{16,12},{20,16},{24,20},{28,24},{1,29},{... | collective-permute-start | bytes 1179656 | tf_op jit(solution)/shard_map/ppermute | solution.py:192
  59.8 1.0 slice_bitcast_fusion.q_ref
  60.9 1.3 collective-permute-start.9
  62.2 3.6 %collective-permute-done.4.refs_5_ = bf16[768,256]{1,0:T(8,128)(2,1)S(1)} collective-permute-done((bf16[768,256]{1,0:T(8,128)(2,1)}, bf16[768,256]{1,0:T(8,128)(2,1)S(1)}, u32[]{:S(2)}, u32[]{:S(2)}) %collective-permute-start.4) | collective-permute-done | bytes 393248 | tf_op jit(solution)/shard_map/ppermute | solution.py:192
  65.8 0.7 slice.38
  66.5 1.9 %collective-permute-start.6 = (bf16[384,256]{1,0:T(8,128)(2,1)}, bf16[384,256]{1,0:T(8,128)(2,1)S(1)}, u32[]{:S(2)}, u32[]{:S(2)}) collective-permute-start(bf16[384,256]{1,0:T(8,128)(2,1)} %slice.38), channel_id=1, source_target_pairs={{0,4},{4,8},{8,12},{12,16},{16,20},{20,24},{24,28},{28,0},{1,5},{5... | collective-permute-start | bytes 589832 | tf_op jit(solution)/shard_map/ppermute | solution.py:192
  68.4 0.7 slice.39
  69.1 4.6 %collective-permute-start.7 = (bf16[384,256]{1,0:T(8,128)(2,1)}, bf16[384,256]{1,0:T(8,128)(2,1)}, u32[]{:S(2)}, u32[]{:S(2)}) collective-permute-start(bf16[384,256]{1,0:T(8,128)(2,1)} %slice.39), channel_id=1, source_target_pairs={{0,28},{4,0},{8,4},{12,8},{16,12},{20,16},{24,20},{28,24},{1,29},{... | collective-permute-start | bytes 589832 | tf_op jit(solution)/shard_map/ppermute | solution.py:192
  73.7 1.0 collective-permute-done.6.refs_7_
  74.7 1.9 %collective-permute-done.7.refs_8_ = bf16[384,256]{1,0:T(8,128)(2,1)} collective-permute-done((bf16[384,256]{1,0:T(8,128)(2,1)}, bf16[384,256]{1,0:T(8,128)(2,1)}, u32[]{:S(2)}, u32[]{:S(2)}) %collective-permute-start.7) | collective-permute-done | bytes 196640 | tf_op jit(solution)/shard_map/ppermute | solution.py:192
  76.6 1.2 copy-done.3
  77.8 2.2 %grad_attended.1 = bf16[768,256]{1,0:T(8,128)(2,1)S(1)} custom-call(s32[1]{0:T(128)} %bitcast.place_ref, bf16[256,2048]{1,0:T(8,128)(2,1)S(1)} %copy-done.3, bf16[768,256]{1,0:T(8,128)(2,1)S(1)} %bitcast.23, bf16[768,256]{1,0:T(8,128)(2,1)S(1)} %collective-permute-done.refs_1_, bf16[768,256]{1,0:T(8,128)(2,1)S(1)} %collective-permute-done.1.refs_2_, ...), custom_call_target="tpu_custom_call" | custom-call | flops 800000000 | bytes 4500000 | tf_op jit(solution)/shard_map/grad_attended/pallas_call | solution.py:170
  80.0 0.7 copy-done
  80.7 5.0 %attend.1 = bf16[8,96,256]{2,1,0:T(8,128)(2,1)S(1)} custom-call(s32[1]{0:T(128)} %bitcast.1.side_ref, bf16[8,96,256]{2,1,0:T(8,128)(2,1)S(1)} %slice_bitcast_fusion.q_ref, bf16[8,2,96,256]{3,2,1,0:T(8,128)(2,1)S(1)} %slice.37.kv_ref, bf16[8,2,96,256]{3,2,1,0:T(8,128)(2,1)} %collective-permute-done.8.recv_ref), custom_call_target="tpu_custom_call" | custom-call | flops 400000000 | bytes 4000000 | tf_op jit(solution)/shard_map/attend/pallas_call | solution.py:156
  85.7 3.3 %term.1 = bf16[256,2048]{1,0:T(8,128)(2,1)} custom-call(s32[1]{0:T(128)} %bitcast.place_ref, bf16[768,256]{1,0:T(8,128)(2,1)S(1)} %bitcast.25, bf16[768,256]{1,0:T(8,128)(2,1)S(1)} %bitcast.24, bf16[768,256]{1,0:T(8,128)(2,1)S(1)} %collective-permute-done.refs_1_, bf16[768,256]{1,0:T(8,128)(2,1)S(1)} %collective-permute-done.1.refs_2_, ...), custom_call_target="tpu_custom_call" | custom-call | flops 800000000 | bytes 4500000 | tf_op jit(solution)/shard_map/term/pallas_call | solution.py:170
  89.0 3.8 %all-to-all-start.2 = ((bf16[4,64,2048]{2,1,0:T(8,128)(2,1)}), bf16[4,64,2048]{2,1,0:T(8,128)(2,1)S(1)}, u32[]{:S(2)}, u32[]{:S(2)}) async-start(bf16[4,64,2048]{2,1,0:T(8,128)(2,1)} %bitcast.10), calls=%async_computation.2 | async-start | bytes 2097152 | tf_op jit(solution)/shard_map/all_to_all | solution.py:182
  92.8 1.3 collective-permute-start.10
  94.1 5.6 %grad_queries.1 = (bf16[8,96,256]{2,1,0:T(8,128)(2,1)S(1)}, f32[6,8,128]{2,1,0:T(8,128)S(1)}) custom-call(s32[1]{0:T(128)} %bitcast.1.side_ref, bf16[8,96,256]{2,1,0:T(8,128)(2,1)S(1)} %slice_bitcast_fusion.q_ref, bf16[8,2,96,256]{3,2,1,0:T(8,128)(2,1)S(1)} %slice.37.kv_ref, bf16[8,2,96,256]{3,2,1,0:T(8,128)(2,1)} %collective-permute-done.8.recv_ref, ...), custom_call_target="tpu_custom_call" | custom-call | flops 700000000 | bytes 4000000 | tf_op jit(solution)/shard_map/grad_queries/pallas_call | solution.py:156
  99.7 0.7 copy-done.6
  100.4 2.1 %all-to-all-done.2 = bf16[4,64,2048]{2,1,0:T(8,128)(2,1)S(1)} async-done(((bf16[4,64,2048]{2,1,0:T(8,128)(2,1)}), bf16[4,64,2048]{2,1,0:T(8,128)(2,1)S(1)}, u32[]{:S(2)}, u32[]{:S(2)}) %all-to-all-start.2) | async-done | bytes 1048608 | tf_op jit(solution)/shard_map/all_to_all | solution.py:182
  102.7 11.2 %all_to_all.35 = bf16[2,32,2048]{2,1,0:T(8,128)(2,1)S(1)} all-to-all(bf16[2,32,2048]{2,1,0:T(8,128)(2,1)S(1)} %bitcast.30), channel_id=1, replica_groups=mesh['zh'=2,'x'=4,'core'=2,'tensor'=8,'dp'=4] {'core'}, dimensions={0} | all-to-all | bytes 524288 | tf_op jit(solution)/shard_map/all_to_all | solution.py:182
  114.0 0.8 reshape.56
  114.8 12.2 %all-to-all-start.4 = ((bf16[8,4,2048]{2,1,0:T(4,128)(2,1)}), bf16[8,4,2048]{2,1,0:T(4,128)(2,1)S(1)}, u32[]{:S(2)}, u32[]{:S(2)}) async-start(bf16[8,4,2048]{2,1,0:T(4,128)(2,1)} %reshape.56), calls=%async_computation.4 | async-start | bytes 262144 | tf_op jit(solution)/shard_map/all_to_all | solution.py:182
  127.0 1.3 collective-permute-start.11
  128.3 6.6 %all-to-all-done.4 = bf16[8,4,2048]{2,1,0:T(4,128)(2,1)S(1)} async-done(((bf16[8,4,2048]{2,1,0:T(4,128)(2,1)}), bf16[8,4,2048]{2,1,0:T(4,128)(2,1)S(1)}, u32[]{:S(2)}, u32[]{:S(2)}) %all-to-all-start.4) | async-done | bytes 131104 | tf_op jit(solution)/shard_map/all_to_all | solution.py:182
  135.1 1.7 collective-permute-done.11.stats_recv_ref
  136.8 0.7 broadcast_in_dim.6
  137.5 4.0 %all-to-all-start.5 = ((bf16[8,4,2048]{2,1,0:T(4,128)(2,1)}), bf16[8,4,2048]{2,1,0:T(4,128)(2,1)}, u32[]{:S(2)}, u32[]{:S(2)}) async-start(bf16[8,4,2048]{2,1,0:T(4,128)(2,1)} %broadcast_in_dim.6), calls=%async_computation.5 | async-start | bytes 262144 | tf_op jit(solution)/shard_map/all_to_all | solution.py:182
  141.5 1.0 copy-done.2
  142.5 1.0 copy-done.5
  143.5 1.0 copy-done.7
  144.5 4.7 %grad_keys_values.1 = bf16[8,34,16,256]{3,2,1,0:T(8,128)(2,1)S(1)} custom-call(s32[1]{0:T(128)} %bitcast.1.side_ref, bf16[8,96,256]{2,1,0:T(8,128)(2,1)S(1)} %slice_bitcast_fusion.q_ref, bf16[8,2,96,256]{3,2,1,0:T(8,128)(2,1)S(1)} %slice.37.kv_ref, bf16[8,96,256]{2,1,0:T(8,128)(2,1)} %collective-permute-done.9.q_recv_ref, bf16[8,96,256]{2,1,0:T(8,128)(2,1)S(1)} %bitcast.28, ...), custom_call_target="tpu_custom_call" | custom-call | flops 1000000000 | bytes 4000000 | tf_op jit(solution)/shard_map/grad_keys_values/pallas_call | solution.py:156
  149.4 0.9 reshape.57
  150.5 33.3 %all_to_all.36 = bf16[8,34,16,256]{3,2,1,0:T(8,128)(2,1)S(1)} all-to-all(bf16[8,34,16,256]{3,2,1,0:T(8,128)(2,1)S(1)} %broadcast_dynamic-update-slice_fusion), channel_id=1, replica_groups=mesh['zh'=2,'x'=4,'core'=2,'tensor'=8,'dp'=4] {'x','core'}, dimensions={0} | all-to-all | bytes 4456448 | tf_op jit(solution)/shard_map/all_to_all | solution.py:182
  183.9 1.0 fusion
  185.0 1.3 reshape.59
  (27 shorter events, 1.0 us)
Async XLA Ops:
  0.6 18.3 %all-to-all-start = ((bf16[8,96,256]{2,1,0:T(8,128)(2,1)}), bf16[8,96,256]{2,1,0:T(8,128)(2,1)S(1)}, u32[]{:S(2)}, u32[]{:S(2)}) async-start(bf16[8,96,256]{2,1,0:T(8,128)(2,1)} %bitcast.37), calls=%async_computation | async-start | bytes 786432 | tf_op jit(solution)/shard_map/all_to_all | solution.py:182
  19.0 25.2 %all-to-all-start.1 = ((bf16[8,3,96,256]{3,2,1,0:T(8,128)(2,1)}), bf16[8,3,96,256]{3,2,1,0:T(8,128)(2,1)}, u32[]{:S(2)}, u32[]{:S(2)}) async-start(bf16[8,3,96,256]{3,2,1,0:T(8,128)(2,1)} %pad_maximum_fusion), calls=%async_computation.1 | async-start | bytes 2359296 | tf_op jit(solution)/shard_map/all_to_all | solution.py:182
  24.0 13.7 %collective-permute-start = (bf16[768,256]{1,0:T(8,128)(2,1)S(1)}, bf16[768,256]{1,0:T(8,128)(2,1)S(1)}, u32[]{:S(2)}, u32[]{:S(2)}) collective-permute-start(bf16[768,256]{1,0:T(8,128)(2,1)S(1)} %bitcast.21), channel_id=1, source_target_pairs={{0,4},{4,8},{8,12},{12,16},{16,20},{20,24},{24,28},{28,0},{1,5},{5... | collective-permute-start | bytes 1179656 | tf_op jit(solution)/shard_map/ppermute | solution.py:192
  25.9 13.7 %collective-permute-start.1 = (bf16[768,256]{1,0:T(8,128)(2,1)S(1)}, bf16[768,256]{1,0:T(8,128)(2,1)S(1)}, u32[]{:S(2)}, u32[]{:S(2)}) collective-permute-start(bf16[768,256]{1,0:T(8,128)(2,1)S(1)} %bitcast.22), channel_id=1, source_target_pairs={{0,28},{4,0},{8,4},{12,8},{16,12},{20,16},{24,20},{28,24},{1,29},{... | collective-permute-start | bytes 1179656 | tf_op jit(solution)/shard_map/ppermute | solution.py:192
  37.6 15.7 %collective-permute-start.2 = (bf16[768,256]{1,0:T(8,128)(2,1)S(1)}, bf16[768,256]{1,0:T(8,128)(2,1)}, u32[]{:S(2)}, u32[]{:S(2)}) collective-permute-start(bf16[768,256]{1,0:T(8,128)(2,1)S(1)} %collective-permute-done.refs_1_), channel_id=1, source_target_pairs={{0,4},{4,8},{8,12},{12,16},{16,20},{20,24},{24,28},{28,0},{1,5},{5... | collective-permute-start | bytes 1179656 | tf_op jit(solution)/shard_map/ppermute | solution.py:192
  39.6 15.7 %collective-permute-start.3 = (bf16[768,256]{1,0:T(8,128)(2,1)S(1)}, bf16[768,256]{1,0:T(8,128)(2,1)}, u32[]{:S(2)}, u32[]{:S(2)}) collective-permute-start(bf16[768,256]{1,0:T(8,128)(2,1)S(1)} %collective-permute-done.1.refs_2_), channel_id=1, source_target_pairs={{0,28},{4,0},{8,4},{12,8},{16,12},{20,16},{24,20},{28,24},{1,29},{... | collective-permute-start | bytes 1179656 | tf_op jit(solution)/shard_map/ppermute | solution.py:192
  45.4 35.4 %collective-permute-start.8 = (bf16[8,2,96,256]{3,2,1,0:T(8,128)(2,1)S(1)}, bf16[8,2,96,256]{3,2,1,0:T(8,128)(2,1)}, u32[]{:S(2)}, u32[]{:S(2)}) collective-permute-start(bf16[8,2,96,256]{3,2,1,0:T(8,128)(2,1)S(1)} %slice.37.kv_ref), channel_id=1, source_target_pairs={{0,256},{1,257},{2,258},{3,259},{4,260},{5,261},{6,262},{7,263},{8... | collective-permute-start | bytes 2359304 | tf_op jit(solution)/shard_map/ppermute | solution.py:225
  53.3 12.5 %collective-permute-start.4 = (bf16[768,256]{1,0:T(8,128)(2,1)}, bf16[768,256]{1,0:T(8,128)(2,1)S(1)}, u32[]{:S(2)}, u32[]{:S(2)}) collective-permute-start(bf16[768,256]{1,0:T(8,128)(2,1)} %collective-permute-done.2.refs_3_), channel_id=1, source_target_pairs={{0,4},{4,8},{8,12},{12,16},{16,20},{20,24},{24,28},{28,0},{1,5},{5... | collective-permute-start | bytes 1179656 | tf_op jit(solution)/shard_map/ppermute | solution.py:192
  55.2 13.1 %collective-permute-start.5 = (bf16[768,256]{1,0:T(8,128)(2,1)}, bf16[768,256]{1,0:T(8,128)(2,1)S(1)}, u32[]{:S(2)}, u32[]{:S(2)}) collective-permute-start(bf16[768,256]{1,0:T(8,128)(2,1)} %collective-permute-done.3.refs_4_), channel_id=1, source_target_pairs={{0,28},{4,0},{8,4},{12,8},{16,12},{20,16},{24,20},{28,24},{1,29},{... | collective-permute-start | bytes 1179656 | tf_op jit(solution)/shard_map/ppermute | solution.py:192
  60.9 28.1 %collective-permute-start.9 = (bf16[8,96,256]{2,1,0:T(8,128)(2,1)S(1)}, bf16[8,96,256]{2,1,0:T(8,128)(2,1)}, u32[]{:S(2)}, u32[]{:S(2)}) collective-permute-start(bf16[8,96,256]{2,1,0:T(8,128)(2,1)S(1)} %slice_bitcast_fusion.q_ref), channel_id=1, source_target_pairs={{256,0},{257,1},{258,2},{259,3},{260,4},{261,5},{262,6},{263,7},{2... | collective-permute-start | bytes 1179656 | tf_op jit(solution)/shard_map/ppermute | solution.py:228
  66.5 8.2 %collective-permute-start.6 = (bf16[384,256]{1,0:T(8,128)(2,1)}, bf16[384,256]{1,0:T(8,128)(2,1)S(1)}, u32[]{:S(2)}, u32[]{:S(2)}) collective-permute-start(bf16[384,256]{1,0:T(8,128)(2,1)} %slice.38), channel_id=1, source_target_pairs={{0,4},{4,8},{8,12},{12,16},{16,20},{20,24},{24,28},{28,0},{1,5},{5... | collective-permute-start | bytes 589832 | tf_op jit(solution)/shard_map/ppermute | solution.py:192
  69.1 7.5 %collective-permute-start.7 = (bf16[384,256]{1,0:T(8,128)(2,1)}, bf16[384,256]{1,0:T(8,128)(2,1)}, u32[]{:S(2)}, u32[]{:S(2)}) collective-permute-start(bf16[384,256]{1,0:T(8,128)(2,1)} %slice.39), channel_id=1, source_target_pairs={{0,28},{4,0},{8,4},{12,8},{16,12},{20,16},{24,20},{28,24},{1,29},{... | collective-permute-start | bytes 589832 | tf_op jit(solution)/shard_map/ppermute | solution.py:192
  76.6 1.2 copy-start.3
  80.0 0.7 copy-start
  89.0 3.8 %copy-start.1 = (bf16[768,256]{1,0:T(8,128)(2,1)S(1)}, bf16[768,256]{1,0:T(8,128)(2,1)}, u32[]{:S(2)}) copy-start(bf16[768,256]{1,0:T(8,128)(2,1)} %copy-done) | copy-start | bytes 1179652
  89.0 13.5 %all-to-all-start.2 = ((bf16[4,64,2048]{2,1,0:T(8,128)(2,1)}), bf16[4,64,2048]{2,1,0:T(8,128)(2,1)S(1)}, u32[]{:S(2)}, u32[]{:S(2)}) async-start(bf16[4,64,2048]{2,1,0:T(8,128)(2,1)} %bitcast.10), calls=%async_computation.2 | async-start | bytes 2097152 | tf_op jit(solution)/shard_map/all_to_all | solution.py:182
  92.8 21.2 %collective-permute-start.10 = (bf16[8,96,256]{2,1,0:T(8,128)(2,1)S(1)}, bf16[8,96,256]{2,1,0:T(8,128)(2,1)S(1)}, u32[]{:S(2)}, u32[]{:S(2)}) collective-permute-start(bf16[8,96,256]{2,1,0:T(8,128)(2,1)S(1)} %bitcast.26), channel_id=1, source_target_pairs={{256,0},{257,1},{258,2},{259,3},{260,4},{261,5},{262,6},{263,7},{2... | collective-permute-start | bytes 1179656 | tf_op jit(solution)/shard_map/ppermute | solution.py:234
  99.7 0.7 copy-start.6
  114.0 23.4 %copy-start.4 = (bf16[8,96,256]{2,1,0:T(8,128)(2,1)}, bf16[8,96,256]{2,1,0:T(8,128)(2,1)S(1)}, u32[]{:S(2)}) copy-start(bf16[8,96,256]{2,1,0:T(8,128)(2,1)S(1)} %collective-permute-done.10.g_recv_ref) | copy-start | bytes 1179652
  114.8 20.1 %all-to-all-start.4 = ((bf16[8,4,2048]{2,1,0:T(4,128)(2,1)}), bf16[8,4,2048]{2,1,0:T(4,128)(2,1)S(1)}, u32[]{:S(2)}, u32[]{:S(2)}) async-start(bf16[8,4,2048]{2,1,0:T(4,128)(2,1)} %reshape.56), calls=%async_computation.4 | async-start | bytes 262144 | tf_op jit(solution)/shard_map/all_to_all | solution.py:182
  127.0 9.8 %collective-permute-start.11 = (f32[6,8,128]{2,1,0:T(8,128)S(1)}, f32[6,8,128]{2,1,0:T(8,128)S(1)}, u32[]{:S(2)}, u32[]{:S(2)}) collective-permute-start(f32[6,8,128]{2,1,0:T(8,128)S(1)} %get-tuple-element.28.stats_ref), channel_id=1, source_target_pairs={{256,0},{257,1},{258,2},{259,3},{260,4},{261,5},{262,6},{263,7},{2... | collective-permute-start | bytes 73736 | tf_op jit(solution)/shard_map/ppermute | solution.py:242
  137.5 11.9 %all-to-all-start.5 = ((bf16[8,4,2048]{2,1,0:T(4,128)(2,1)}), bf16[8,4,2048]{2,1,0:T(4,128)(2,1)}, u32[]{:S(2)}, u32[]{:S(2)}) async-start(bf16[8,4,2048]{2,1,0:T(4,128)(2,1)} %broadcast_in_dim.6), calls=%async_computation.5 | async-start | bytes 262144 | tf_op jit(solution)/shard_map/all_to_all | solution.py:182
  141.5 1.0 copy-start.2
  142.5 1.0 copy-start.5
  143.5 1.0 copy-start.7

commit v5 on v4

--- a/solution.py
+++ b/solution.py
@@ -236,8 +236,7 @@
     stats = jax.ShapeDtypeStruct((items // GROUP, 8, near * GROUP), F32)
     grad_q, stats = per_group(query_kernel, "grad_queries", 700_000_000, side, [q, kv, kv_recv, g], [like, stats], 8)
 
-    total = scatter_sum(term, "x").astype(BF16)
-    total = scatter_sum(total, "core").astype(BF16)
+    total = scatter_sum(term, NEAR).astype(BF16)
     total, g_recv, grad_q, stats = lax.optimization_barrier((total, g_recv, grad_q, stats))
     stats_recv = lax.ppermute(stats, "zh", [(1, 0)])
     total = (scatter_sum(total, ("zh", "dp")) * factor).astype(BF16)

time: 188 us -> 191 us (1.016)
  blocking collectives: 44.6 us -> 35.2 us
  waiting for transfers between devices: 30.1 us -> 36.6 us
  starting transfers between devices: 73 us -> 79.4 us
    all_to_all x2 -> x1, blocking collectives: 44.6 us -> 35.2 us  [exchange(): return lax.all_to_all(x, axes, 0, 0, tiled=True)]
    all_to_all x5, starting transfers between devices: 35.2 us -> 41.7 us  [exchange(): return lax.all_to_all(x, axes, 0, 0, tiled=True)]
    all_to_all x5, waiting for transfers between devices: 14.7 us -> 19.9 us  [exchange(): return lax.all_to_all(x, axes, 0, 0, tiled=True)]
  transfers between devices with their start and end apart: 17 -> 17, of which waited for: 9 -> 10; matrix products, arithmetic and copies ran while one was open for 3% -> 3% of each run, Pallas kernels for 11% -> 11%
where the time goes in v5:
time: 191 us; the launch traced here: 190 us
  starting transfers between devices  79.4 us (42%)
  waiting for transfers between devices  36.6 us (19%)
  blocking collectives  35.2 us (18%)
  Pallas kernels  20.7 us (11%)
  local copies, waits for them, and re-layouts  14.4 us (8%)
  other arithmetic  2.69 us (1%)
    all_to_all x5, starting transfers between devices, exchange(): return lax.all_to_all(x, axes, 0, 0, tiled=True)  41.7 us
    all_to_all x1, blocking collectives, exchange(): return lax.all_to_all(x, axes, 0, 0, tiled=True)  35.2 us
    ppermute x8, starting transfers between devices, shift(): return lax.ppermute(x, axis, [(i, (i + by) % size) for i in range(size)])  25.9 us
    all_to_all x5, waiting for transfers between devices, exchange(): return lax.all_to_all(x, axes, 0, 0, tiled=True)  19.9 us
    pallas_call x3, Pallas kernels, per_group(): pl.pallas_call(kernel, grid=(items // (STEP_GROUPS * GROUP),), in_specs=[...  15.3 us
    ppermute x8, waiting for transfers between devices, shift(): return lax.ppermute(x, axis, [(i, (i + by) % size) for i in range(size)])  13.7 us
    ppermute x1, starting transfers between devices, local(): kv_recv = lax.ppermute(kv, 'zh', [(0, 1)])  7.96 us
    unnamed x16, local copies, waits for them, and re-layouts  5.69 us
  transfers between devices with their start and end apart: 17, of which 10 were waited for; matrix products, arithmetic and copies ran while one was open for 3% of the time, Pallas kernels for 11%

profile of v5, /device:TPU:1, one launch (start us, length us, event | category | flops | bytes accessed | tf_op | source)
XLA Modules:
  0.0 190.0 jit_solution(12804210345533358607)
XLA Ops:
  0.6 10.2 %all-to-all-start = ((bf16[8,96,256]{2,1,0:T(8,128)(2,1)}), bf16[8,96,256]{2,1,0:T(8,128)(2,1)S(1)}, u32[]{:S(2)}, u32[]{:S(2)}) async-start(bf16[8,96,256]{2,1,0:T(8,128)(2,1)} %bitcast.35), calls=%async_computation | async-start | bytes 786432 | tf_op jit(solution)/shard_map/all_to_all | solution.py:182
  10.9 2.4 %pad_maximum_fusion = bf16[8,3,96,256]{3,2,1,0:T(8,128)(2,1)} fusion(bf16[8,1,96,256]{3,2,1,0:T(8,128)(2,1)} %bitcast.29, bf16[8,1,96,256]{3,2,1,0:T(8,128)(2,1)} %bitcast.30, bf16[8,1,96,256]{3,2,1,0:T(8,128)(2,1)} %bitcast.31), kind=kLoop, calls=%fused_computation | loop fusion | flops 1179648 | bytes 2359296 | tf_op jit(solution)/shard_map/stack | solution.py:222
  13.3 5.7 %all-to-all-done = bf16[8,96,256]{2,1,0:T(8,128)(2,1)S(1)} async-done(((bf16[8,96,256]{2,1,0:T(8,128)(2,1)}), bf16[8,96,256]{2,1,0:T(8,128)(2,1)S(1)}, u32[]{:S(2)}, u32[]{:S(2)}) %all-to-all-start) | async-done | bytes 393248 | tf_op jit(solution)/shard_map/all_to_all | solution.py:182
  19.0 5.0 %all-to-all-start.1 = ((bf16[8,3,96,256]{3,2,1,0:T(8,128)(2,1)}), bf16[8,3,96,256]{3,2,1,0:T(8,128)(2,1)}, u32[]{:S(2)}, u32[]{:S(2)}) async-start(bf16[8,3,96,256]{3,2,1,0:T(8,128)(2,1)} %pad_maximum_fusion), calls=%async_computation.1 | async-start | bytes 2359296 | tf_op jit(solution)/shard_map/all_to_all | solution.py:182
  24.0 1.9 %collective-permute-start = (bf16[768,256]{1,0:T(8,128)(2,1)S(1)}, bf16[768,256]{1,0:T(8,128)(2,1)S(1)}, u32[]{:S(2)}, u32[]{:S(2)}) collective-permute-start(bf16[768,256]{1,0:T(8,128)(2,1)S(1)} %bitcast.20), channel_id=1, source_target_pairs={{0,4},{4,8},{8,12},{12,16},{16,20},{20,24},{24,28},{28,0},{1,5},{5... | collective-permute-start | bytes 1179656 | tf_op jit(solution)/shard_map/ppermute | solution.py:192
  25.9 4.6 %collective-permute-start.1 = (bf16[768,256]{1,0:T(8,128)(2,1)S(1)}, bf16[768,256]{1,0:T(8,128)(2,1)S(1)}, u32[]{:S(2)}, u32[]{:S(2)}) collective-permute-start(bf16[768,256]{1,0:T(8,128)(2,1)S(1)} %bitcast.21), channel_id=1, source_target_pairs={{0,28},{4,0},{8,4},{12,8},{16,12},{20,16},{24,20},{28,24},{1,29},{... | collective-permute-start | bytes 1179656 | tf_op jit(solution)/shard_map/ppermute | solution.py:192
  30.5 7.2 %collective-permute-done.refs_1_ = bf16[768,256]{1,0:T(8,128)(2,1)S(1)} collective-permute-done((bf16[768,256]{1,0:T(8,128)(2,1)S(1)}, bf16[768,256]{1,0:T(8,128)(2,1)S(1)}, u32[]{:S(2)}, u32[]{:S(2)}) %collective-permute-start) | collective-permute-done | bytes 393248 | tf_op jit(solution)/shard_map/ppermute | solution.py:192
  37.6 1.9 %collective-permute-start.2 = (bf16[768,256]{1,0:T(8,128)(2,1)S(1)}, bf16[768,256]{1,0:T(8,128)(2,1)}, u32[]{:S(2)}, u32[]{:S(2)}) collective-permute-start(bf16[768,256]{1,0:T(8,128)(2,1)S(1)} %collective-permute-done.refs_1_), channel_id=1, source_target_pairs={{0,4},{4,8},{8,12},{12,16},{16,20},{20,24},{24,28},{28,0},{1,5},{5... | collective-permute-start | bytes 1179656 | tf_op jit(solution)/shard_map/ppermute | solution.py:192
  39.6 4.6 %collective-permute-start.3 = (bf16[768,256]{1,0:T(8,128)(2,1)S(1)}, bf16[768,256]{1,0:T(8,128)(2,1)}, u32[]{:S(2)}, u32[]{:S(2)}) collective-permute-start(bf16[768,256]{1,0:T(8,128)(2,1)S(1)} %collective-permute-done.1.refs_2_), channel_id=1, source_target_pairs={{0,28},{4,0},{8,4},{12,8},{16,12},{20,16},{24,20},{28,24},{1,29},{... | collective-permute-start | bytes 1179656 | tf_op jit(solution)/shard_map/ppermute | solution.py:192
  44.2 1.2 slice.37.kv_ref
  45.4 8.0 %collective-permute-start.8 = (bf16[8,2,96,256]{3,2,1,0:T(8,128)(2,1)S(1)}, bf16[8,2,96,256]{3,2,1,0:T(8,128)(2,1)}, u32[]{:S(2)}, u32[]{:S(2)}) collective-permute-start(bf16[8,2,96,256]{3,2,1,0:T(8,128)(2,1)S(1)} %slice.37.kv_ref), channel_id=1, source_target_pairs={{0,256},{1,257},{2,258},{3,259},{4,260},{5,261},{6,262},{7,263},{8... | collective-permute-start | bytes 2359304 | tf_op jit(solution)/shard_map/ppermute | solution.py:225
  53.3 1.9 %collective-permute-start.4 = (bf16[768,256]{1,0:T(8,128)(2,1)}, bf16[768,256]{1,0:T(8,128)(2,1)S(1)}, u32[]{:S(2)}, u32[]{:S(2)}) collective-permute-start(bf16[768,256]{1,0:T(8,128)(2,1)} %collective-permute-done.2.refs_3_), channel_id=1, source_target_pairs={{0,4},{4,8},{8,12},{12,16},{16,20},{20,24},{24,28},{28,0},{1,5},{5... | collective-permute-start | bytes 1179656 | tf_op jit(solution)/shard_map/ppermute | solution.py:192
  55.2 4.6 %collective-permute-start.5 = (bf16[768,256]{1,0:T(8,128)(2,1)}, bf16[768,256]{1,0:T(8,128)(2,1)S(1)}, u32[]{:S(2)}, u32[]{:S(2)}) collective-permute-start(bf16[768,256]{1,0:T(8,128)(2,1)} %collective-permute-done.3.refs_4_), channel_id=1, source_target_pairs={{0,28},{4,0},{8,4},{12,8},{16,12},{20,16},{24,20},{28,24},{1,29},{... | collective-permute-start | bytes 1179656 | tf_op jit(solution)/shard_map/ppermute | solution.py:192
  59.8 1.0 slice_bitcast_fusion.q_ref
  60.9 1.3 collective-permute-start.9
  62.2 3.6 %collective-permute-done.4.refs_5_ = bf16[768,256]{1,0:T(8,128)(2,1)S(1)} collective-permute-done((bf16[768,256]{1,0:T(8,128)(2,1)}, bf16[768,256]{1,0:T(8,128)(2,1)S(1)}, u32[]{:S(2)}, u32[]{:S(2)}) %collective-permute-start.4) | collective-permute-done | bytes 393248 | tf_op jit(solution)/shard_map/ppermute | solution.py:192
  65.8 0.7 slice.38
  66.5 1.9 %collective-permute-start.6 = (bf16[384,256]{1,0:T(8,128)(2,1)}, bf16[384,256]{1,0:T(8,128)(2,1)S(1)}, u32[]{:S(2)}, u32[]{:S(2)}) collective-permute-start(bf16[384,256]{1,0:T(8,128)(2,1)} %slice.38), channel_id=1, source_target_pairs={{0,4},{4,8},{8,12},{12,16},{16,20},{20,24},{24,28},{28,0},{1,5},{5... | collective-permute-start | bytes 589832 | tf_op jit(solution)/shard_map/ppermute | solution.py:192
  68.4 0.7 slice.39
  69.1 4.6 %collective-permute-start.7 = (bf16[384,256]{1,0:T(8,128)(2,1)}, bf16[384,256]{1,0:T(8,128)(2,1)}, u32[]{:S(2)}, u32[]{:S(2)}) collective-permute-start(bf16[384,256]{1,0:T(8,128)(2,1)} %slice.39), channel_id=1, source_target_pairs={{0,28},{4,0},{8,4},{12,8},{16,12},{20,16},{24,20},{28,24},{1,29},{... | collective-permute-start | bytes 589832 | tf_op jit(solution)/shard_map/ppermute | solution.py:192
  73.7 1.0 collective-permute-done.6.refs_7_
  74.7 1.9 collective-permute-done.7.refs_8_
  76.6 1.2 copy-done.3
  77.8 2.2 %grad_attended.1 = bf16[768,256]{1,0:T(8,128)(2,1)S(1)} custom-call(s32[1]{0:T(128)} %bitcast.place_ref, bf16[256,2048]{1,0:T(8,128)(2,1)S(1)} %copy-done.3, bf16[768,256]{1,0:T(8,128)(2,1)S(1)} %bitcast.22, bf16[768,256]{1,0:T(8,128)(2,1)S(1)} %collective-permute-done.refs_1_, bf16[768,256]{1,0:T(8,128)(2,1)S(1)} %collective-permute-done.1.refs_2_, ...), custom_call_target="tpu_custom_call" | custom-call | flops 800000000 | bytes 4500000 | tf_op jit(solution)/shard_map/grad_attended/pallas_call | solution.py:170
  80.0 0.7 copy-done
  80.7 5.0 %attend.1 = bf16[8,96,256]{2,1,0:T(8,128)(2,1)S(1)} custom-call(s32[1]{0:T(128)} %bitcast.1.side_ref, bf16[8,96,256]{2,1,0:T(8,128)(2,1)S(1)} %slice_bitcast_fusion.q_ref, bf16[8,2,96,256]{3,2,1,0:T(8,128)(2,1)S(1)} %slice.37.kv_ref, bf16[8,2,96,256]{3,2,1,0:T(8,128)(2,1)} %collective-permute-done.8.recv_ref), custom_call_target="tpu_custom_call" | custom-call | flops 400000000 | bytes 4000000 | tf_op jit(solution)/shard_map/attend/pallas_call | solution.py:156
  85.8 3.3 %term.1 = bf16[256,2048]{1,0:T(8,128)(2,1)} custom-call(s32[1]{0:T(128)} %bitcast.place_ref, bf16[768,256]{1,0:T(8,128)(2,1)S(1)} %bitcast.24, bf16[768,256]{1,0:T(8,128)(2,1)S(1)} %bitcast.23, bf16[768,256]{1,0:T(8,128)(2,1)S(1)} %collective-permute-done.refs_1_, bf16[768,256]{1,0:T(8,128)(2,1)S(1)} %collective-permute-done.1.refs_2_, ...), custom_call_target="tpu_custom_call" | custom-call | flops 800000000 | bytes 4500000 | tf_op jit(solution)/shard_map/term/pallas_call | solution.py:170
  89.0 10.3 %all-to-all-start.2 = ((bf16[8,32,2048]{2,1,0:T(8,128)(2,1)}), bf16[8,32,2048]{2,1,0:T(8,128)(2,1)S(1)}, u32[]{:S(2)}, u32[]{:S(2)}) async-start(bf16[8,32,2048]{2,1,0:T(8,128)(2,1)} %bitcast.10), calls=%async_computation.2 | async-start | bytes 2097152 | tf_op jit(solution)/shard_map/all_to_all | solution.py:182
  99.3 1.3 collective-permute-start.10
  100.6 5.6 %grad_queries.1 = (bf16[8,96,256]{2,1,0:T(8,128)(2,1)S(1)}, f32[6,8,128]{2,1,0:T(8,128)S(1)}) custom-call(s32[1]{0:T(128)} %bitcast.1.side_ref, bf16[8,96,256]{2,1,0:T(8,128)(2,1)S(1)} %slice_bitcast_fusion.q_ref, bf16[8,2,96,256]{3,2,1,0:T(8,128)(2,1)S(1)} %slice.37.kv_ref, bf16[8,2,96,256]{3,2,1,0:T(8,128)(2,1)} %collective-permute-done.8.recv_ref, ...), custom_call_target="tpu_custom_call" | custom-call | flops 700000000 | bytes 4000000 | tf_op jit(solution)/shard_map/grad_queries/pallas_call | solution.py:156
  106.2 0.7 copy-done.6
  106.9 7.5 %all-to-all-done.2 = bf16[8,32,2048]{2,1,0:T(8,128)(2,1)S(1)} async-done(((bf16[8,32,2048]{2,1,0:T(8,128)(2,1)}), bf16[8,32,2048]{2,1,0:T(8,128)(2,1)S(1)}, u32[]{:S(2)}, u32[]{:S(2)}) %all-to-all-start.2) | async-done | bytes 1048608 | tf_op jit(solution)/shard_map/all_to_all | solution.py:182
  114.5 1.3 collective-permute-done.10.g_recv_ref
  115.8 0.8 reshape.52
  116.6 12.2 %all-to-all-start.3 = ((bf16[8,4,2048]{2,1,0:T(4,128)(2,1)}), bf16[8,4,2048]{2,1,0:T(4,128)(2,1)S(1)}, u32[]{:S(2)}, u32[]{:S(2)}) async-start(bf16[8,4,2048]{2,1,0:T(4,128)(2,1)} %reshape.52), calls=%async_computation.3 | async-start | bytes 262144 | tf_op jit(solution)/shard_map/all_to_all | solution.py:182
  128.8 1.3 collective-permute-start.11
  130.1 6.5 %all-to-all-done.3 = bf16[8,4,2048]{2,1,0:T(4,128)(2,1)S(1)} async-done(((bf16[8,4,2048]{2,1,0:T(4,128)(2,1)}), bf16[8,4,2048]{2,1,0:T(4,128)(2,1)S(1)}, u32[]{:S(2)}, u32[]{:S(2)}) %all-to-all-start.3) | async-done | bytes 131104 | tf_op jit(solution)/shard_map/all_to_all | solution.py:182
  136.8 1.7 collective-permute-done.11.stats_recv_ref
  138.5 0.7 broadcast_in_dim.6
  139.2 4.0 %all-to-all-start.4 = ((bf16[8,4,2048]{2,1,0:T(4,128)(2,1)}), bf16[8,4,2048]{2,1,0:T(4,128)(2,1)}, u32[]{:S(2)}, u32[]{:S(2)}) async-start(bf16[8,4,2048]{2,1,0:T(4,128)(2,1)} %broadcast_in_dim.6), calls=%async_computation.4 | async-start | bytes 262144 | tf_op jit(solution)/shard_map/all_to_all | solution.py:182
  143.2 1.0 copy-done.2
  144.2 1.0 copy-done.5
  145.2 1.0 copy-done.7
  146.2 4.7 %grad_keys_values.1 = bf16[8,34,16,256]{3,2,1,0:T(8,128)(2,1)S(1)} custom-call(s32[1]{0:T(128)} %bitcast.1.side_ref, bf16[8,96,256]{2,1,0:T(8,128)(2,1)S(1)} %slice_bitcast_fusion.q_ref, bf16[8,2,96,256]{3,2,1,0:T(8,128)(2,1)S(1)} %slice.37.kv_ref, bf16[8,96,256]{2,1,0:T(8,128)(2,1)} %collective-permute-done.9.q_recv_ref, bf16[8,96,256]{2,1,0:T(8,128)(2,1)S(1)} %bitcast.27, ...), custom_call_target="tpu_custom_call" | custom-call | flops 1000000000 | bytes 4000000 | tf_op jit(solution)/shard_map/grad_keys_values/pallas_call | solution.py:156
  151.1 0.9 reshape.53
  152.2 35.2 %all_to_all.30 = bf16[8,34,16,256]{3,2,1,0:T(8,128)(2,1)S(1)} all-to-all(bf16[8,34,16,256]{3,2,1,0:T(8,128)(2,1)S(1)} %broadcast_dynamic-update-slice_fusion), channel_id=1, replica_groups=mesh['zh'=2,'x'=4,'core'=2,'tensor'=8,'dp'=4] {'x','core'}, dimensions={0} | all-to-all | bytes 4456448 | tf_op jit(solution)/shard_map/all_to_all | solution.py:182
  187.6 1.0 fusion
  188.7 1.3 reshape.55
  (25 shorter events, 0.9 us)
Async XLA Ops:
  0.6 18.3 %all-to-all-start = ((bf16[8,96,256]{2,1,0:T(8,128)(2,1)}), bf16[8,96,256]{2,1,0:T(8,128)(2,1)S(1)}, u32[]{:S(2)}, u32[]{:S(2)}) async-start(bf16[8,96,256]{2,1,0:T(8,128)(2,1)} %bitcast.35), calls=%async_computation | async-start | bytes 786432 | tf_op jit(solution)/shard_map/all_to_all | solution.py:182
  19.0 25.2 %all-to-all-start.1 = ((bf16[8,3,96,256]{3,2,1,0:T(8,128)(2,1)}), bf16[8,3,96,256]{3,2,1,0:T(8,128)(2,1)}, u32[]{:S(2)}, u32[]{:S(2)}) async-start(bf16[8,3,96,256]{3,2,1,0:T(8,128)(2,1)} %pad_maximum_fusion), calls=%async_computation.1 | async-start | bytes 2359296 | tf_op jit(solution)/shard_map/all_to_all | solution.py:182
  24.0 13.7 %collective-permute-start = (bf16[768,256]{1,0:T(8,128)(2,1)S(1)}, bf16[768,256]{1,0:T(8,128)(2,1)S(1)}, u32[]{:S(2)}, u32[]{:S(2)}) collective-permute-start(bf16[768,256]{1,0:T(8,128)(2,1)S(1)} %bitcast.20), channel_id=1, source_target_pairs={{0,4},{4,8},{8,12},{12,16},{16,20},{20,24},{24,28},{28,0},{1,5},{5... | collective-permute-start | bytes 1179656 | tf_op jit(solution)/shard_map/ppermute | solution.py:192
  25.9 13.7 %collective-permute-start.1 = (bf16[768,256]{1,0:T(8,128)(2,1)S(1)}, bf16[768,256]{1,0:T(8,128)(2,1)S(1)}, u32[]{:S(2)}, u32[]{:S(2)}) collective-permute-start(bf16[768,256]{1,0:T(8,128)(2,1)S(1)} %bitcast.21), channel_id=1, source_target_pairs={{0,28},{4,0},{8,4},{12,8},{16,12},{20,16},{24,20},{28,24},{1,29},{... | collective-permute-start | bytes 1179656 | tf_op jit(solution)/shard_map/ppermute | solution.py:192
  37.6 15.7 %collective-permute-start.2 = (bf16[768,256]{1,0:T(8,128)(2,1)S(1)}, bf16[768,256]{1,0:T(8,128)(2,1)}, u32[]{:S(2)}, u32[]{:S(2)}) collective-permute-start(bf16[768,256]{1,0:T(8,128)(2,1)S(1)} %collective-permute-done.refs_1_), channel_id=1, source_target_pairs={{0,4},{4,8},{8,12},{12,16},{16,20},{20,24},{24,28},{28,0},{1,5},{5... | collective-permute-start | bytes 1179656 | tf_op jit(solution)/shard_map/ppermute | solution.py:192
  39.6 15.7 %collective-permute-start.3 = (bf16[768,256]{1,0:T(8,128)(2,1)S(1)}, bf16[768,256]{1,0:T(8,128)(2,1)}, u32[]{:S(2)}, u32[]{:S(2)}) collective-permute-start(bf16[768,256]{1,0:T(8,128)(2,1)S(1)} %collective-permute-done.1.refs_2_), channel_id=1, source_target_pairs={{0,28},{4,0},{8,4},{12,8},{16,12},{20,16},{24,20},{28,24},{1,29},{... | collective-permute-start | bytes 1179656 | tf_op jit(solution)/shard_map/ppermute | solution.py:192
  45.4 35.4 %collective-permute-start.8 = (bf16[8,2,96,256]{3,2,1,0:T(8,128)(2,1)S(1)}, bf16[8,2,96,256]{3,2,1,0:T(8,128)(2,1)}, u32[]{:S(2)}, u32[]{:S(2)}) collective-permute-start(bf16[8,2,96,256]{3,2,1,0:T(8,128)(2,1)S(1)} %slice.37.kv_ref), channel_id=1, source_target_pairs={{0,256},{1,257},{2,258},{3,259},{4,260},{5,261},{6,262},{7,263},{8... | collective-permute-start | bytes 2359304 | tf_op jit(solution)/shard_map/ppermute | solution.py:225
  53.3 12.5 %collective-permute-start.4 = (bf16[768,256]{1,0:T(8,128)(2,1)}, bf16[768,256]{1,0:T(8,128)(2,1)S(1)}, u32[]{:S(2)}, u32[]{:S(2)}) collective-permute-start(bf16[768,256]{1,0:T(8,128)(2,1)} %collective-permute-done.2.refs_3_), channel_id=1, source_target_pairs={{0,4},{4,8},{8,12},{12,16},{16,20},{20,24},{24,28},{28,0},{1,5},{5... | collective-permute-start | bytes 1179656 | tf_op jit(solution)/shard_map/ppermute | solution.py:192
  55.2 13.1 %collective-permute-start.5 = (bf16[768,256]{1,0:T(8,128)(2,1)}, bf16[768,256]{1,0:T(8,128)(2,1)S(1)}, u32[]{:S(2)}, u32[]{:S(2)}) collective-permute-start(bf16[768,256]{1,0:T(8,128)(2,1)} %collective-permute-done.3.refs_4_), channel_id=1, source_target_pairs={{0,28},{4,0},{8,4},{12,8},{16,12},{20,16},{24,20},{28,24},{1,29},{... | collective-permute-start | bytes 1179656 | tf_op jit(solution)/shard_map/ppermute | solution.py:192
  60.9 28.1 %collective-permute-start.9 = (bf16[8,96,256]{2,1,0:T(8,128)(2,1)S(1)}, bf16[8,96,256]{2,1,0:T(8,128)(2,1)}, u32[]{:S(2)}, u32[]{:S(2)}) collective-permute-start(bf16[8,96,256]{2,1,0:T(8,128)(2,1)S(1)} %slice_bitcast_fusion.q_ref), channel_id=1, source_target_pairs={{256,0},{257,1},{258,2},{259,3},{260,4},{261,5},{262,6},{263,7},{2... | collective-permute-start | bytes 1179656 | tf_op jit(solution)/shard_map/ppermute | solution.py:228
  66.5 8.2 %collective-permute-start.6 = (bf16[384,256]{1,0:T(8,128)(2,1)}, bf16[384,256]{1,0:T(8,128)(2,1)S(1)}, u32[]{:S(2)}, u32[]{:S(2)}) collective-permute-start(bf16[384,256]{1,0:T(8,128)(2,1)} %slice.38), channel_id=1, source_target_pairs={{0,4},{4,8},{8,12},{12,16},{16,20},{20,24},{24,28},{28,0},{1,5},{5... | collective-permute-start | bytes 589832 | tf_op jit(solution)/shard_map/ppermute | solution.py:192
  69.1 7.5 %collective-permute-start.7 = (bf16[384,256]{1,0:T(8,128)(2,1)}, bf16[384,256]{1,0:T(8,128)(2,1)}, u32[]{:S(2)}, u32[]{:S(2)}) collective-permute-start(bf16[384,256]{1,0:T(8,128)(2,1)} %slice.39), channel_id=1, source_target_pairs={{0,28},{4,0},{8,4},{12,8},{16,12},{20,16},{24,20},{28,24},{1,29},{... | collective-permute-start | bytes 589832 | tf_op jit(solution)/shard_map/ppermute | solution.py:192
  76.6 1.2 copy-start.3
  80.0 0.7 copy-start
  89.0 10.3 %copy-start.1 = (bf16[768,256]{1,0:T(8,128)(2,1)S(1)}, bf16[768,256]{1,0:T(8,128)(2,1)}, u32[]{:S(2)}) copy-start(bf16[768,256]{1,0:T(8,128)(2,1)} %copy-done) | copy-start | bytes 1179652
  89.0 25.4 %all-to-all-start.2 = ((bf16[8,32,2048]{2,1,0:T(8,128)(2,1)}), bf16[8,32,2048]{2,1,0:T(8,128)(2,1)S(1)}, u32[]{:S(2)}, u32[]{:S(2)}) async-start(bf16[8,32,2048]{2,1,0:T(8,128)(2,1)} %bitcast.10), calls=%async_computation.2 | async-start | bytes 2097152 | tf_op jit(solution)/shard_map/all_to_all | solution.py:182
  99.3 16.5 %collective-permute-start.10 = (bf16[8,96,256]{2,1,0:T(8,128)(2,1)S(1)}, bf16[8,96,256]{2,1,0:T(8,128)(2,1)S(1)}, u32[]{:S(2)}, u32[]{:S(2)}) collective-permute-start(bf16[8,96,256]{2,1,0:T(8,128)(2,1)S(1)} %bitcast.25), channel_id=1, source_target_pairs={{256,0},{257,1},{258,2},{259,3},{260,4},{261,5},{262,6},{263,7},{2... | collective-permute-start | bytes 1179656 | tf_op jit(solution)/shard_map/ppermute | solution.py:234
  106.2 0.7 copy-start.6
  115.8 23.4 %copy-start.4 = (bf16[8,96,256]{2,1,0:T(8,128)(2,1)}, bf16[8,96,256]{2,1,0:T(8,128)(2,1)S(1)}, u32[]{:S(2)}) copy-start(bf16[8,96,256]{2,1,0:T(8,128)(2,1)S(1)} %collective-permute-done.10.g_recv_ref) | copy-start | bytes 1179652
  116.6 20.0 %all-to-all-start.3 = ((bf16[8,4,2048]{2,1,0:T(4,128)(2,1)}), bf16[8,4,2048]{2,1,0:T(4,128)(2,1)S(1)}, u32[]{:S(2)}, u32[]{:S(2)}) async-start(bf16[8,4,2048]{2,1,0:T(4,128)(2,1)} %reshape.52), calls=%async_computation.3 | async-start | bytes 262144 | tf_op jit(solution)/shard_map/all_to_all | solution.py:182
  128.8 9.7 %collective-permute-start.11 = (f32[6,8,128]{2,1,0:T(8,128)S(1)}, f32[6,8,128]{2,1,0:T(8,128)S(1)}, u32[]{:S(2)}, u32[]{:S(2)}) collective-permute-start(f32[6,8,128]{2,1,0:T(8,128)S(1)} %get-tuple-element.28.stats_ref), channel_id=1, source_target_pairs={{256,0},{257,1},{258,2},{259,3},{260,4},{261,5},{262,6},{263,7},{2... | collective-permute-start | bytes 73736 | tf_op jit(solution)/shard_map/ppermute | solution.py:241
  139.2 11.9 %all-to-all-start.4 = ((bf16[8,4,2048]{2,1,0:T(4,128)(2,1)}), bf16[8,4,2048]{2,1,0:T(4,128)(2,1)}, u32[]{:S(2)}, u32[]{:S(2)}) async-start(bf16[8,4,2048]{2,1,0:T(4,128)(2,1)} %broadcast_in_dim.6), calls=%async_computation.4 | async-start | bytes 262144 | tf_op jit(solution)/shard_map/all_to_all | solution.py:182
  143.2 1.0 copy-start.2
  144.2 1.0 copy-start.5
  145.2 1.0 copy-start.7
